TPU v7x, 256 devices: a whole 4x4x8 slice. The times are simulated.
256 devices in a mesh: atom: 64 (over z, y_hi, x), wave: 4 (over y_lo, core).
Axes of the slice: x: 4, y: 4 (y_hi: 2, y_lo: 2; y = y_hi * 2 + y_lo), z: 8, core: 2. Of those that a mesh axis runs over, the one named last changes fastest.
Arguments:
- positions: float32 [3, 262144], P(None, 'atom'), may hold values from 0 to 256
- features: bfloat16 [262144, 128], P('atom'), may hold values from -6 to 6
- cotangent: bfloat16 [262144, 128], P('atom'), may hold values from -6 to 6
- miller: int32 [3, 4096], P(None, 'wave'), may hold values from -8 to 8
- radial_filter: float32 [4096, 128], P('wave'), may hold values from 0.3 to 3
Outputs:
- feature_grad: float32 [262144, 128], P('atom')
- position_grad: float32 [3, 262144], P(None, 'atom')
- filter_grad: float32 [4096, 128], P('wave')
All inputs are finite; a program needn't handle non-finite values.
Results may differ from a plain program's by a relative error of at most 0.008.
Values sent between devices are 32-bit elements; how exact they have to be, the bound alone decides.
No kernel may reach another device: no remote copies, remote signals or barrier semaphores. Data moves between devices by JAX's collectives and lax.ppermute only.
A program may use at most 128 MiB of HBM per device.

v0:
```python
import math

import jax
import jax.numpy as jnp
from jax import lax
from jax.sharding import PartitionSpec as P

phase_step = 2.0 * math.pi / 256.0


def trig_pair(place, indices):
    millers = indices.astype(jnp.float32)
    theta = phase_step * (
        place[0][:, None] * millers[0][None, :]
        + place[1][:, None] * millers[1][None, :]
        + place[2][:, None] * millers[2][None, :]
    )
    return (jnp.cos(theta).astype(jnp.bfloat16), jnp.sin(theta).astype(jnp.bfloat16))


def factor_block(cosine, sine, rows):
    count = cosine.shape[1]
    tables = jnp.concatenate([cosine, sine], 1)
    product = lax.dot_general(
        tables, rows, (((0,), (0,)), ((), ())), preferred_element_type=jnp.float32
    )
    return jnp.concatenate([product[:count], product[count:]], 1)


def finish(totals, filter_rows, scale, channels):
    factor_sc = totals[:, :channels]
    factor_gc = totals[:, channels : 2 * channels]
    factor_ss = totals[:, 2 * channels : 3 * channels]
    factor_gs = totals[:, 3 * channels :]
    grad_rows = scale * (factor_gc * factor_sc + factor_gs * factor_ss)
    weighted = filter_rows * scale
    filtered = jnp.concatenate(
        [weighted * factor_sc, weighted * factor_gc, weighted * factor_ss, weighted * factor_gs], 1
    )
    return (grad_rows, filtered)


def shards(positions, features, cotangent, miller, radial_filter):
    channels = features.shape[1]
    local_waves = miller.shape[1]
    atom_count = positions.shape[1] * lax.axis_size("atom")
    wave_count = local_waves * lax.axis_size("wave")
    scale = float(atom_count * wave_count) ** (-0.5)
    joined_rows = jnp.concatenate([features, cotangent], 1)
    cosine, sine = trig_pair(positions, miller)
    local_factors = factor_block(cosine, sine, joined_rows)
    totals = lax.psum(local_factors, "atom")
    filter_grad, filtered = finish(totals, radial_filter, scale, channels)
    filtered = filtered.astype(jnp.bfloat16)
    w_sc = filtered[:, :channels]
    w_gc = filtered[:, channels : 2 * channels]
    w_ss = filtered[:, 2 * channels : 3 * channels]
    w_gs = filtered[:, 3 * channels :]
    down_table = jnp.concatenate([w_gc, w_gs], 0)
    right_table = jnp.concatenate(
        [jnp.concatenate([w_gs, w_gc], 0), jnp.concatenate([w_ss, w_sc], 0)], 1
    )
    tables = jnp.concatenate([cosine, sine], 1)
    feat_part = jnp.dot(tables, down_table, preferred_element_type=jnp.float32)
    pq_table = lax.dot_general(
        joined_rows, right_table, (((1,), (1,)), ((), ())), preferred_element_type=jnp.float32
    )
    dtheta = (
        cosine.astype(jnp.float32) * pq_table[:, :local_waves]
        - sine.astype(jnp.float32) * pq_table[:, local_waves:]
    ).astype(jnp.bfloat16)
    pos_part = phase_step * lax.dot_general(
        miller.astype(jnp.bfloat16),
        dtheta,
        (((1,), (1,)), ((), ())),
        preferred_element_type=jnp.float32,
    )
    feature_grad, position_grad = lax.psum((feat_part, pos_part), "wave")
    return (feature_grad, position_grad, filter_grad)


def solution(mesh):
    placed = (P(None, "atom"), P("atom", None), P("atom", None), P(None, "wave"), P("wave", None))
    return jax.shard_map(
        shards,
        mesh=mesh,
        in_specs=placed,
        out_specs=(P("atom", None), P(None, "atom"), P("wave", None)),
        check_vma=False,
    )
```

profile of v0, /device:TPU:1, one launch (start us, length us, event | category | flops | bytes accessed | tf_op | source)
XLA Modules:
  0.0 917.1 jit_solution(12820262514618656380)
XLA Ops:
  7.2 0.0 all-reduce.3.cloned.1.call-start
  7.2 0.7 convert_element_type.22
  7.9 1.0 fusion.28
  9.0 1.4 constant_dynamic-update-slice_fusion.1
  10.4 1.5 constant_dynamic-update-slice_fusion
  11.8 68.9 %cosine_convert_fusion = (bf16[4096,1024]{1,0:T(8,128)(2,1)}, bf16[4096,1024]{1,0:T(8,128)(2,1)}) fusion(f32[1024]{0:T(1024)S(1)} %bitcast.20, f32[4096]{0:T(1024)S(1)} %bitcast.14, f32[1024]{0:T(1024)S(1)} %bitcast.22, f32[4096]{0:T(1024)S(1)} %bitcast.16, f32[1024]{0:T(1024)S(1)} %bitcast.18, f32[4096]{0:T(1024)S(1)} %bitcast.12), kind=kLoop, calls=%fused_computation.6 | loop fusion | flops 33554432 | bytes 16838656 | tf_op jit(solution)/shard_map/convert_element_type | solution.py:18
  80.7 8.8 fusion.3
  89.5 0.2 fusion.27
  89.8 1.5 pad_maximum_fusion.3
  91.3 0.0 all-reduce.3.cloned.1.call-update
  91.3 0.2 all-reduce.5.cloned.1.call-start
  91.5 0.2 copy.8
  91.7 658.7 %all-reduce.3.cloned.1.call-done = f32[1024,512]{0,1:T(8,128)} async-done(((f32[1024,512]{0,1:T(8,128)}), f32[1024,512]{0,1:T(8,128)}) %all-reduce.3.cloned.1.call-update) | async-done | bytes 2097168 | tf_op jit(solution)/shard_map/psum | solution.py:52
  750.4 2.5 multiply_convert_fusion.1
  752.9 0.7 copy-done.1
  753.6 0.1 copy-done.2
  753.7 9.2 %fusion.2 = f32[4096,128]{1,0:T(8,128)} fusion(bf16[4096,1024]{1,0:T(8,128)(2,1)} %get-tuple-element.17, bf16[4096,1024]{1,0:T(8,128)(2,1)} %get-tuple-element.16, bf16[1024,128]{0,1:T(8,128)(2,1)S(1)} %get-tuple-element.8, bf16[1024,128]{0,1:T(8,128)(2,1)S(1)} %get-tuple-element.9), kind=kOutput, calls=%fused_computation.8 | convolution fusion | flops 2182086656 | bytes 19398656 | tf_op jit(solution)/shard_map/dot_general | solution.py:64
  762.9 0.0 all-reduce.5.cloned.1.call-update
  763.0 0.0 copy-start.4
  763.0 14.1 %fusion.12 = f32[4096,2048]{1,0:T(8,128)} fusion(bf16[4096,256]{1,0:T(8,128)(2,1)S(1)} %constant_dynamic-update-slice_fusion, bf16[1024,128]{0,1:T(8,128)(2,1)S(1)} %copy-done, bf16[1024,128]{0,1:T(8,128)(2,1)S(1)} %get-tuple-element.6, bf16[1024,128]{0,1:T(8,128)(2,1)} %copy-done.2, bf16[1024,128]{0,1:T(8,128)(2,1)} %copy-done.1), kind=kOutput, calls=%fused_computation.14 | convolution fusion | flops 4299161600 | bytes 36700160 | tf_op jit(solution)/shard_map/dot_general | solution.py:65
  777.1 1.0 copy.9
  778.1 72.6 %fusion.9 = f32[3,4096]{1,0:T(4,128)S(1)} fusion(f32[4096,2048]{1,0:T(8,128)} %fusion.12, s32[3,1024]{1,0:T(4,128)S(1)} %copy-done.4, f32[1024]{0:T(1024)S(1)} %bitcast.21, f32[4096]{0:T(1024)S(1)} %bitcast.15, f32[1024]{0:T(1024)S(1)} %bitcast.23, f32[4096]{0:T(1024)S(1)} %bitcast.17, f32[1024]{0:T(1024)S(1)} %bitcast.19, f32[4096]{0:T(1024)S(1)} %bitcast.13), kind=kOutput, calls=%fused_computation.12 | convolution fusion | flops 83901440 | bytes 33677312 | tf_op jit(solution)/shard_map/dot_general | solution.py:72
  850.7 56.5 %psum.23 = f32[3,4096]{1,0:T(4,128)} all-reduce(f32[3,4096]{1,0:T(4,128)S(1)} %fusion.9), channel_id=1, replica_groups=mesh['atom'=64,'wave'=4] {'wave'}, use_global_device_ids=true, to_apply=%region_2.0 | all-reduce | flops 12288 | bytes 98304 | tf_op jit(solution)/shard_map/psum | solution.py:78
  907.2 3.0 copy.13
  (9 shorter events, 0.0 us)
Async XLA Ops:
  7.2 743.2 %all-reduce.3.cloned.1.call-start = ((), (), s32[]{:S(2)}) async-start(), calls=%async_computation | async-start | bytes 4194304 | tf_op jit(solution)/shard_map/psum | solution.py:52
  80.7 10.8 %copy-start.3 = (f32[1024,128]{1,0:T(8,128)S(1)}, f32[1024,128]{1,0:T(8,128)}, u32[]{:S(2)}) copy-start(f32[1024,128]{1,0:T(8,128)} %param.9) | copy-start | bytes 1572868
  91.3 816.0 %all-reduce.5.cloned.1.call-start = ((), (), s32[]{:S(2)}) async-start(), calls=%async_computation.1 | async-start | bytes 4194304 | tf_op jit(solution)/shard_map/psum | solution.py:78
  752.9 0.7 copy-start.1
  752.9 0.8 copy-start.2
  753.7 9.2 %copy-start = (bf16[1024,128]{0,1:T(8,128)(2,1)S(1)}, bf16[1024,128]{0,1:T(8,128)(2,1)}, u32[]{:S(2)}) copy-start(bf16[1024,128]{0,1:T(8,128)(2,1)} %get-tuple-element.7) | copy-start | bytes 786436
  763.0 15.1 %copy-start.4 = (s32[3,1024]{1,0:T(4,128)S(1)}, s32[3,1024]{1,0:T(4,128)}, u32[]{:S(2)}) copy-start(s32[3,1024]{1,0:T(4,128)} %param.8) | copy-start | bytes 36868
Sparse Core Ops, SparseCore 0:
  91.4 658.9 all-reduce.2
  763.1 106.0 all-reduce.4
where the time goes:
time: 917 us
  waiting for transfers between devices  659 us (72%)
  matrix products  105 us (11%)
  other arithmetic  73.6 us (8%)
  blocking collectives  56.5 us (6%)
  between operations  14.1 us (2%)
  local copies, waits for them, and re-layouts  9.2 us (1%)
    psum x1, waiting for transfers between devices, shards(): totals = lax.psum(local_factors, 'atom')  659 us
    dot_general x1, matrix products, shards(): lax.dot_general(miller.astype(jnp.bfloat16), dtheta, (((1,), (1,)), ((),...  72.6 us
    convert_element_type x1, other arithmetic, trig_pair(): jnp.cos(theta).astype(jnp.bfloat16)  68.9 us
    psum x1, blocking collectives, shards(): feature_grad, position_grad = lax.psum((feat_part, pos_part), 'wave')  56.5 us
  transfers between devices with their start and end apart: 2, of which 1 were waited for; matrix products, arithmetic and copies ran while one was open for 10% of the time, Pallas kernels for 0%

commit v1 on v0

v1 whole, which is shorter than its diff:
```python
import functools
import math

import jax
import jax.numpy as jnp
from jax import lax
from jax.experimental import pallas as pl
from jax.experimental.pallas import tpu as pltpu
from jax.sharding import Mesh, PartitionSpec as P

phase_step = 2.0 * math.pi / 256.0
PAIRS = 296
PAIR_ROWS = 304
TILES = 9
SLOTS = 17 * 64
CLASSES = 896
PACKED = 2560
f32 = jnp.float32
bf16 = jnp.bfloat16
VMEM_LIMIT = 56 * 1024 * 1024


def nt_dot(a, b):
    return lax.dot_general(a, b, (((1,), (1,)), ((), ())), preferred_element_type=f32)


def turn_trig(turns):
    x = (turns - jnp.floor(turns + 0.5)) * (2.0 * math.pi)
    square = x * x
    cosine = jnp.full_like(x, 1.0 / math.factorial(18) * -1.0)
    for power in range(16, -1, -2):
        cosine = cosine * square + ((-1.0) ** (power // 2) / math.factorial(power))
    sine = jnp.full_like(x, 1.0 / math.factorial(17))
    for power in range(15, 0, -2):
        sine = sine * square + ((-1.0) ** (power // 2) / math.factorial(power))
    return cosine, sine * x


def multiples(position_rows):
    count = position_rows.shape[1]
    orders = lax.broadcasted_iota(jnp.int32, (8, count), 0).astype(f32) + 1.0
    return [turn_trig(orders * (position_rows[d : d + 1, :] * (1.0 / 256.0))) for d in range(3)]


def pair_table(trig1, trig2):
    (c1, s1), (c2, s2) = trig1, trig2
    count = c1.shape[1]
    tiles = []
    for left in (c1, s1):
        for right in (c2, s2):
            for m in range(8):
                tiles.append(left[m : m + 1, :] * right)
    one = (lax.broadcasted_iota(jnp.int32, (16, count), 0) == 0).astype(f32)
    tiles += [c2, s2, c1, s1, one]
    return jnp.concatenate(tiles, 0)


def row_tables(pick_ref, features, cotangent):
    lane = lax.broadcasted_iota(jnp.int32, (32, 128), 1)
    row = lax.broadcasted_iota(jnp.int32, (32, 128), 0)
    pick = (lane == row + 32 * pick_ref[0]).astype(bf16)
    return jnp.concatenate([nt_dot(pick, features), nt_dot(pick, cotangent)], 0)


def fill_slots(slots_ref, trig0, rows):
    c0, s0 = trig0
    for t in range(8):
        slots_ref[128 * t : 128 * t + 64, :] = (c0[t : t + 1, :] * rows).astype(bf16)
        slots_ref[128 * t + 64 : 128 * t + 128, :] = (s0[t : t + 1, :] * rows).astype(bf16)
    slots_ref[1024:1088, :] = rows.astype(bf16)


def factor_kernel(pick_ref, pos_ref, feat_ref, cot_ref, out_ref, slots_ref, total_ref):
    step = pl.program_id(0)
    trig = multiples(pos_ref[...])
    fill_slots(slots_ref, trig[0], row_tables(pick_ref, feat_ref[...], cot_ref[...]))
    pairs = pair_table(trig[1], trig[2]).astype(bf16)
    product = nt_dot(pairs, slots_ref[...])

    @pl.when(step == 0)
    def _():
        total_ref[...] = product

    @pl.when(step > 0)
    def _():
        total_ref[...] += product

    @pl.when(step == pl.num_programs(0) - 1)
    def _():
        for t in range(8):
            out_ref[PAIRS * t : PAIRS * (t + 1), :] = total_ref[0:PAIRS, 128 * t : 128 * t + 128]
        last = total_ref[:, 1024:1088]
        out_ref[2368:2520, :] = jnp.concatenate([last[0:152], last[152:304]], 1)
        out_ref[2520:2560, :] = jnp.zeros((40, 128), f32)


def factors(pick, positions, features, cotangent, block):
    atoms = positions.shape[1]
    return pl.pallas_call(
        factor_kernel,
        grid=(atoms // block,),
        in_specs=[
            pl.BlockSpec(memory_space=pltpu.SMEM),
            pl.BlockSpec((3, block), lambda i: (0, i)),
            pl.BlockSpec((block, 128), lambda i: (i, 0)),
            pl.BlockSpec((block, 128), lambda i: (i, 0)),
        ],
        out_specs=pl.BlockSpec((PACKED, 128), lambda i: (0, 0)),
        out_shape=jax.ShapeDtypeStruct((PACKED, 128), f32),
        scratch_shapes=[pltpu.VMEM((SLOTS, block), bf16), pltpu.VMEM((PAIR_ROWS, SLOTS), f32)],
        compiler_params=pltpu.CompilerParams(vmem_limit_bytes=VMEM_LIMIT),
        cost_estimate=pl.CostEstimate(flops=2 * PAIR_ROWS * SLOTS * atoms, bytes_accessed=atoms * 520, transcendentals=0),
        name="factors",
    )(pick, positions, features, cotangent)


def wave_class(m):
    m0, m1, m2 = [m[d : d + 1, :] for d in range(3)]
    size0, size1, size2 = jnp.abs(m0), jnp.abs(m1), jnp.abs(m2)
    signs = [jnp.clip(v, -1.0, 1.0) for v in (m0, m1, m2)]
    both = (size1 - 1.0) * 8.0 + size2 - 1.0
    inner = jnp.where(
        size1 > 0.0,
        jnp.where(size2 > 0.0, both, 72.0 + size1 - 1.0),
        jnp.where(size2 > 0.0, 64.0 + size2 - 1.0, 80.0),
    )
    tile = jnp.where(size0 > 0.0, size0 - 1.0, 8.0)
    index = (tile * 88.0 + inner).astype(jnp.int32)
    return index, (signs[1] * signs[2], signs[0] * signs[1], signs[0] * signs[2])


def split_hi_lo(v):
    hi = v.astype(bf16)
    return hi, (v - hi.astype(f32)).astype(bf16)


def class_kernel(miller_ref, radial_ref, out_ref):
    step = pl.program_id(0)
    index, products = wave_class(miller_ref[0:3, :])
    radial = radial_ref[...]
    signed = jnp.concatenate([radial] + [radial * p for p in products], 0)
    hi, lo = split_hi_lo(signed)
    hot = (lax.broadcasted_iota(jnp.int32, (CLASSES, index.shape[1]), 0) == index).astype(f32).astype(bf16)
    part = nt_dot(hot, jnp.concatenate([hi, lo], 0))
    part = part[:, :128] + part[:, 128:]

    @pl.when(step == 0)
    def _():
        out_ref[...] = part

    @pl.when(step > 0)
    def _():
        out_ref[...] += part


def class_sums(miller_rows, radial_rows, block):
    waves = miller_rows.shape[1]
    return pl.pallas_call(
        class_kernel,
        grid=(waves // block,),
        in_specs=[pl.BlockSpec((8, block), lambda i: (0, i)), pl.BlockSpec((32, block), lambda i: (0, i))],
        out_specs=pl.BlockSpec((CLASSES, 128), lambda i: (0, 0)),
        out_shape=jax.ShapeDtypeStruct((CLASSES, 128), f32),
        compiler_params=pltpu.CompilerParams(vmem_limit_bytes=VMEM_LIMIT),
        cost_estimate=pl.CostEstimate(flops=2 * CLASSES * 256 * waves, bytes_accessed=waves * 160, transcendentals=0),
        name="class_sums",
    )(miller_rows, radial_rows)


def spread(x, q):
    part = x[:, 32 * q : 32 * q + 32]
    return jnp.concatenate([part, part, part, part], 1)


def combine_kernel(scale, total_ref, class_ref, uv_ref, down_ref, pair_ref):
    lane = lax.broadcasted_iota(jnp.int32, (1, 128), 1)
    half = jnp.where(lane < 64, 1.0, -1.0).astype(f32)
    swap = (lane % 64) < 32
    pick_lane = lax.broadcasted_iota(jnp.int32, (64, 128), 1)
    pick_row = lax.broadcasted_iota(jnp.int32, (64, 128), 0)
    pick = (pick_lane == jnp.where(pick_row < 32, pick_row + 32, pick_row + 64)).astype(bf16)
    pair_ref[...] = jnp.zeros((CLASSES, 128), f32)
    for t in range(TILES):
        if t < 8:
            a = total_ref[PAIRS * t : PAIRS * (t + 1), :]
        else:
            fold = total_ref[2368:2520, :]
            a = jnp.concatenate([fold[:, :64], fold[0:144, 64:]], 0)
            a = jnp.concatenate([a, jnp.zeros((PAIRS, 64), f32)], 1)
        b = half * pltpu.roll(a, 64, 1)
        sa = pltpu.roll(a, 32, 1)
        sb = pltpu.roll(b, 32, 1)
        x = class_ref[88 * t : 88 * t + 88, :] * scale
        x0, x1, x2, x3 = [spread(x, q) for q in range(4)]
        i0, i1, i2, i3 = [v[0:64] for v in (x0, x1, x2, x3)]
        cut = lambda v: [v[0:64], v[64:128], v[128:192], v[192:256]] + [v[256 + 8 * k : 264 + 8 * k] for k in range(5)]
        cc, cs, sc, ss, e2c, e2s, e1c, e1s, co = cut(a)
        bcc, bcs, bsc, bss, be2c, be2s, be1c, be1s, _ = cut(b)
        f0, f3 = x0[64:72], x3[64:72]
        g0, g2 = x0[72:80], x2[72:80]
        w = jnp.concatenate(
            [
                i0 * cc - i1 * ss - i2 * bsc - i3 * bcs,
                i0 * cs + i1 * sc - i2 * bss + i3 * bcc,
                i0 * sc + i1 * cs + i2 * bcc - i3 * bss,
                i0 * ss - i1 * cc + i2 * bcs + i3 * bsc,
                f0 * e2c - f3 * be2s,
                f0 * e2s + f3 * be2c,
                g0 * e1c - g2 * be1s,
                g0 * e1s + g2 * be1c,
                x0[80:88] * co,
                jnp.zeros((8, 128), f32),
            ],
            0,
        )
        swapped = jnp.where(swap, pltpu.roll(w, 96, 1), pltpu.roll(w, 32, 1))
        uv_ref[0:PAIR_ROWS, 128 * t : 128 * t + 128] = swapped.astype(bf16)
        slope = float(t + 1 if t < 8 else 0)
        uv_ref[PAIR_ROWS : 2 * PAIR_ROWS, 128 * t : 128 * t + 128] = (
            (slope * half) * pltpu.roll(swapped, 64, 1)
        ).astype(bf16)
        down_ref[64 * t : 64 * t + 64, :] = nt_dot(pick, w.astype(bf16)).astype(bf16)
        scc, scs, ssc, sss, se2c, se2s, se1c, se1s, sco = cut(sa)
        tcc, tcs, tsc, tss, te2c, te2s, te1c, te1s, _ = cut(sb)
        zero = jnp.zeros((8, 128), f32)
        y = [
            [cc * scc + cs * scs + sc * ssc + ss * sss, e2c * se2c + e2s * se2s, e1c * se1c + e1s * se1s, co * sco],
            [cs * ssc + sc * scs - cc * sss - ss * scc, zero, zero, zero],
            [sc * tcc + ss * tcs - cc * tsc - cs * tss, zero, e1s * te1c - e1c * te1s, zero],
            [cs * tcc + ss * tsc - cc * tcs - sc * tss, e2s * te2c - e2c * te2s, zero, zero],
        ]
        parts = []
        for q in range(4):
            z = jnp.concatenate(y[q], 0)
            parts.append(z[:, 32:64] + z[:, 96:128])
        pair_ref[88 * t : 88 * t + 88, :] = jnp.concatenate(parts, 1)


def combine(total, classes, scale):
    return pl.pallas_call(
        functools.partial(combine_kernel, scale),
        out_shape=(
            jax.ShapeDtypeStruct((2 * PAIR_ROWS, 128 * TILES), bf16),
            jax.ShapeDtypeStruct((64 * TILES, PAIR_ROWS), bf16),
            jax.ShapeDtypeStruct((CLASSES, 128), f32),
        ),
        compiler_params=pltpu.CompilerParams(vmem_limit_bytes=VMEM_LIMIT),
        name="combine",
    )(total, classes)


def filter_kernel(scale, miller_ref, pair_ref, out_ref):
    index, products = wave_class(miller_ref[0:3, :])
    hot = (lax.broadcasted_iota(jnp.int32, (CLASSES, index.shape[1]), 0) == index).astype(f32).astype(bf16)
    turned = pair_ref[...].T
    hi, lo = split_hi_lo(turned)
    values = jnp.dot(jnp.concatenate([hi, lo], 0), hot, preferred_element_type=f32)
    values = values[:128] + values[128:]
    total = values[0:32]
    for q in range(3):
        total = total + products[q] * values[32 * (q + 1) : 32 * (q + 2)]
    out_ref[...] = scale * total


def filter_rows(miller_rows, pair_products, scale, block):
    waves = miller_rows.shape[1]
    return pl.pallas_call(
        functools.partial(filter_kernel, scale),
        grid=(waves // block,),
        in_specs=[pl.BlockSpec((8, block), lambda i: (0, i)), pl.BlockSpec((CLASSES, 128), lambda i: (0, 0))],
        out_specs=pl.BlockSpec((32, block), lambda i: (0, i)),
        out_shape=jax.ShapeDtypeStruct((32, waves), f32),
        compiler_params=pltpu.CompilerParams(vmem_limit_bytes=VMEM_LIMIT),
        cost_estimate=pl.CostEstimate(flops=2 * CLASSES * 256 * waves, bytes_accessed=waves * 160, transcendentals=0),
        name="filter_rows",
    )(miller_rows, pair_products)


def gradient_kernel(pick_ref, pos_ref, feat_ref, cot_ref, uv_ref, down_ref, grad_ref, posg_ref, slots_ref):
    trig = multiples(pos_ref[...])
    (c0, s0), (c1, s1), (c2, s2) = trig
    fill_slots(slots_ref, trig[0], row_tables(pick_ref, feat_ref[...], cot_ref[...]))
    pairs = pair_table(trig[1], trig[2]).astype(bf16)
    parts = jnp.dot(down_ref[...], pairs, preferred_element_type=f32)
    grad = parts[512:544]
    for t in range(8):
        grad = grad + c0[t : t + 1, :] * parts[64 * t : 64 * t + 32] + s0[t : t + 1, :] * parts[64 * t + 32 : 64 * t + 64]
    grad_ref[...] = grad
    both = jnp.dot(uv_ref[:, 0:SLOTS], slots_ref[...], preferred_element_type=f32)
    u = both[0:PAIR_ROWS]
    v = both[PAIR_ROWS:]
    orders = lax.broadcasted_iota(jnp.int32, c1.shape, 0).astype(f32) + 1.0
    acc0 = c2 * v[256:264] + s2 * v[264:272] + c1 * v[272:280] + s1 * v[280:288]
    acc1 = orders * (c1 * u[280:288] - s1 * u[272:280])
    acc2 = c2 * u[264:272] - s2 * u[256:264]
    for m in range(8):
        lead_c, lead_s = c1[m : m + 1, :], s1[m : m + 1, :]
        ucc, ucs, usc, uss = [u[64 * k + 8 * m : 64 * k + 8 * m + 8] for k in range(4)]
        vcc, vcs, vsc, vss = [v[64 * k + 8 * m : 64 * k + 8 * m + 8] for k in range(4)]
        acc0 = acc0 + lead_c * (c2 * vcc + s2 * vcs) + lead_s * (c2 * vsc + s2 * vss)
        acc1 = acc1 + float(m + 1) * (lead_c * (c2 * usc + s2 * uss) - lead_s * (c2 * ucc + s2 * ucs))
        acc2 = acc2 + lead_c * (c2 * ucs - s2 * ucc) + lead_s * (c2 * uss - s2 * usc)
    acc2 = acc2 * orders
    rows = [jnp.sum(acc0, 0, keepdims=True) + v[288:289], jnp.sum(acc1, 0, keepdims=True), jnp.sum(acc2, 0, keepdims=True)]
    posg_ref[...] = phase_step * jnp.concatenate(rows, 0)


def gradients(pick, positions, features, cotangent, uv, down, block):
    atoms = positions.shape[1]
    return pl.pallas_call(
        gradient_kernel,
        grid=(atoms // block,),
        in_specs=[
            pl.BlockSpec(memory_space=pltpu.SMEM),
            pl.BlockSpec((3, block), lambda i: (0, i)),
            pl.BlockSpec((block, 128), lambda i: (i, 0)),
            pl.BlockSpec((block, 128), lambda i: (i, 0)),
            pl.BlockSpec((2 * PAIR_ROWS, 128 * TILES), lambda i: (0, 0)),
            pl.BlockSpec((64 * TILES, PAIR_ROWS), lambda i: (0, 0)),
        ],
        out_specs=(pl.BlockSpec((32, block), lambda i: (0, i)), pl.BlockSpec((3, block), lambda i: (0, i))),
        out_shape=(jax.ShapeDtypeStruct((32, atoms), f32), jax.ShapeDtypeStruct((3, atoms), f32)),
        scratch_shapes=[pltpu.VMEM((SLOTS, block), bf16)],
        compiler_params=pltpu.CompilerParams(vmem_limit_bytes=VMEM_LIMIT),
        cost_estimate=pl.CostEstimate(flops=6 * PAIR_ROWS * SLOTS * atoms, bytes_accessed=atoms * 700, transcendentals=0),
        name="gradients",
    )(pick, positions, features, cotangent, uv, down)


def swap(value, axis):
    return lax.ppermute(value, axis, [(0, 1), (1, 0)])


def sum_scatter(value, axis):
    n = lax.axis_size(axis)
    parts = lax.all_to_all(value.reshape(n, value.shape[0] // n, 128), axis, 0, 0)
    return jnp.sum(parts, 0)


def gather(value, axis):
    n = lax.axis_size(axis)
    copies = jnp.broadcast_to(value[None], (n,) + value.shape)
    return lax.all_to_all(copies, axis, 0, 0).reshape(n * value.shape[0], 128)


def order_channels(own, across, beside, far, y_at, core_at):
    mine_y = jnp.where(y_at == 0, jnp.stack([own, across]), jnp.stack([across, own]))
    other_y = jnp.where(y_at == 0, jnp.stack([beside, far]), jnp.stack([far, beside]))
    even = jnp.where(core_at == 0, mine_y, other_y)
    odd = jnp.where(core_at == 0, other_y, mine_y)
    return jnp.concatenate([even[0], odd[0], even[1], odd[1]], 0).T


def shards(block, positions, features, cotangent, miller, radial_filter):
    atoms = positions.shape[1]
    waves = miller.shape[1]
    y_at, core_at = lax.axis_index("yl"), lax.axis_index("core")
    atom_count = atoms * lax.axis_size(("z", "yh", "x"))
    wave_count = waves * lax.axis_size(("yl", "core"))
    scale = float(atom_count * wave_count) ** (-0.5)
    pick = (2 * y_at + core_at).astype(jnp.int32).reshape(1)

    turned = radial_filter.T.reshape(2, 64, waves)
    indices = jnp.concatenate([miller.astype(f32), jnp.zeros((5, waves), f32)], 0)
    keep = jnp.where(y_at == 0, turned[0], turned[1])
    send = jnp.where(y_at == 0, turned[1], turned[0])
    here = jnp.concatenate([keep, indices], 0)
    there = swap(jnp.concatenate([send, indices], 0), "yl")
    pair = jnp.concatenate([here, there], 1)
    first, second, pair_indices = pair[:32], pair[32:64], pair[64:]
    keep = jnp.where(core_at == 0, first, second)
    send = jnp.where(core_at == 0, second, first)
    beside = swap(jnp.concatenate([send, pair_indices], 0), "core")
    radial_rows = jnp.concatenate([keep, beside[:32]], 1)
    miller_rows = jnp.concatenate([pair_indices, beside[32:]], 1)
    wave_block = min(1024, 4 * waves)
    classes = class_sums(miller_rows, radial_rows, wave_block)

    part = factors(pick, positions, features, cotangent, block)
    part = sum_scatter(part, "x")
    part = sum_scatter(part, "z")
    part = part + swap(part, "yh")
    part = gather(part, "z")
    total = gather(part, "x")
    uv, down, pair_products = combine(total, classes, scale)
    grad, posg = gradients(pick, positions, features, cotangent, uv, down, block)
    across = swap(grad, "yl")
    near = swap(jnp.concatenate([grad, across], 0), "core")
    feature_grad = order_channels(grad, across, near[:32], near[32:], y_at, core_at)
    posg = posg + swap(posg, "core")
    position_grad = posg + swap(posg, "yl")

    rows = filter_rows(miller_rows, pair_products, scale, wave_block).reshape(32, 4, waves)
    came = swap(rows[:, 1::2].reshape(32, 2 * waves), "yl").reshape(32, 2, waves)
    both = jnp.concatenate([rows[:, 0::2], came], 0)
    near = swap(both[:, 1], "core")
    filter_grad = order_channels(both[:32, 0], both[32:, 0], near[:32], near[32:], y_at, core_at)
    return feature_grad, position_grad, filter_grad


def solution(mesh):
    x, yh = 4, 2
    z = mesh.shape["atom"] // (x * yh)
    fine = Mesh(mesh.devices.reshape(z, yh, x, 2, 2), ("z", "yh", "x", "yl", "core"))
    atom, wave = ("z", "yh", "x"), ("yl", "core")
    placed = (P(None, atom), P(atom, None), P(atom, None), P(None, wave), P(wave, None))
    return jax.shard_map(
        functools.partial(shards, 512),
        mesh=fine,
        in_specs=placed,
        out_specs=(P(atom, None), P(None, atom), P(wave, None)),
        check_vma=False,
    )
```

time: 917 us -> 140 us (0.15)
  waiting for transfers between devices: 659 us -> 37.9 us
  matrix products: 105 us -> 0 us
  other arithmetic: 73.6 us -> 4.64 us
  blocking collectives: 56.5 us -> 0 us
  starting transfers between devices: 0.26 us -> 45.5 us
  Pallas kernels: 0 us -> 41.6 us
  between operations: 14.1 us -> 0.88 us
    psum x2 -> x0, waiting for transfers between devices: 659 us -> none  [the longest x1 659 us: shards(): totals = lax.psum(local_factors, 'atom')]
    dot_general x4 -> x0, matrix products: 105 us -> none  [the longest x1 72.6 us: shards(): lax.dot_general(miller.astype(jnp.bfloat16), dtheta, (((1,), (1,)), ((),...]
    convert_element_type x2 -> x1, other arithmetic: 69.6 us -> 0.01 us  [shards(): miller.astype(f32)]
    psum x1 -> x0, blocking collectives: 56.5 us -> none  [shards(): feature_grad, position_grad = lax.psum((feat_part, pos_part), 'wave')]
    pallas_call x0 -> x5, Pallas kernels: none -> 41.6 us  [the longest x1 14.8 us: gradients(): pl.pallas_call(gradient_kernel, grid=(atoms // block,), in_specs=[pl.Bloc...]
    all_to_all x0 -> x4, waiting for transfers between devices: none -> 33.9 us  [the longest x2 24.9 us: sum_scatter(): lax.all_to_all(value.reshape(n, value.shape[0] // n, 128), axis, 0, 0)]
    ppermute x0 -> x9, starting transfers between devices: none -> 24.4 us  [swap(): return lax.ppermute(value, axis, [(0, 1), (1, 0)])]
    all_to_all x0 -> x4, starting transfers between devices: none -> 21.1 us  [the longest x2 14.1 us: sum_scatter(): lax.all_to_all(value.reshape(n, value.shape[0] // n, 128), axis, 0, 0)]
  transfers between devices with their start and end apart: 2 -> 13, of which waited for: 1 -> 8; matrix products, arithmetic and copies ran while one was open for 10% -> 5% of each run, Pallas kernels for 0% -> 7%
where the time goes in v1:
time: 140 us; the launch traced here: 139 us
  starting transfers between devices  45.5 us (32%)
  Pallas kernels  41.6 us (30%)
  waiting for transfers between devices  37.9 us (27%)
  local copies, waits for them, and re-layouts  8.93 us (6%)
  other arithmetic  4.64 us (3%)
    all_to_all x2, waiting for transfers between devices, sum_scatter(): lax.all_to_all(value.reshape(n, value.shape[0] // n, 128), axis, 0, 0)  24.9 us
    ppermute x9, starting transfers between devices, swap(): return lax.ppermute(value, axis, [(0, 1), (1, 0)])  24.4 us
    pallas_call x1, Pallas kernels, gradients(): pl.pallas_call(gradient_kernel, grid=(atoms // block,), in_specs=[pl.Bloc...  14.8 us
    all_to_all x2, starting transfers between devices, sum_scatter(): lax.all_to_all(value.reshape(n, value.shape[0] // n, 128), axis, 0, 0)  14.1 us
    pallas_call x1, Pallas kernels, factors(): pl.pallas_call(factor_kernel, grid=(atoms // block,), in_specs=[pl.BlockS...  9.85 us
    all_to_all x2, waiting for transfers between devices, gather(): return lax.all_to_all(copies, axis, 0, 0).reshape(n * value.shape[0], 128)  9.05 us
    pallas_call x1, Pallas kernels, combine(): pl.pallas_call(functools.partial(combine_kernel, scale), out_shape=(jax.S...  7.23 us
    all_to_all x2, starting transfers between devices, gather(): return lax.all_to_all(copies, axis, 0, 0).reshape(n * value.shape[0], 128)  6.97 us
  transfers between devices with their start and end apart: 13, of which 8 were waited for; matrix products, arithmetic and copies ran while one was open for 5% of the time, Pallas kernels for 7%

profile of v1, /device:TPU:1, one launch (start us, length us, event | category | flops | bytes accessed | tf_op | source)
XLA Modules:
  0.0 139.4 jit_solution(1787887790225136276)
XLA Ops:
  0.6 9.9 %factors.1 = f32[2560,128]{1,0:T(8,128)} custom-call(s32[1]{0:T(128)} %bitcast.pick_ref, f32[3,4096]{1,0:T(4,128)} %pos_ref.3, bf16[4096,128]{1,0:T(8,128)(2,1)} %feat_ref.3, bf16[4096,128]{1,0:T(8,128)(2,1)} %cot_ref.3), custom_call_target="tpu_custom_call" | custom-call | flops 2709520384 | bytes 2129920 | tf_op jit(solution)/shard_map/factors/pallas_call | solution.py:99
  10.5 5.0 %all-to-all-start = ((f32[4,640,128]{2,1,0:T(8,128)}), f32[4,640,128]{2,1,0:T(8,128)S(1)}, u32[]{:S(2)}, u32[]{:S(2)}) async-start(f32[4,640,128]{2,1,0:T(8,128)} %bitcast.54), calls=%async_computation | async-start | bytes 2621440 | tf_op jit(solution)/shard_map/all_to_all | solution.py:336
  15.7 15.8 %all-to-all-done = f32[4,640,128]{2,1,0:T(8,128)S(1)} async-done(((f32[4,640,128]{2,1,0:T(8,128)}), f32[4,640,128]{2,1,0:T(8,128)S(1)}, u32[]{:S(2)}, u32[]{:S(2)}) %all-to-all-start) | async-done | bytes 1310752 | tf_op jit(solution)/shard_map/all_to_all | solution.py:336
  32.3 9.2 %all-to-all-start.1 = ((f32[8,80,128]{2,1,0:T(8,128)}), f32[8,80,128]{2,1,0:T(8,128)S(1)}, u32[]{:S(2)}, u32[]{:S(2)}) async-start(f32[8,80,128]{2,1,0:T(8,128)} %bitcast.2), calls=%async_computation.1 | async-start | bytes 655360 | tf_op jit(solution)/shard_map/all_to_all | solution.py:336
  41.6 1.4 collective-permute-start.1
  42.9 9.1 %all-to-all-done.1 = f32[8,80,128]{2,1,0:T(8,128)S(1)} async-done(((f32[8,80,128]{2,1,0:T(8,128)}), f32[8,80,128]{2,1,0:T(8,128)S(1)}, u32[]{:S(2)}, u32[]{:S(2)}) %all-to-all-start.1) | async-done | bytes 327712 | tf_op jit(solution)/shard_map/all_to_all | solution.py:336
  52.1 3.0 %collective-permute-start = (f32[80,128]{1,0:T(8,128)S(1)}, f32[80,128]{1,0:T(8,128)S(1)}, u32[]{:S(2)}, u32[]{:S(2)}) collective-permute-start(f32[80,128]{1,0:T(8,128)S(1)} %reduce_sum.19), channel_id=1, source_target_pairs={{0,16},{16,0},{1,17},{17,1},{2,18},{18,2},{3,19},{19,3},{4,20},{20... | collective-permute-start | bytes 122888 | tf_op jit(solution)/shard_map/ppermute | solution.py:331
  55.1 1.4 %collective-permute-done = f32[80,128]{1,0:T(8,128)S(1)} collective-permute-done((f32[80,128]{1,0:T(8,128)S(1)}, f32[80,128]{1,0:T(8,128)S(1)}, u32[]{:S(2)}, u32[]{:S(2)}) %collective-permute-start) | collective-permute-done | bytes 40992 | tf_op jit(solution)/shard_map/ppermute | solution.py:331
  57.3 3.4 %all-to-all-start.2 = ((f32[8,80,128]{2,1,0:T(8,128)}), f32[8,80,128]{2,1,0:T(8,128)S(1)}, u32[]{:S(2)}, u32[]{:S(2)}) async-start(f32[8,80,128]{2,1,0:T(8,128)} %broadcast_in_dim.16), calls=%async_computation.2 | async-start | bytes 655360 | tf_op jit(solution)/shard_map/all_to_all | solution.py:343
  60.7 4.9 %collective-permute-start.2 = (f32[40,2048]{1,0:T(8,128)S(1)}, f32[40,2048]{1,0:T(8,128)S(1)}, u32[]{:S(2)}, u32[]{:S(2)}) collective-permute-start(f32[40,2048]{1,0:T(8,128)S(1)} %pad_maximum_fusion.2), channel_id=1, source_target_pairs={{0,1},{1,0},{2,3},{3,2},{4,5},{5,4},{6,7},{7,6},{8,9},{9,8},{10,11... | collective-permute-start | bytes 983048 | tf_op jit(solution)/shard_map/ppermute | solution.py:331
  65.7 1.3 collective-permute-done.2
  66.9 3.7 %all-to-all-done.2 = f32[8,80,128]{2,1,0:T(8,128)S(1)} async-done(((f32[8,80,128]{2,1,0:T(8,128)}), f32[8,80,128]{2,1,0:T(8,128)S(1)}, u32[]{:S(2)}, u32[]{:S(2)}) %all-to-all-start.2) | async-done | bytes 327712 | tf_op jit(solution)/shard_map/all_to_all | solution.py:343
  71.8 3.5 %all-to-all-start.3 = ((f32[4,640,128]{2,1,0:T(8,128)}), f32[4,640,128]{2,1,0:T(8,128)S(1)}, u32[]{:S(2)}, u32[]{:S(2)}) async-start(f32[4,640,128]{2,1,0:T(8,128)} %broadcast_in_dim.18), calls=%async_computation.3 | async-start | bytes 2621440 | tf_op jit(solution)/shard_map/all_to_all | solution.py:343
  76.8 4.8 %class_sums.1.class_ref = f32[896,128]{1,0:T(8,128)} custom-call(f32[8,4096]{1,0:T(8,128)} %pad_maximum_fusion.9.miller_ref, f32[32,4096]{1,0:T(8,128)} %pad_maximum_fusion.1.radial_ref), custom_call_target="tpu_custom_call" | custom-call | flops 1879048192 | bytes 655360 | tf_op jit(solution)/shard_map/class_sums/pallas_call | solution.py:158
  81.6 5.3 %all-to-all-done.3 = f32[4,640,128]{2,1,0:T(8,128)S(1)} async-done(((f32[4,640,128]{2,1,0:T(8,128)}), f32[4,640,128]{2,1,0:T(8,128)S(1)}, u32[]{:S(2)}, u32[]{:S(2)}) %all-to-all-start.3) | async-done | bytes 1310752 | tf_op jit(solution)/shard_map/all_to_all | solution.py:343
  88.1 7.2 %combine.1 = (bf16[608,1152]{1,0:T(8,128)(2,1)}, bf16[576,304]{1,0:T(8,128)(2,1)}, f32[896,128]{1,0:T(8,128)}) custom-call(f32[2560,128]{1,0:T(8,128)} %bitcast.48, f32[896,128]{1,0:T(8,128)} %class_sums.1.class_ref), custom_call_target="tpu_custom_call" | custom-call | tf_op jit(solution)/shard_map/combine/pallas_call | solution.py:240
  95.3 14.8 %gradients.1 = (f32[32,4096]{1,0:T(8,128)}, f32[3,4096]{1,0:T(4,128)}) custom-call(s32[1]{0:T(128)} %bitcast.pick_ref, f32[3,4096]{1,0:T(4,128)} %pos_ref.3, bf16[4096,128]{1,0:T(8,128)(2,1)} %feat_ref.3, bf16[4096,128]{1,0:T(8,128)(2,1)} %cot_ref.3, bf16[608,1152]{1,0:T(8,128)(2,1)} %get-tuple-element.8.uv_ref, bf16[576,304]{1,0:T(8,128)(2,1)} %get-tuple-element.9.down_ref), custom_call_target="tpu_custom_call" | custom-call | flops 8128561152 | bytes 2867200 | tf_op jit(solution)/shard_map/gradients/pallas_call | solution.py:310
  110.0 1.3 collective-permute-start.3
  111.3 4.9 %filter_rows.1 = f32[32,4096]{1,0:T(8,128)} custom-call(f32[8,4096]{1,0:T(8,128)} %pad_maximum_fusion.9.miller_ref, f32[896,128]{1,0:T(8,128)} %get-tuple-element.12.pair_ref), custom_call_target="tpu_custom_call" | custom-call | flops 1879048192 | bytes 655360 | tf_op jit(solution)/shard_map/filter_rows/pallas_call | solution.py:267
  116.3 1.5 %reshape.38 = f32[32,4,1024]{2,1,0:T(4,128)S(1)} reshape(f32[32,4096]{1,0:T(8,128)} %filter_rows.1) | data formatting | bytes 1048576 | tf_op jit(solution)/shard_map/reshape | solution.py:393
  118.6 7.7 %collective-permute-start.5 = (f32[3,4096]{1,0:T(4,128)S(1)}, f32[3,4096]{1,0:T(4,128)S(1)}, u32[]{:S(2)}, u32[]{:S(2)}) collective-permute-start(f32[3,4096]{1,0:T(4,128)S(1)} %copy-done.3), channel_id=1, source_target_pairs={{0,1},{1,0},{2,3},{3,2},{4,5},{5,4},{6,7},{7,6},{8,9},{9,8},{10,11... | collective-permute-start | bytes 147464 | tf_op jit(solution)/shard_map/ppermute | solution.py:331
  127.2 1.4 collective-permute-start.6
  128.7 4.4 %collective-permute-start.8 = (f32[64,1024]{1,0:T(8,128)S(1)}, f32[64,1024]{1,0:T(8,128)S(1)}, u32[]{:S(2)}, u32[]{:S(2)}) collective-permute-start(f32[64,1024]{1,0:T(8,128)S(1)} %fusion.2), channel_id=1, source_target_pairs={{0,1},{1,0},{2,3},{3,2},{4,5},{5,4},{6,7},{7,6},{8,9},{9,8},{10,11... | collective-permute-start | bytes 786440 | tf_op jit(solution)/shard_map/ppermute | solution.py:331
  137.6 1.8 %copy.22 = f32[4096,128]{1,0:T(8,128)} copy(f32[4096,128]{0,1:T(8,128)S(1)} %maximum_bitcast_fusion) | data formatting | bytes 4194304
  (56 shorter events, 11.9 us)
Async XLA Ops:
  10.5 5.0 %copy-start.4 = (s32[3,1024]{1,0:T(4,128)S(1)}, s32[3,1024]{1,0:T(4,128)}, u32[]{:S(2)}) copy-start(s32[3,1024]{1,0:T(4,128)} %param.8) | copy-start | bytes 36868
  10.5 5.0 %copy-start.2 = (f32[1024,128]{1,0:T(8,128)S(1)}, f32[1024,128]{1,0:T(8,128)}, u32[]{:S(2)}) copy-start(f32[1024,128]{1,0:T(8,128)} %param.9) | copy-start | bytes 1572868
  10.5 21.0 %all-to-all-start = ((f32[4,640,128]{2,1,0:T(8,128)}), f32[4,640,128]{2,1,0:T(8,128)S(1)}, u32[]{:S(2)}, u32[]{:S(2)}) async-start(f32[4,640,128]{2,1,0:T(8,128)} %bitcast.54), calls=%async_computation | async-start | bytes 2621440 | tf_op jit(solution)/shard_map/all_to_all | solution.py:336
  32.3 19.7 %all-to-all-start.1 = ((f32[8,80,128]{2,1,0:T(8,128)}), f32[8,80,128]{2,1,0:T(8,128)S(1)}, u32[]{:S(2)}, u32[]{:S(2)}) async-start(f32[8,80,128]{2,1,0:T(8,128)} %bitcast.2), calls=%async_computation.1 | async-start | bytes 655360 | tf_op jit(solution)/shard_map/all_to_all | solution.py:336
  41.6 13.5 %collective-permute-start.1 = (f32[72,1024]{1,0:T(8,128)S(1)}, f32[72,1024]{1,0:T(8,128)S(1)}, u32[]{:S(2)}, u32[]{:S(2)}) collective-permute-start(f32[72,1024]{1,0:T(8,128)S(1)} %pad_maximum_fusion.3), channel_id=1, source_target_pairs={{0,2},{2,0},{1,3},{3,1},{4,6},{6,4},{5,7},{7,5},{8,10},{10,8},{9,1... | collective-permute-start | bytes 884744 | tf_op jit(solution)/shard_map/ppermute | solution.py:331
  52.1 4.4 %collective-permute-start = (f32[80,128]{1,0:T(8,128)S(1)}, f32[80,128]{1,0:T(8,128)S(1)}, u32[]{:S(2)}, u32[]{:S(2)}) collective-permute-start(f32[80,128]{1,0:T(8,128)S(1)} %reduce_sum.19), channel_id=1, source_target_pairs={{0,16},{16,0},{1,17},{17,1},{2,18},{18,2},{3,19},{19,3},{4,20},{20... | collective-permute-start | bytes 122888 | tf_op jit(solution)/shard_map/ppermute | solution.py:331
  57.3 13.4 %all-to-all-start.2 = ((f32[8,80,128]{2,1,0:T(8,128)}), f32[8,80,128]{2,1,0:T(8,128)S(1)}, u32[]{:S(2)}, u32[]{:S(2)}) async-start(f32[8,80,128]{2,1,0:T(8,128)} %broadcast_in_dim.16), calls=%async_computation.2 | async-start | bytes 655360 | tf_op jit(solution)/shard_map/all_to_all | solution.py:343
  60.7 6.2 %collective-permute-start.2 = (f32[40,2048]{1,0:T(8,128)S(1)}, f32[40,2048]{1,0:T(8,128)S(1)}, u32[]{:S(2)}, u32[]{:S(2)}) collective-permute-start(f32[40,2048]{1,0:T(8,128)S(1)} %pad_maximum_fusion.2), channel_id=1, source_target_pairs={{0,1},{1,0},{2,3},{3,2},{4,5},{5,4},{6,7},{7,6},{8,9},{9,8},{10,11... | collective-permute-start | bytes 983048 | tf_op jit(solution)/shard_map/ppermute | solution.py:331
  71.8 15.2 %all-to-all-start.3 = ((f32[4,640,128]{2,1,0:T(8,128)}), f32[4,640,128]{2,1,0:T(8,128)S(1)}, u32[]{:S(2)}, u32[]{:S(2)}) async-start(f32[4,640,128]{2,1,0:T(8,128)} %broadcast_in_dim.18), calls=%async_computation.3 | async-start | bytes 2621440 | tf_op jit(solution)/shard_map/all_to_all | solution.py:343
  87.0 1.1 copy-start
  110.0 23.0 %collective-permute-start.3 = (f32[32,4096]{1,0:T(8,128)}, f32[32,4096]{1,0:T(8,128)S(1)}, u32[]{:S(2)}, u32[]{:S(2)}) collective-permute-start(f32[32,4096]{1,0:T(8,128)} %get-tuple-element.10), channel_id=1, source_target_pairs={{0,2},{2,0},{1,3},{3,1},{4,6},{6,4},{5,7},{7,5},{8,10},{10,8},{9,1... | collective-permute-start | bytes 1572872 | tf_op jit(solution)/shard_map/ppermute | solution.py:331
  116.3 2.3 %copy-start.3 = (f32[3,4096]{1,0:T(4,128)S(1)}, f32[3,4096]{1,0:T(4,128)}, u32[]{:S(2)}) copy-start(f32[3,4096]{1,0:T(4,128)} %get-tuple-element.11) | copy-start | bytes 147460
  116.3 16.8 %copy-start.1 = (f32[32,4096]{1,0:T(8,128)S(1)}, f32[32,4096]{1,0:T(8,128)}, u32[]{:S(2)}) copy-start(f32[32,4096]{1,0:T(8,128)} %get-tuple-element.10) | copy-start | bytes 1572868
  118.3 10.3 %collective-permute-start.7 = (f32[32,2048]{1,0:T(8,128)S(1)}, f32[32,2048]{1,0:T(8,128)S(1)}, u32[]{:S(2)}, u32[]{:S(2)}) collective-permute-start(f32[32,2048]{1,0:T(8,128)S(1)} %bitcast.57), channel_id=1, source_target_pairs={{0,2},{2,0},{1,3},{3,1},{4,6},{6,4},{5,7},{7,5},{8,10},{10,8},{9,1... | collective-permute-start | bytes 786440 | tf_op jit(solution)/shard_map/ppermute | solution.py:331
  118.6 8.6 %collective-permute-start.5 = (f32[3,4096]{1,0:T(4,128)S(1)}, f32[3,4096]{1,0:T(4,128)S(1)}, u32[]{:S(2)}, u32[]{:S(2)}) collective-permute-start(f32[3,4096]{1,0:T(4,128)S(1)} %copy-done.3), channel_id=1, source_target_pairs={{0,1},{1,0},{2,3},{3,2},{4,5},{5,4},{6,7},{7,6},{8,9},{9,8},{10,11... | collective-permute-start | bytes 147464 | tf_op jit(solution)/shard_map/ppermute | solution.py:331
  127.2 6.9 %collective-permute-start.6 = (f32[3,4096]{1,0:T(4,128)S(1)}, f32[3,4096]{1,0:T(4,128)S(1)}, u32[]{:S(2)}, u32[]{:S(2)}) collective-permute-start(f32[3,4096]{1,0:T(4,128)S(1)} %add.14), channel_id=1, source_target_pairs={{0,2},{2,0},{1,3},{3,1},{4,6},{6,4},{5,7},{7,5},{8,10},{10,8},{9,1... | collective-permute-start | bytes 147464 | tf_op jit(solution)/shard_map/ppermute | solution.py:331
  128.7 6.2 %collective-permute-start.8 = (f32[64,1024]{1,0:T(8,128)S(1)}, f32[64,1024]{1,0:T(8,128)S(1)}, u32[]{:S(2)}, u32[]{:S(2)}) collective-permute-start(f32[64,1024]{1,0:T(8,128)S(1)} %fusion.2), channel_id=1, source_target_pairs={{0,1},{1,0},{2,3},{3,2},{4,5},{5,4},{6,7},{7,6},{8,9},{9,8},{10,11... | collective-permute-start | bytes 786440 | tf_op jit(solution)/shard_map/ppermute | solution.py:331
  134.1 2.9 %collective-permute-start.4 = (f32[64,4096]{1,0:T(8,128)}, f32[64,4096]{1,0:T(8,128)S(1)}, u32[]{:S(2)}, u32[]{:S(2)}) collective-permute-start(f32[64,4096]{1,0:T(8,128)} %pad_maximum_fusion), channel_id=1, source_target_pairs={{0,1},{1,0},{2,3},{3,2},{4,5},{5,4},{6,7},{7,6},{8,9},{9,8},{10,11... | collective-permute-start | bytes 3145736 | tf_op jit(solution)/shard_map/ppermute | solution.py:331

commit v2 on v1

--- a/solution.py
+++ b/solution.py
@@ -70,12 +70,17 @@
     slots_ref[1024:1088, :] = rows.astype(bf16)
 
 
-def factor_kernel(pick_ref, pos_ref, feat_ref, cot_ref, out_ref, slots_ref, total_ref):
+def factor_kernel(pick_ref, pos_ref, feat_ref, cot_ref, out_ref, total_ref, *slots_refs):
     step = pl.program_id(0)
-    trig = multiples(pos_ref[...])
-    fill_slots(slots_ref, trig[0], row_tables(pick_ref, feat_ref[...], cot_ref[...]))
-    pairs = pair_table(trig[1], trig[2]).astype(bf16)
-    product = nt_dot(pairs, slots_ref[...])
+    size = slots_refs[0].shape[1]
+    product = None
+    for k, slots_ref in enumerate(slots_refs):
+        at = slice(k * size, (k + 1) * size)
+        trig = multiples(pos_ref[:, at])
+        fill_slots(slots_ref, trig[0], row_tables(pick_ref, feat_ref[at, :], cot_ref[at, :]))
+        pairs = pair_table(trig[1], trig[2]).astype(bf16)
+        part = nt_dot(pairs, slots_ref[...])
+        product = part if product is None else product + part
 
     @pl.when(step == 0)
     def _():
@@ -94,7 +99,7 @@
         out_ref[2520:2560, :] = jnp.zeros((40, 128), f32)
 
 
-def factors(pick, positions, features, cotangent, block):
+def factors(pick, positions, features, cotangent, block, cuts):
     atoms = positions.shape[1]
     return pl.pallas_call(
         factor_kernel,
@@ -107,7 +112,7 @@
         ],
         out_specs=pl.BlockSpec((PACKED, 128), lambda i: (0, 0)),
         out_shape=jax.ShapeDtypeStruct((PACKED, 128), f32),
-        scratch_shapes=[pltpu.VMEM((SLOTS, block), bf16), pltpu.VMEM((PAIR_ROWS, SLOTS), f32)],
+        scratch_shapes=[pltpu.VMEM((PAIR_ROWS, SLOTS), f32)] + [pltpu.VMEM((SLOTS, block // cuts), bf16)] * cuts,
         compiler_params=pltpu.CompilerParams(vmem_limit_bytes=VMEM_LIMIT),
         cost_estimate=pl.CostEstimate(flops=2 * PAIR_ROWS * SLOTS * atoms, bytes_accessed=atoms * 520, transcendentals=0),
         name="factors",
@@ -134,7 +139,7 @@
     return hi, (v - hi.astype(f32)).astype(bf16)
 
 
-def class_kernel(miller_ref, radial_ref, out_ref):
+def class_kernel(scale, miller_ref, radial_ref, out_ref, sum_ref):
     step = pl.program_id(0)
     index, products = wave_class(miller_ref[0:3, :])
     radial = radial_ref[...]
@@ -146,60 +151,67 @@
 
     @pl.when(step == 0)
     def _():
-        out_ref[...] = part
+        sum_ref[...] = part
 
     @pl.when(step > 0)
     def _():
-        out_ref[...] += part
-
-
-def class_sums(miller_rows, radial_rows, block):
+        sum_ref[...] += part
+
+    @pl.when(step == pl.num_programs(0) - 1)
+    def _():
+        for q in range(4):
+            one = sum_ref[:, 32 * q : 32 * q + 32] * scale
+            out_ref[q] = jnp.concatenate([one, one, one, one], 1)
+
+
+def class_sums(miller_rows, radial_rows, scale, block):
     waves = miller_rows.shape[1]
     return pl.pallas_call(
-        class_kernel,
+        functools.partial(class_kernel, scale),
         grid=(waves // block,),
         in_specs=[pl.BlockSpec((8, block), lambda i: (0, i)), pl.BlockSpec((32, block), lambda i: (0, i))],
-        out_specs=pl.BlockSpec((CLASSES, 128), lambda i: (0, 0)),
-        out_shape=jax.ShapeDtypeStruct((CLASSES, 128), f32),
+        out_specs=pl.BlockSpec((4, CLASSES, 128), lambda i: (0, 0, 0)),
+        out_shape=jax.ShapeDtypeStruct((4, CLASSES, 128), f32),
+        scratch_shapes=[pltpu.VMEM((CLASSES, 128), f32)],
         compiler_params=pltpu.CompilerParams(vmem_limit_bytes=VMEM_LIMIT),
         cost_estimate=pl.CostEstimate(flops=2 * CLASSES * 256 * waves, bytes_accessed=waves * 160, transcendentals=0),
         name="class_sums",
     )(miller_rows, radial_rows)
 
 
-def spread(x, q):
-    part = x[:, 32 * q : 32 * q + 32]
-    return jnp.concatenate([part, part, part, part], 1)
-
-
-def combine_kernel(scale, total_ref, class_ref, uv_ref, down_ref, pair_ref):
+def load_tile(total_ref, t):
+    if t < 8:
+        return total_ref[PAIRS * t : PAIRS * (t + 1), :]
+    fold = total_ref[2368:2520, :]
+    last = jnp.concatenate([fold[:, :64], fold[0:144, 64:]], 0)
+    return jnp.concatenate([last, jnp.zeros((PAIRS, 64), f32)], 1)
+
+
+def lane_signs():
     lane = lax.broadcasted_iota(jnp.int32, (1, 128), 1)
-    half = jnp.where(lane < 64, 1.0, -1.0).astype(f32)
+    return lane, jnp.where(lane < 64, 1.0, -1.0).astype(f32)
+
+
+def cut(v):
+    return [v[0:64], v[64:128], v[128:192], v[192:256]] + [v[256 + 8 * k : 264 + 8 * k] for k in range(5)]
+
+
+def combine(total_ref, class_ref, uv_ref, down_ref):
+    lane, half = lane_signs()
     swap = (lane % 64) < 32
     pick_lane = lax.broadcasted_iota(jnp.int32, (64, 128), 1)
     pick_row = lax.broadcasted_iota(jnp.int32, (64, 128), 0)
     pick = (pick_lane == jnp.where(pick_row < 32, pick_row + 32, pick_row + 64)).astype(bf16)
-    pair_ref[...] = jnp.zeros((CLASSES, 128), f32)
     for t in range(TILES):
-        if t < 8:
-            a = total_ref[PAIRS * t : PAIRS * (t + 1), :]
-        else:
-            fold = total_ref[2368:2520, :]
-            a = jnp.concatenate([fold[:, :64], fold[0:144, 64:]], 0)
-            a = jnp.concatenate([a, jnp.zeros((PAIRS, 64), f32)], 1)
-        b = half * pltpu.roll(a, 64, 1)
-        sa = pltpu.roll(a, 32, 1)
-        sb = pltpu.roll(b, 32, 1)
-        x = class_ref[88 * t : 88 * t + 88, :] * scale
-        x0, x1, x2, x3 = [spread(x, q) for q in range(4)]
+        a = load_tile(total_ref, t)
+        x0, x1, x2, x3 = [class_ref[q, 88 * t : 88 * t + 88, :] for q in range(4)]
         i0, i1, i2, i3 = [v[0:64] for v in (x0, x1, x2, x3)]
-        cut = lambda v: [v[0:64], v[64:128], v[128:192], v[192:256]] + [v[256 + 8 * k : 264 + 8 * k] for k in range(5)]
         cc, cs, sc, ss, e2c, e2s, e1c, e1s, co = cut(a)
-        bcc, bcs, bsc, bss, be2c, be2s, be1c, be1s, _ = cut(b)
         f0, f3 = x0[64:72], x3[64:72]
         g0, g2 = x0[72:80], x2[72:80]
-        w = jnp.concatenate(
-            [
+        if t < 8:
+            bcc, bcs, bsc, bss, be2c, be2s, be1c, be1s, _ = cut(half * pltpu.roll(a, 64, 1))
+            blocks = [
                 i0 * cc - i1 * ss - i2 * bsc - i3 * bcs,
                 i0 * cs + i1 * sc - i2 * bss + i3 * bcc,
                 i0 * sc + i1 * cs + i2 * bcc - i3 * bss,
@@ -208,18 +220,30 @@
                 f0 * e2s + f3 * be2c,
                 g0 * e1c - g2 * be1s,
                 g0 * e1s + g2 * be1c,
-                x0[80:88] * co,
-                jnp.zeros((8, 128), f32),
-            ],
-            0,
-        )
+            ]
+        else:
+            blocks = [i0 * cc - i1 * ss, i0 * cs + i1 * sc, i0 * sc + i1 * cs, i0 * ss - i1 * cc]
+            blocks += [f0 * e2c, f0 * e2s, g0 * e1c, g0 * e1s]
+        w = jnp.concatenate(blocks + [x0[80:88] * co, jnp.zeros((8, 128), f32)], 0)
         swapped = jnp.where(swap, pltpu.roll(w, 96, 1), pltpu.roll(w, 32, 1))
         uv_ref[0:PAIR_ROWS, 128 * t : 128 * t + 128] = swapped.astype(bf16)
-        slope = float(t + 1 if t < 8 else 0)
-        uv_ref[PAIR_ROWS : 2 * PAIR_ROWS, 128 * t : 128 * t + 128] = (
-            (slope * half) * pltpu.roll(swapped, 64, 1)
-        ).astype(bf16)
+        if t < 8:
+            slope = (t + 1.0) * half * pltpu.roll(swapped, 64, 1)
+        else:
+            slope = jnp.zeros((PAIR_ROWS, 128), f32)
+        uv_ref[PAIR_ROWS : 2 * PAIR_ROWS, 128 * t : 128 * t + 128] = slope.astype(bf16)
         down_ref[64 * t : 64 * t + 64, :] = nt_dot(pick, w.astype(bf16)).astype(bf16)
+
+
+def pair_products(total_ref, pair_ref):
+    _, half = lane_signs()
+    pair_ref[...] = jnp.zeros((CLASSES, 128), f32)
+    for t in range(TILES):
+        a = load_tile(total_ref, t)
+        b = half * pltpu.roll(a, 64, 1)
+        sa = pltpu.roll(a, 32, 1)
+        sb = pltpu.roll(b, 32, 1)
+        cc, cs, sc, ss, e2c, e2s, e1c, e1s, co = cut(a)
         scc, scs, ssc, sss, se2c, se2s, se1c, se1s, sco = cut(sa)
         tcc, tcs, tsc, tss, te2c, te2s, te1c, te1s, _ = cut(sb)
         zero = jnp.zeros((8, 128), f32)
@@ -236,59 +260,109 @@
         pair_ref[88 * t : 88 * t + 88, :] = jnp.concatenate(parts, 1)
 
 
-def combine(total, classes, scale):
-    return pl.pallas_call(
-        functools.partial(combine_kernel, scale),
-        out_shape=(
-            jax.ShapeDtypeStruct((2 * PAIR_ROWS, 128 * TILES), bf16),
-            jax.ShapeDtypeStruct((64 * TILES, PAIR_ROWS), bf16),
-            jax.ShapeDtypeStruct((CLASSES, 128), f32),
-        ),
-        compiler_params=pltpu.CompilerParams(vmem_limit_bytes=VMEM_LIMIT),
-        name="combine",
-    )(total, classes)
-
-
-def filter_kernel(scale, miller_ref, pair_ref, out_ref):
+def filter_kernel(scale, miller_ref, total_ref, own_ref, beside_ref, send_ref, pair_ref, turned_ref):
+    step = pl.program_id(0)
+
+    @pl.when(step == 0)
+    def _():
+        pair_products(total_ref, pair_ref)
+        hi, lo = split_hi_lo(pair_ref[...].T)
+        turned_ref[0:128, :] = hi
+        turned_ref[128:256, :] = lo
+
     index, products = wave_class(miller_ref[0:3, :])
     hot = (lax.broadcasted_iota(jnp.int32, (CLASSES, index.shape[1]), 0) == index).astype(f32).astype(bf16)
-    turned = pair_ref[...].T
-    hi, lo = split_hi_lo(turned)
-    values = jnp.dot(jnp.concatenate([hi, lo], 0), hot, preferred_element_type=f32)
+    values = jnp.dot(turned_ref[...], hot, preferred_element_type=f32)
     values = values[:128] + values[128:]
-    total = values[0:32]
+    rows = values[0:32]
     for q in range(3):
-        total = total + products[q] * values[32 * (q + 1) : 32 * (q + 2)]
-    out_ref[...] = scale * total
-
-
-def filter_rows(miller_rows, pair_products, scale, block):
-    waves = miller_rows.shape[1]
+        rows = rows + products[q] * values[32 * (q + 1) : 32 * (q + 2)]
+    rows = scale * rows
+
+    @pl.when(step == 0)
+    def _():
+        own_ref[...] = rows
+
+    @pl.when(step == 2)
+    def _():
+        beside_ref[...] = rows
+
+    @pl.when(lax.rem(step, 2) == 1)
+    def _():
+        send_ref[0] = rows
+
+
+def filter_rows(miller_rows, total, scale):
+    block = miller_rows.shape[1] // 4
+    one = jax.ShapeDtypeStruct((32, block), f32)
     return pl.pallas_call(
         functools.partial(filter_kernel, scale),
-        grid=(waves // block,),
-        in_specs=[pl.BlockSpec((8, block), lambda i: (0, i)), pl.BlockSpec((CLASSES, 128), lambda i: (0, 0))],
-        out_specs=pl.BlockSpec((32, block), lambda i: (0, i)),
-        out_shape=jax.ShapeDtypeStruct((32, waves), f32),
+        grid=(4,),
+        in_specs=[pl.BlockSpec((8, block), lambda i: (0, i)), pl.BlockSpec((PACKED, 128), lambda i: (0, 0))],
+        out_specs=(
+            pl.BlockSpec((32, block), lambda i: (0, 0)),
+            pl.BlockSpec((32, block), lambda i: (0, 0)),
+            pl.BlockSpec((1, 32, block), lambda i: (i // 2, 0, 0)),
+        ),
+        out_shape=(one, one, jax.ShapeDtypeStruct((2, 32, block), f32)),
+        scratch_shapes=[pltpu.VMEM((CLASSES, 128), f32), pltpu.VMEM((256, CLASSES), bf16)],
         compiler_params=pltpu.CompilerParams(vmem_limit_bytes=VMEM_LIMIT),
-        cost_estimate=pl.CostEstimate(flops=2 * CLASSES * 256 * waves, bytes_accessed=waves * 160, transcendentals=0),
+        cost_estimate=pl.CostEstimate(flops=2 * CLASSES * 1024 * block, bytes_accessed=block * 640, transcendentals=0),
         name="filter_rows",
-    )(miller_rows, pair_products)
-
-
-def gradient_kernel(pick_ref, pos_ref, feat_ref, cot_ref, uv_ref, down_ref, grad_ref, posg_ref, slots_ref):
-    trig = multiples(pos_ref[...])
-    (c0, s0), (c1, s1), (c2, s2) = trig
-    fill_slots(slots_ref, trig[0], row_tables(pick_ref, feat_ref[...], cot_ref[...]))
-    pairs = pair_table(trig[1], trig[2]).astype(bf16)
+    )(miller_rows, total)
+
+
+def feature_kernel(pos_ref, total_ref, class_ref, grad_ref, uv_ref, down_ref):
+    @pl.when(pl.program_id(0) == 0)
+    def _():
+        combine(total_ref, class_ref, uv_ref, down_ref)
+
+    (c0, s0), trig1, trig2 = multiples(pos_ref[...])
+    pairs = pair_table(trig1, trig2).astype(bf16)
     parts = jnp.dot(down_ref[...], pairs, preferred_element_type=f32)
     grad = parts[512:544]
     for t in range(8):
         grad = grad + c0[t : t + 1, :] * parts[64 * t : 64 * t + 32] + s0[t : t + 1, :] * parts[64 * t + 32 : 64 * t + 64]
     grad_ref[...] = grad
-    both = jnp.dot(uv_ref[:, 0:SLOTS], slots_ref[...], preferred_element_type=f32)
-    u = both[0:PAIR_ROWS]
-    v = both[PAIR_ROWS:]
+
+
+def feature_rows(positions, total, classes, block):
+    atoms = positions.shape[1]
+    return pl.pallas_call(
+        feature_kernel,
+        grid=(atoms // block,),
+        in_specs=[
+            pl.BlockSpec((3, block), lambda i: (0, i)),
+            pl.BlockSpec((PACKED, 128), lambda i: (0, 0)),
+            pl.BlockSpec((4, CLASSES, 128), lambda i: (0, 0, 0)),
+        ],
+        out_specs=(
+            pl.BlockSpec((32, block), lambda i: (0, i)),
+            pl.BlockSpec((2 * PAIR_ROWS, 128 * TILES), lambda i: (0, 0)),
+        ),
+        out_shape=(
+            jax.ShapeDtypeStruct((32, atoms), f32),
+            jax.ShapeDtypeStruct((2 * PAIR_ROWS, 128 * TILES), bf16),
+        ),
+        scratch_shapes=[pltpu.VMEM((64 * TILES, PAIR_ROWS), bf16)],
+        compiler_params=pltpu.CompilerParams(vmem_limit_bytes=VMEM_LIMIT),
+        cost_estimate=pl.CostEstimate(flops=2 * PAIR_ROWS * SLOTS * atoms, bytes_accessed=atoms * 700, transcendentals=0),
+        name="feature_rows",
+    )(positions, total, classes)
+
+
+def position_kernel(pick_ref, pos_ref, feat_ref, cot_ref, uv_ref, posg_ref, *slots_refs):
+    size = slots_refs[0].shape[1]
+    for k, slots_ref in enumerate(slots_refs):
+        at = slice(k * size, (k + 1) * size)
+        trig = multiples(pos_ref[:, at])
+        fill_slots(slots_ref, trig[0], row_tables(pick_ref, feat_ref[at, :], cot_ref[at, :]))
+        both = jnp.dot(uv_ref[:, 0:SLOTS], slots_ref[...], preferred_element_type=f32)
+        posg_ref[:, at] = position_sums(trig, both[0:PAIR_ROWS], both[PAIR_ROWS:])
+
+
+def position_sums(trig, u, v):
+    _, (c1, s1), (c2, s2) = trig
     orders = lax.broadcasted_iota(jnp.int32, c1.shape, 0).astype(f32) + 1.0
     acc0 = c2 * v[256:264] + s2 * v[264:272] + c1 * v[272:280] + s1 * v[280:288]
     acc1 = orders * (c1 * u[280:288] - s1 * u[272:280])
@@ -302,13 +376,13 @@
         acc2 = acc2 + lead_c * (c2 * ucs - s2 * ucc) + lead_s * (c2 * uss - s2 * usc)
     acc2 = acc2 * orders
     rows = [jnp.sum(acc0, 0, keepdims=True) + v[288:289], jnp.sum(acc1, 0, keepdims=True), jnp.sum(acc2, 0, keepdims=True)]
-    posg_ref[...] = phase_step * jnp.concatenate(rows, 0)
-
-
-def gradients(pick, positions, features, cotangent, uv, down, block):
+    return phase_step * jnp.concatenate(rows, 0)
+
+
+def position_rows(pick, positions, features, cotangent, uv, block, cuts):
     atoms = positions.shape[1]
     return pl.pallas_call(
-        gradient_kernel,
+        position_kernel,
         grid=(atoms // block,),
         in_specs=[
             pl.BlockSpec(memory_space=pltpu.SMEM),
@@ -316,15 +390,14 @@
             pl.BlockSpec((block, 128), lambda i: (i, 0)),
             pl.BlockSpec((block, 128), lambda i: (i, 0)),
             pl.BlockSpec((2 * PAIR_ROWS, 128 * TILES), lambda i: (0, 0)),
-            pl.BlockSpec((64 * TILES, PAIR_ROWS), lambda i: (0, 0)),
         ],
-        out_specs=(pl.BlockSpec((32, block), lambda i: (0, i)), pl.BlockSpec((3, block), lambda i: (0, i))),
-        out_shape=(jax.ShapeDtypeStruct((32, atoms), f32), jax.ShapeDtypeStruct((3, atoms), f32)),
-        scratch_shapes=[pltpu.VMEM((SLOTS, block), bf16)],
+        out_specs=pl.BlockSpec((3, block), lambda i: (0, i)),
+        out_shape=jax.ShapeDtypeStruct((3, atoms), f32),
+        scratch_shapes=[pltpu.VMEM((SLOTS, block // cuts), bf16)] * cuts,
         compiler_params=pltpu.CompilerParams(vmem_limit_bytes=VMEM_LIMIT),
-        cost_estimate=pl.CostEstimate(flops=6 * PAIR_ROWS * SLOTS * atoms, bytes_accessed=atoms * 700, transcendentals=0),
-        name="gradients",
-    )(pick, positions, features, cotangent, uv, down)
+        cost_estimate=pl.CostEstimate(flops=4 * PAIR_ROWS * SLOTS * atoms, bytes_accessed=atoms * 700, transcendentals=0),
+        name="position_rows",
+    )(pick, positions, features, cotangent, uv)
 
 
 def swap(value, axis):
@@ -353,6 +426,7 @@
 
 def shards(block, positions, features, cotangent, miller, radial_filter):
     atoms = positions.shape[1]
+    block = min(block, atoms)
     waves = miller.shape[1]
     y_at, core_at = lax.axis_index("yl"), lax.axis_index("core")
     atom_count = atoms * lax.axis_size(("z", "yh", "x"))
@@ -373,28 +447,25 @@
     beside = swap(jnp.concatenate([send, pair_indices], 0), "core")
     radial_rows = jnp.concatenate([keep, beside[:32]], 1)
     miller_rows = jnp.concatenate([pair_indices, beside[32:]], 1)
-    wave_block = min(1024, 4 * waves)
-    classes = class_sums(miller_rows, radial_rows, wave_block)
-
-    part = factors(pick, positions, features, cotangent, block)
-    part = sum_scatter(part, "x")
+    classes = class_sums(miller_rows, radial_rows, scale, min(1024, 4 * waves))
+
+    part = factors(pick, positions, features, cotangent, block, 1)
+    part = sum_scatter(part, ("x", "yh"))
     part = sum_scatter(part, "z")
-    part = part + swap(part, "yh")
     part = gather(part, "z")
-    total = gather(part, "x")
-    uv, down, pair_products = combine(total, classes, scale)
-    grad, posg = gradients(pick, positions, features, cotangent, uv, down, block)
-    across = swap(grad, "yl")
-    near = swap(jnp.concatenate([grad, across], 0), "core")
-    feature_grad = order_channels(grad, across, near[:32], near[32:], y_at, core_at)
-    posg = posg + swap(posg, "core")
-    position_grad = posg + swap(posg, "yl")
-
-    rows = filter_rows(miller_rows, pair_products, scale, wave_block).reshape(32, 4, waves)
-    came = swap(rows[:, 1::2].reshape(32, 2 * waves), "yl").reshape(32, 2, waves)
-    both = jnp.concatenate([rows[:, 0::2], came], 0)
-    near = swap(both[:, 1], "core")
-    filter_grad = order_channels(both[:32, 0], both[32:, 0], near[:32], near[32:], y_at, core_at)
+    total = gather(part, ("x", "yh"))
+    grad, uv = feature_rows(positions, total, classes, atoms)
+    grad_y, grad_core = swap(grad, "yl"), swap(grad, "core")
+    total = lax.optimization_barrier((total, grad))[0]
+    own, beside, send = filter_rows(miller_rows, total, scale)
+    came, beside = swap(send, "yl"), swap(beside, "core")
+    uv = lax.optimization_barrier((uv, own))[0]
+    posg = position_rows(pick, positions, features, cotangent, uv, block, 1)
+    grad_y, came, posg = lax.optimization_barrier((grad_y, came, posg))
+    both = lax.ppermute(posg, ("yl", "core"), [(i, 3 - i) for i in range(4)])
+    position_grad = (posg + swap(posg, "core")) + (swap(posg, "yl") + both)
+    feature_grad = order_channels(grad, grad_y, grad_core, swap(grad_y, "core"), y_at, core_at)
+    filter_grad = order_channels(own, came[0], beside, swap(came, "core")[1], y_at, core_at)
     return feature_grad, position_grad, filter_grad
 
 
@@ -405,7 +476,7 @@
     atom, wave = ("z", "yh", "x"), ("yl", "core")
     placed = (P(None, atom), P(atom, None), P(atom, None), P(None, wave), P(wave, None))
     return jax.shard_map(
-        functools.partial(shards, 512),
+        functools.partial(shards, 2048),
         mesh=fine,
         in_specs=placed,
         out_specs=(P(atom, None), P(None, atom), P(wave, None)),

time: 140 us -> 129 us (0.921)
  starting transfers between devices: 45.5 us -> 37 us
  local copies, waits for them, and re-layouts: 8.93 us -> 6.17 us
  waiting for transfers between devices: 37.9 us -> 40.2 us
  Pallas kernels: 41.6 us -> 39.5 us
    ppermute x9 -> x10, starting transfers between devices: 24.4 us -> 8.7 us  [swap(): return lax.ppermute(value, axis, [(0, 1), (1, 0)])]
    ppermute x0 -> x1, starting transfers between devices: none -> 5.51 us  [shards(): both = lax.ppermute(posg, ('yl', 'core'), [(i, 3 - i) for i in range(4)])]
    ppermute x9 -> x10, waiting for transfers between devices: 3.96 us -> 0.87 us  [swap(): return lax.ppermute(value, axis, [(0, 1), (1, 0)])]
    all_to_all x2, waiting for transfers between devices: 9.05 us -> 12.1 us  [gather(): return lax.all_to_all(copies, axis, 0, 0).reshape(n * value.shape[0], 128)]
    pallas_call x1, Pallas kernels: 9.85 us -> 7.55 us  [factors(): pl.pallas_call(factor_kernel, grid=(atoms // block,), in_specs=[pl.BlockS...]
    all_to_all x2, waiting for transfers between devices: 24.9 us -> 26.7 us  [sum_scatter(): lax.all_to_all(value.reshape(n, value.shape[0] // n, 128), axis, 0, 0)]
    all_to_all x2, starting transfers between devices: 14.1 us -> 15.8 us  [sum_scatter(): lax.all_to_all(value.reshape(n, value.shape[0] // n, 128), axis, 0, 0)]
    reshape x2 -> x0, local copies, waits for them, and re-layouts: 1.47 us -> none  [the longest x1 1.45 us: shards(): filter_rows(miller_rows, pair_products, scale, wave_block)]
  transfers between devices with their start and end apart: 13 -> 15, of which waited for: 8 -> 6; matrix products, arithmetic and copies ran while one was open for 5% -> 5% of each run, Pallas kernels for 7% -> 20%
where the time goes in v2:
time: 129 us; the launch traced here: 128 us
  waiting for transfers between devices  40.2 us (31%)
  Pallas kernels  39.5 us (31%)
  starting transfers between devices  37 us (29%)
  local copies, waits for them, and re-layouts  6.17 us (5%)
  other arithmetic  4.34 us (3%)
    all_to_all x2, waiting for transfers between devices, sum_scatter(): lax.all_to_all(value.reshape(n, value.shape[0] // n, 128), axis, 0, 0)  26.7 us
    all_to_all x2, starting transfers between devices, sum_scatter(): lax.all_to_all(value.reshape(n, value.shape[0] // n, 128), axis, 0, 0)  15.8 us
    all_to_all x2, waiting for transfers between devices, gather(): return lax.all_to_all(copies, axis, 0, 0).reshape(n * value.shape[0], 128)  12.1 us
    pallas_call x1, Pallas kernels, position_rows(): pl.pallas_call(position_kernel, grid=(atoms // block,), in_specs=[pl.Bloc...  11 us
    ppermute x10, starting transfers between devices, swap(): return lax.ppermute(value, axis, [(0, 1), (1, 0)])  8.7 us
    pallas_call x1, Pallas kernels, filter_rows(): pl.pallas_call(functools.partial(filter_kernel, scale), grid=(4,), in_spe...  7.89 us
    pallas_call x1, Pallas kernels, factors(): pl.pallas_call(factor_kernel, grid=(atoms // block,), in_specs=[pl.BlockS...  7.55 us
    all_to_all x2, starting transfers between devices, gather(): return lax.all_to_all(copies, axis, 0, 0).reshape(n * value.shape[0], 128)  6.95 us
  transfers between devices with their start and end apart: 15, of which 6 were waited for; matrix products, arithmetic and copies ran while one was open for 5% of the time, Pallas kernels for 20%

profile of v2, /device:TPU:1, one launch (start us, length us, event | category | flops | bytes accessed | tf_op | source)
XLA Modules:
  0.0 128.1 jit_solution(14366127681466604818)
XLA Ops:
  0.6 7.6 %factors.1 = f32[2560,128]{1,0:T(8,128)} custom-call(s32[1]{0:T(128)} %bitcast.pick_ref, f32[3,4096]{1,0:T(4,128)} %pos_ref.5, bf16[4096,128]{1,0:T(8,128)(2,1)} %feat_ref.3, bf16[4096,128]{1,0:T(8,128)(2,1)} %cot_ref.3), custom_call_target="tpu_custom_call" | custom-call | flops 2709520384 | bytes 2129920 | tf_op jit(solution)/shard_map/factors/pallas_call | solution.py:104
  8.2 7.6 %all-to-all-start = ((f32[8,320,128]{2,1,0:T(8,128)}), f32[8,320,128]{2,1,0:T(8,128)S(1)}, u32[]{:S(2)}, u32[]{:S(2)}) async-start(f32[8,320,128]{2,1,0:T(8,128)} %bitcast.35), calls=%async_computation | async-start | bytes 2621440 | tf_op jit(solution)/shard_map/all_to_all | solution.py:409
  16.6 18.4 %all-to-all-done = f32[8,320,128]{2,1,0:T(8,128)S(1)} async-done(((f32[8,320,128]{2,1,0:T(8,128)}), f32[8,320,128]{2,1,0:T(8,128)S(1)}, u32[]{:S(2)}, u32[]{:S(2)}) %all-to-all-start) | async-done | bytes 1310752 | tf_op jit(solution)/shard_map/all_to_all | solution.py:409
  35.8 8.2 %all-to-all-start.1 = ((f32[8,40,128]{2,1,0:T(8,128)}), f32[8,40,128]{2,1,0:T(8,128)S(1)}, u32[]{:S(2)}, u32[]{:S(2)}) async-start(f32[8,40,128]{2,1,0:T(8,128)} %bitcast.2), calls=%async_computation.1 | async-start | bytes 327680 | tf_op jit(solution)/shard_map/all_to_all | solution.py:409
  44.1 8.2 %all-to-all-done.1 = f32[8,40,128]{2,1,0:T(8,128)S(1)} async-done(((f32[8,40,128]{2,1,0:T(8,128)}), f32[8,40,128]{2,1,0:T(8,128)S(1)}, u32[]{:S(2)}, u32[]{:S(2)}) %all-to-all-start.1) | async-done | bytes 163872 | tf_op jit(solution)/shard_map/all_to_all | solution.py:409
  53.0 3.4 %all-to-all-start.2 = ((f32[8,40,128]{2,1,0:T(8,128)}), f32[8,40,128]{2,1,0:T(8,128)S(1)}, u32[]{:S(2)}, u32[]{:S(2)}) async-start(f32[8,40,128]{2,1,0:T(8,128)} %broadcast_in_dim.16), calls=%async_computation.2 | async-start | bytes 327680 | tf_op jit(solution)/shard_map/all_to_all | solution.py:416
  56.4 3.1 %collective-permute-start.1 = (f32[40,2048]{1,0:T(8,128)S(1)}, f32[40,2048]{1,0:T(8,128)S(1)}, u32[]{:S(2)}, u32[]{:S(2)}) collective-permute-start(f32[40,2048]{1,0:T(8,128)S(1)} %pad_maximum_fusion.1), channel_id=1, source_target_pairs={{0,1},{1,0},{2,3},{3,2},{4,5},{5,4},{6,7},{7,6},{8,9},{9,8},{10,11... | collective-permute-start | bytes 983048 | tf_op jit(solution)/shard_map/ppermute | solution.py:404
  59.5 5.0 %all-to-all-done.2 = f32[8,40,128]{2,1,0:T(8,128)S(1)} async-done(((f32[8,40,128]{2,1,0:T(8,128)}), f32[8,40,128]{2,1,0:T(8,128)S(1)}, u32[]{:S(2)}, u32[]{:S(2)}) %all-to-all-start.2) | async-done | bytes 163872 | tf_op jit(solution)/shard_map/all_to_all | solution.py:416
  64.6 1.2 broadcast_in_dim.18
  65.7 3.6 %all-to-all-start.3 = ((f32[8,320,128]{2,1,0:T(8,128)}), f32[8,320,128]{2,1,0:T(8,128)S(1)}, u32[]{:S(2)}, u32[]{:S(2)}) async-start(f32[8,320,128]{2,1,0:T(8,128)} %broadcast_in_dim.18), calls=%async_computation.3 | async-start | bytes 2621440 | tf_op jit(solution)/shard_map/all_to_all | solution.py:416
  70.8 6.8 %class_sums.1.class_ref = f32[4,896,128]{2,1,0:T(8,128)} custom-call(f32[8,4096]{1,0:T(8,128)} %pad_maximum_fusion.7.miller_ref, f32[32,4096]{1,0:T(8,128)} %pad_maximum_fusion.radial_ref), custom_call_target="tpu_custom_call" | custom-call | flops 1879048192 | bytes 655360 | tf_op jit(solution)/shard_map/class_sums/pallas_call | solution.py:169
  77.6 7.1 %all-to-all-done.3 = f32[8,320,128]{2,1,0:T(8,128)S(1)} async-done(((f32[8,320,128]{2,1,0:T(8,128)}), f32[8,320,128]{2,1,0:T(8,128)S(1)}, u32[]{:S(2)}, u32[]{:S(2)}) %all-to-all-start.3) | async-done | bytes 1310752 | tf_op jit(solution)/shard_map/all_to_all | solution.py:416
  84.7 1.1 copy-done
  85.8 6.4 %feature_rows.1 = (f32[32,4096]{1,0:T(8,128)}, bf16[608,1152]{1,0:T(8,128)(2,1)}) custom-call(f32[3,4096]{1,0:T(4,128)} %pos_ref.5, f32[2560,128]{1,0:T(8,128)} %bitcast.33, f32[4,896,128]{2,1,0:T(8,128)} %class_sums.1.class_ref), custom_call_target="tpu_custom_call" | custom-call | flops 2709520384 | bytes 2867200 | tf_op jit(solution)/shard_map/feature_rows/pallas_call | solution.py:331
  92.3 7.9 %filter_rows.1 = (f32[32,1024]{1,0:T(8,128)}, f32[32,1024]{1,0:T(8,128)}, f32[2,32,1024]{2,1,0:T(8,128)}) custom-call(f32[8,4096]{1,0:T(8,128)} %pad_maximum_fusion.7.miller_ref, f32[2560,128]{1,0:T(8,128)} %bitcast.34), custom_call_target="tpu_custom_call" | custom-call | flops 1879048192 | bytes 655360 | tf_op jit(solution)/shard_map/filter_rows/pallas_call | solution.py:298
  100.2 1.4 %collective-permute-start.3 = (f32[2,32,1024]{2,1,0:T(8,128)}, f32[2,32,1024]{2,1,0:T(8,128)S(1)}, u32[]{:S(2)}, u32[]{:S(2)}) collective-permute-start(f32[2,32,1024]{2,1,0:T(8,128)} %get-tuple-element.15), channel_id=1, source_target_pairs={{0,2},{2,0},{1,3},{3,1},{4,6},{6,4},{5,7},{7,5},{8,10},{10,8},{9,1... | collective-permute-start | bytes 786440 | tf_op jit(solution)/shard_map/ppermute | solution.py:404
  101.6 11.0 %position_rows.1 = f32[3,4096]{1,0:T(4,128)} custom-call(s32[1]{0:T(128)} %bitcast.pick_ref, f32[3,4096]{1,0:T(4,128)} %pos_ref.5, bf16[4096,128]{1,0:T(8,128)(2,1)} %feat_ref.3, bf16[4096,128]{1,0:T(8,128)(2,1)} %cot_ref.3, bf16[608,1152]{1,0:T(8,128)(2,1)} %get-tuple-element.18.uv_ref), custom_call_target="tpu_custom_call" | custom-call | flops 5419040768 | bytes 2867200 | tf_op jit(solution)/shard_map/position_rows/pallas_call | solution.py:384
  112.6 5.5 %collective-permute-start.8 = (f32[3,4096]{1,0:T(4,128)}, f32[3,4096]{1,0:T(4,128)S(1)}, u32[]{:S(2)}, u32[]{:S(2)}) collective-permute-start(f32[3,4096]{1,0:T(4,128)} %position_rows.1), channel_id=1, source_target_pairs={{0,3},{1,2},{2,1},{3,0},{4,7},{5,6},{6,5},{7,4},{8,11},{9,10},{10,... | collective-permute-start | bytes 147464 | tf_op jit(solution)/shard_map/ppermute | solution.py:465
  118.1 1.1 collective-permute-start.7
  120.3 1.5 %collective-permute-start.10 = (f32[2,32,1024]{2,1,0:T(8,128)S(1)}, f32[2,32,1024]{2,1,0:T(8,128)S(1)}, u32[]{:S(2)}, u32[]{:S(2)}) collective-permute-start(f32[2,32,1024]{2,1,0:T(8,128)S(1)} %collective-permute-done.3), channel_id=1, source_target_pairs={{0,1},{1,0},{2,3},{3,2},{4,5},{5,4},{6,7},{7,6},{8,9},{9,8},{10,11... | collective-permute-start | bytes 786440 | tf_op jit(solution)/shard_map/ppermute | solution.py:404
  121.8 0.8 collective-permute-done.7
  123.0 1.5 %add_add_fusion = f32[3,4096]{1,0:T(4,128)} fusion(f32[3,4096]{1,0:T(4,128)S(1)} %collective-permute-done.7, f32[3,4096]{1,0:T(4,128)S(1)} %collective-permute-done.8, f32[3,4096]{1,0:T(4,128)} %position_rows.1, f32[3,4096]{1,0:T(4,128)S(1)} %collective-permute-done.6), kind=kLoop, calls=%fused_computation.31 | loop fusion | flops 36864 | bytes 245760 | tf_op jit(solution)/shard_map/add | solution.py:466
  124.7 1.0 copy.13
  126.3 1.8 %copy.12 = f32[4096,128]{1,0:T(8,128)} copy(f32[4096,128]{0,1:T(8,128)S(1)} %maximum_bitcast_fusion) | data formatting | bytes 4194304
  (50 shorter events, 6.1 us)
Async XLA Ops:
  8.2 7.6 %copy-start.4 = (s32[3,1024]{1,0:T(4,128)S(1)}, s32[3,1024]{1,0:T(4,128)}, u32[]{:S(2)}) copy-start(s32[3,1024]{1,0:T(4,128)} %param.8) | copy-start | bytes 36868
  8.2 7.6 %copy-start.2 = (f32[1024,128]{1,0:T(8,128)S(1)}, f32[1024,128]{1,0:T(8,128)}, u32[]{:S(2)}) copy-start(f32[1024,128]{1,0:T(8,128)} %param.9) | copy-start | bytes 1572868
  8.2 26.9 %all-to-all-start = ((f32[8,320,128]{2,1,0:T(8,128)}), f32[8,320,128]{2,1,0:T(8,128)S(1)}, u32[]{:S(2)}, u32[]{:S(2)}) async-start(f32[8,320,128]{2,1,0:T(8,128)} %bitcast.35), calls=%async_computation | async-start | bytes 2621440 | tf_op jit(solution)/shard_map/all_to_all | solution.py:409
  16.1 27.9 %collective-permute-start = (f32[72,1024]{1,0:T(8,128)S(1)}, f32[72,1024]{1,0:T(8,128)S(1)}, u32[]{:S(2)}, u32[]{:S(2)}) collective-permute-start(f32[72,1024]{1,0:T(8,128)S(1)} %pad_maximum_fusion.2), channel_id=1, source_target_pairs={{0,2},{2,0},{1,3},{3,1},{4,6},{6,4},{5,7},{7,5},{8,10},{10,8},{9,1... | collective-permute-start | bytes 884744 | tf_op jit(solution)/shard_map/ppermute | solution.py:404
  35.8 16.5 %all-to-all-start.1 = ((f32[8,40,128]{2,1,0:T(8,128)}), f32[8,40,128]{2,1,0:T(8,128)S(1)}, u32[]{:S(2)}, u32[]{:S(2)}) async-start(f32[8,40,128]{2,1,0:T(8,128)} %bitcast.2), calls=%async_computation.1 | async-start | bytes 327680 | tf_op jit(solution)/shard_map/all_to_all | solution.py:409
  53.0 11.6 %all-to-all-start.2 = ((f32[8,40,128]{2,1,0:T(8,128)}), f32[8,40,128]{2,1,0:T(8,128)S(1)}, u32[]{:S(2)}, u32[]{:S(2)}) async-start(f32[8,40,128]{2,1,0:T(8,128)} %broadcast_in_dim.16), calls=%async_computation.2 | async-start | bytes 327680 | tf_op jit(solution)/shard_map/all_to_all | solution.py:416
  56.4 12.9 %collective-permute-start.1 = (f32[40,2048]{1,0:T(8,128)S(1)}, f32[40,2048]{1,0:T(8,128)S(1)}, u32[]{:S(2)}, u32[]{:S(2)}) collective-permute-start(f32[40,2048]{1,0:T(8,128)S(1)} %pad_maximum_fusion.1), channel_id=1, source_target_pairs={{0,1},{1,0},{2,3},{3,2},{4,5},{5,4},{6,7},{7,6},{8,9},{9,8},{10,11... | collective-permute-start | bytes 983048 | tf_op jit(solution)/shard_map/ppermute | solution.py:404
  65.7 19.0 %all-to-all-start.3 = ((f32[8,320,128]{2,1,0:T(8,128)}), f32[8,320,128]{2,1,0:T(8,128)S(1)}, u32[]{:S(2)}, u32[]{:S(2)}) async-start(f32[8,320,128]{2,1,0:T(8,128)} %broadcast_in_dim.18), calls=%async_computation.3 | async-start | bytes 2621440 | tf_op jit(solution)/shard_map/all_to_all | solution.py:416
  84.7 1.1 copy-start
  92.1 20.4 %collective-permute-start.2 = (f32[32,4096]{1,0:T(8,128)}, f32[32,4096]{1,0:T(8,128)S(1)}, u32[]{:S(2)}, u32[]{:S(2)}) collective-permute-start(f32[32,4096]{1,0:T(8,128)} %get-tuple-element.13), channel_id=1, source_target_pairs={{0,2},{2,0},{1,3},{3,1},{4,6},{6,4},{5,7},{7,5},{8,10},{10,8},{9,1... | collective-permute-start | bytes 1572872 | tf_op jit(solution)/shard_map/ppermute | solution.py:404
  100.2 19.0 %copy-start.1 = (f32[32,4096]{1,0:T(8,128)S(1)}, f32[32,4096]{1,0:T(8,128)}, u32[]{:S(2)}) copy-start(f32[32,4096]{1,0:T(8,128)} %get-tuple-element.13) | copy-start | bytes 1572868
  100.2 19.5 %copy-start.5 = (f32[32,1024]{1,0:T(8,128)S(1)}, f32[32,1024]{1,0:T(8,128)}, u32[]{:S(2)}) copy-start(f32[32,1024]{1,0:T(8,128)} %get-tuple-element.22) | copy-start | bytes 393220
  100.2 24.4 %copy-start.3 = (f32[32,1024]{1,0:T(8,128)S(1)}, f32[32,1024]{1,0:T(8,128)}, u32[]{:S(2)}) copy-start(f32[32,1024]{1,0:T(8,128)} %get-tuple-element.17) | copy-start | bytes 393220
  100.2 12.4 %collective-permute-start.3 = (f32[2,32,1024]{2,1,0:T(8,128)}, f32[2,32,1024]{2,1,0:T(8,128)S(1)}, u32[]{:S(2)}, u32[]{:S(2)}) collective-permute-start(f32[2,32,1024]{2,1,0:T(8,128)} %get-tuple-element.15), channel_id=1, source_target_pairs={{0,2},{2,0},{1,3},{3,1},{4,6},{6,4},{5,7},{7,5},{8,10},{10,8},{9,1... | collective-permute-start | bytes 786440 | tf_op jit(solution)/shard_map/ppermute | solution.py:404
  112.6 7.7 %collective-permute-start.8 = (f32[3,4096]{1,0:T(4,128)}, f32[3,4096]{1,0:T(4,128)S(1)}, u32[]{:S(2)}, u32[]{:S(2)}) collective-permute-start(f32[3,4096]{1,0:T(4,128)} %position_rows.1), channel_id=1, source_target_pairs={{0,3},{1,2},{2,1},{3,0},{4,7},{5,6},{6,5},{7,4},{8,11},{9,10},{10,... | collective-permute-start | bytes 147464 | tf_op jit(solution)/shard_map/ppermute | solution.py:465
  118.1 4.6 %collective-permute-start.7 = (f32[3,4096]{1,0:T(4,128)}, f32[3,4096]{1,0:T(4,128)S(1)}, u32[]{:S(2)}, u32[]{:S(2)}) collective-permute-start(f32[3,4096]{1,0:T(4,128)} %position_rows.1), channel_id=1, source_target_pairs={{0,2},{2,0},{1,3},{3,1},{4,6},{6,4},{5,7},{7,5},{8,10},{10,8},{9,1... | collective-permute-start | bytes 147464 | tf_op jit(solution)/shard_map/ppermute | solution.py:404
  119.2 3.9 %collective-permute-start.6 = (f32[3,4096]{1,0:T(4,128)}, f32[3,4096]{1,0:T(4,128)S(1)}, u32[]{:S(2)}, u32[]{:S(2)}) collective-permute-start(f32[3,4096]{1,0:T(4,128)} %position_rows.1), channel_id=1, source_target_pairs={{0,1},{1,0},{2,3},{3,2},{4,5},{5,4},{6,7},{7,6},{8,9},{9,8},{10,11... | collective-permute-start | bytes 147464 | tf_op jit(solution)/shard_map/ppermute | solution.py:404
  119.2 6.6 %collective-permute-start.4 = (f32[32,4096]{1,0:T(8,128)S(1)}, f32[32,4096]{1,0:T(8,128)S(1)}, u32[]{:S(2)}, u32[]{:S(2)}) collective-permute-start(f32[32,4096]{1,0:T(8,128)S(1)} %copy-done.1), channel_id=1, source_target_pairs={{0,1},{1,0},{2,3},{3,2},{4,5},{5,4},{6,7},{7,6},{8,9},{9,8},{10,11... | collective-permute-start | bytes 1572872 | tf_op jit(solution)/shard_map/ppermute | solution.py:404
  119.7 4.9 %collective-permute-start.9 = (f32[32,1024]{1,0:T(8,128)S(1)}, f32[32,1024]{1,0:T(8,128)S(1)}, u32[]{:S(2)}, u32[]{:S(2)}) collective-permute-start(f32[32,1024]{1,0:T(8,128)S(1)} %copy-done.5), channel_id=1, source_target_pairs={{0,1},{1,0},{2,3},{3,2},{4,5},{5,4},{6,7},{7,6},{8,9},{9,8},{10,11... | collective-permute-start | bytes 393224 | tf_op jit(solution)/shard_map/ppermute | solution.py:404
  120.3 4.2 %collective-permute-start.10 = (f32[2,32,1024]{2,1,0:T(8,128)S(1)}, f32[2,32,1024]{2,1,0:T(8,128)S(1)}, u32[]{:S(2)}, u32[]{:S(2)}) collective-permute-start(f32[2,32,1024]{2,1,0:T(8,128)S(1)} %collective-permute-done.3), channel_id=1, source_target_pairs={{0,1},{1,0},{2,3},{3,2},{4,5},{5,4},{6,7},{7,6},{8,9},{9,8},{10,11... | collective-permute-start | bytes 786440 | tf_op jit(solution)/shard_map/ppermute | solution.py:404
  122.6 3.1 %collective-permute-start.5 = (f32[32,4096]{1,0:T(8,128)S(1)}, f32[32,4096]{1,0:T(8,128)S(1)}, u32[]{:S(2)}, u32[]{:S(2)}) collective-permute-start(f32[32,4096]{1,0:T(8,128)S(1)} %collective-permute-done.2), channel_id=1, source_target_pairs={{0,1},{1,0},{2,3},{3,2},{4,5},{5,4},{6,7},{7,6},{8,9},{9,8},{10,11... | collective-permute-start | bytes 1572872 | tf_op jit(solution)/shard_map/ppermute | solution.py:404

commit v3 on v2

--- a/solution.py
+++ b/solution.py
@@ -17,7 +17,7 @@
 PACKED = 2560
 f32 = jnp.float32
 bf16 = jnp.bfloat16
-VMEM_LIMIT = 56 * 1024 * 1024
+MIB = 1024 * 1024
 
 
 def nt_dot(a, b):
@@ -113,7 +113,7 @@
         out_specs=pl.BlockSpec((PACKED, 128), lambda i: (0, 0)),
         out_shape=jax.ShapeDtypeStruct((PACKED, 128), f32),
         scratch_shapes=[pltpu.VMEM((PAIR_ROWS, SLOTS), f32)] + [pltpu.VMEM((SLOTS, block // cuts), bf16)] * cuts,
-        compiler_params=pltpu.CompilerParams(vmem_limit_bytes=VMEM_LIMIT),
+        compiler_params=pltpu.CompilerParams(vmem_limit_bytes=56 * MIB),
         cost_estimate=pl.CostEstimate(flops=2 * PAIR_ROWS * SLOTS * atoms, bytes_accessed=atoms * 520, transcendentals=0),
         name="factors",
     )(pick, positions, features, cotangent)
@@ -173,7 +173,7 @@
         out_specs=pl.BlockSpec((4, CLASSES, 128), lambda i: (0, 0, 0)),
         out_shape=jax.ShapeDtypeStruct((4, CLASSES, 128), f32),
         scratch_shapes=[pltpu.VMEM((CLASSES, 128), f32)],
-        compiler_params=pltpu.CompilerParams(vmem_limit_bytes=VMEM_LIMIT),
+        compiler_params=pltpu.CompilerParams(vmem_limit_bytes=18 * MIB),
         cost_estimate=pl.CostEstimate(flops=2 * CLASSES * 256 * waves, bytes_accessed=waves * 160, transcendentals=0),
         name="class_sums",
     )(miller_rows, radial_rows)
@@ -260,7 +260,8 @@
         pair_ref[88 * t : 88 * t + 88, :] = jnp.concatenate(parts, 1)
 
 
-def filter_kernel(scale, miller_ref, total_ref, own_ref, beside_ref, send_ref, pair_ref, turned_ref):
+def filter_kernel(scale, miller_ref, total_ref, *refs):
+    *out_refs, pair_ref, turned_ref = refs
     step = pl.program_id(0)
 
     @pl.when(step == 0)
@@ -279,17 +280,11 @@
         rows = rows + products[q] * values[32 * (q + 1) : 32 * (q + 2)]
     rows = scale * rows
 
-    @pl.when(step == 0)
-    def _():
-        own_ref[...] = rows
-
-    @pl.when(step == 2)
-    def _():
-        beside_ref[...] = rows
-
-    @pl.when(lax.rem(step, 2) == 1)
-    def _():
-        send_ref[0] = rows
+    for k, out_ref in enumerate(out_refs):
+
+        @pl.when(step == k)
+        def _():
+            out_ref[...] = rows
 
 
 def filter_rows(miller_rows, total, scale):
@@ -299,14 +294,10 @@
         functools.partial(filter_kernel, scale),
         grid=(4,),
         in_specs=[pl.BlockSpec((8, block), lambda i: (0, i)), pl.BlockSpec((PACKED, 128), lambda i: (0, 0))],
-        out_specs=(
-            pl.BlockSpec((32, block), lambda i: (0, 0)),
-            pl.BlockSpec((32, block), lambda i: (0, 0)),
-            pl.BlockSpec((1, 32, block), lambda i: (i // 2, 0, 0)),
-        ),
-        out_shape=(one, one, jax.ShapeDtypeStruct((2, 32, block), f32)),
+        out_specs=(pl.BlockSpec((32, block), lambda i: (0, 0)),) * 4,
+        out_shape=(one,) * 4,
         scratch_shapes=[pltpu.VMEM((CLASSES, 128), f32), pltpu.VMEM((256, CLASSES), bf16)],
-        compiler_params=pltpu.CompilerParams(vmem_limit_bytes=VMEM_LIMIT),
+        compiler_params=pltpu.CompilerParams(vmem_limit_bytes=18 * MIB),
         cost_estimate=pl.CostEstimate(flops=2 * CLASSES * 1024 * block, bytes_accessed=block * 640, transcendentals=0),
         name="filter_rows",
     )(miller_rows, total)
@@ -345,20 +336,54 @@
             jax.ShapeDtypeStruct((2 * PAIR_ROWS, 128 * TILES), bf16),
         ),
         scratch_shapes=[pltpu.VMEM((64 * TILES, PAIR_ROWS), bf16)],
-        compiler_params=pltpu.CompilerParams(vmem_limit_bytes=VMEM_LIMIT),
+        compiler_params=pltpu.CompilerParams(vmem_limit_bytes=38 * MIB),
         cost_estimate=pl.CostEstimate(flops=2 * PAIR_ROWS * SLOTS * atoms, bytes_accessed=atoms * 700, transcendentals=0),
         name="feature_rows",
     )(positions, total, classes)
 
 
-def position_kernel(pick_ref, pos_ref, feat_ref, cot_ref, uv_ref, posg_ref, *slots_refs):
-    size = slots_refs[0].shape[1]
-    for k, slots_ref in enumerate(slots_refs):
-        at = slice(k * size, (k + 1) * size)
-        trig = multiples(pos_ref[:, at])
-        fill_slots(slots_ref, trig[0], row_tables(pick_ref, feat_ref[at, :], cot_ref[at, :]))
-        both = jnp.dot(uv_ref[:, 0:SLOTS], slots_ref[...], preferred_element_type=f32)
-        posg_ref[:, at] = position_sums(trig, both[0:PAIR_ROWS], both[PAIR_ROWS:])
+def position_half(pick_ref, pos_ref, feat_ref, cot_ref, uv_ref, slots_ref):
+    trig = multiples(pos_ref[...])
+    fill_slots(slots_ref, trig[0], row_tables(pick_ref, feat_ref[...], cot_ref[...]))
+    both = jnp.dot(uv_ref[:, 0:1024], slots_ref[0:1024, :], preferred_element_type=f32)
+    last = jnp.dot(uv_ref[0:PAIR_ROWS, 1024:SLOTS], slots_ref[1024:SLOTS, :], preferred_element_type=f32)
+    return position_sums(trig, both[0:PAIR_ROWS] + last, both[PAIR_ROWS:])
+
+
+def position_kernel(pick_ref, pos_ref, feat_ref, cot_ref, uv_ref, *refs):
+    *early_refs, posg_ref, slots_ref = refs
+    at = 0
+    for early_ref in early_refs:
+        at = early_ref.shape[1]
+        posg_ref[:, 0:at] = early_ref[...]
+    posg_ref[:, at : at + pos_ref.shape[1]] = position_half(pick_ref, pos_ref, feat_ref, cot_ref, uv_ref, slots_ref)
+
+
+def place_kernel(pick_ref, *refs):
+    place = pick_ref[0]
+    out_refs, all_refs = refs[8:10], refs[10:12]
+    for k, (out_ref, all_ref) in enumerate(zip(out_refs, all_refs)):
+        for flip, part_ref in enumerate(refs[4 * k : 4 * k + 4]):
+            all_ref[pl.ds(pl.multiple_of(32 * jnp.bitwise_xor(place, flip), 32), 32), :] = part_ref[...]
+        rows = out_ref.shape[0]
+        width = min(512, rows)
+        for at in range(0, rows, width):
+            out_ref[at : at + width, :] = all_ref[:, at : at + width].T
+
+
+def place_rows(pick, first, second):
+    shapes = [first[0].shape, second[0].shape]
+    whole = lambda shape: pl.BlockSpec(shape, lambda: (0, 0))
+    return pl.pallas_call(
+        place_kernel,
+        in_specs=[pl.BlockSpec(memory_space=pltpu.SMEM)] + [whole(s) for s in shapes for _ in range(4)],
+        out_specs=tuple(whole((s[1], 128)) for s in shapes),
+        out_shape=tuple(jax.ShapeDtypeStruct((s[1], 128), f32) for s in shapes),
+        scratch_shapes=[pltpu.VMEM((128, s[1]), f32) for s in shapes],
+        compiler_params=pltpu.CompilerParams(vmem_limit_bytes=20 * MIB),
+        cost_estimate=pl.CostEstimate(flops=6 * 10**9, bytes_accessed=4 * 10**6, transcendentals=0),
+        name="place_rows",
+    )(pick, *first, *second)
 
 
 def position_sums(trig, u, v):
@@ -379,29 +404,35 @@
     return phase_step * jnp.concatenate(rows, 0)
 
 
-def position_rows(pick, positions, features, cotangent, uv, block, cuts):
-    atoms = positions.shape[1]
+def position_rows(pick, positions, features, cotangent, uv, half, early, flops):
+    block = positions.shape[1] // 2
+    width = block * (1 + len(early))
     return pl.pallas_call(
         position_kernel,
-        grid=(atoms // block,),
+        grid=(1,),
         in_specs=[
             pl.BlockSpec(memory_space=pltpu.SMEM),
-            pl.BlockSpec((3, block), lambda i: (0, i)),
-            pl.BlockSpec((block, 128), lambda i: (i, 0)),
-            pl.BlockSpec((block, 128), lambda i: (i, 0)),
+            pl.BlockSpec((3, block), lambda i: (0, half)),
+            pl.BlockSpec((block, 128), lambda i: (half, 0)),
+            pl.BlockSpec((block, 128), lambda i: (half, 0)),
             pl.BlockSpec((2 * PAIR_ROWS, 128 * TILES), lambda i: (0, 0)),
-        ],
-        out_specs=pl.BlockSpec((3, block), lambda i: (0, i)),
-        out_shape=jax.ShapeDtypeStruct((3, atoms), f32),
-        scratch_shapes=[pltpu.VMEM((SLOTS, block // cuts), bf16)] * cuts,
-        compiler_params=pltpu.CompilerParams(vmem_limit_bytes=VMEM_LIMIT),
-        cost_estimate=pl.CostEstimate(flops=4 * PAIR_ROWS * SLOTS * atoms, bytes_accessed=atoms * 700, transcendentals=0),
+        ]
+        + [pl.BlockSpec((3, block), lambda i: (0, 0)) for _ in early],
+        out_specs=pl.BlockSpec((3, width), lambda i: (0, 0)),
+        out_shape=jax.ShapeDtypeStruct((3, width), f32),
+        scratch_shapes=[pltpu.VMEM((SLOTS, block), bf16)],
+        compiler_params=pltpu.CompilerParams(vmem_limit_bytes=24 * MIB),
+        cost_estimate=pl.CostEstimate(flops=flops, bytes_accessed=block * 700, transcendentals=0),
         name="position_rows",
-    )(pick, positions, features, cotangent, uv)
+    )(pick, positions, features, cotangent, uv, *early)
 
 
 def swap(value, axis):
     return lax.ppermute(value, axis, [(0, 1), (1, 0)])
+
+
+def swap_both(value):
+    return lax.ppermute(value, ("yl", "core"), [(i, 3 - i) for i in range(4)])
 
 
 def sum_scatter(value, axis):
@@ -414,14 +445,6 @@
     n = lax.axis_size(axis)
     copies = jnp.broadcast_to(value[None], (n,) + value.shape)
     return lax.all_to_all(copies, axis, 0, 0).reshape(n * value.shape[0], 128)
-
-
-def order_channels(own, across, beside, far, y_at, core_at):
-    mine_y = jnp.where(y_at == 0, jnp.stack([own, across]), jnp.stack([across, own]))
-    other_y = jnp.where(y_at == 0, jnp.stack([beside, far]), jnp.stack([far, beside]))
-    even = jnp.where(core_at == 0, mine_y, other_y)
-    odd = jnp.where(core_at == 0, other_y, mine_y)
-    return jnp.concatenate([even[0], odd[0], even[1], odd[1]], 0).T
 
 
 def shards(block, positions, features, cotangent, miller, radial_filter):
@@ -457,15 +480,18 @@
     grad, uv = feature_rows(positions, total, classes, atoms)
     grad_y, grad_core = swap(grad, "yl"), swap(grad, "core")
     total = lax.optimization_barrier((total, grad))[0]
-    own, beside, send = filter_rows(miller_rows, total, scale)
-    came, beside = swap(send, "yl"), swap(beside, "core")
+    own, across, beside, far = filter_rows(miller_rows, total, scale)
     uv = lax.optimization_barrier((uv, own))[0]
-    posg = position_rows(pick, positions, features, cotangent, uv, block, 1)
-    grad_y, came, posg = lax.optimization_barrier((grad_y, came, posg))
-    both = lax.ppermute(posg, ("yl", "core"), [(i, 3 - i) for i in range(4)])
-    position_grad = (posg + swap(posg, "core")) + (swap(posg, "yl") + both)
-    feature_grad = order_channels(grad, grad_y, grad_core, swap(grad_y, "core"), y_at, core_at)
-    filter_grad = order_channels(own, came[0], beside, swap(came, "core")[1], y_at, core_at)
+    across, beside, far = swap(across, "yl"), swap(beside, "core"), swap_both(far)
+    early = position_rows(pick, positions, features, cotangent, uv, 0, [], 10**9)
+    grad_y, early = lax.optimization_barrier((grad_y, early))
+    grad_far = swap(grad_y, "core")
+    posg = position_rows(pick, positions, features, cotangent, uv, 1, [early], 10**9)
+    across, far, grad_far, posg = lax.optimization_barrier((across, far, grad_far, posg))
+    posg_far, posg_y, posg_core = swap_both(posg), swap(posg, "yl"), swap(posg, "core")
+    feature_grad, filter_grad = place_rows(pick, (grad, grad_core, grad_y, grad_far), (own, beside, across, far))
+    posg_far, posg_y, posg_core, filter_grad = lax.optimization_barrier((posg_far, posg_y, posg_core, filter_grad))
+    position_grad = (posg + posg_core) + (posg_y + posg_far)
     return feature_grad, position_grad, filter_grad
 
 

time: 129 us -> 119 us (0.922)
  Pallas kernels: 39.5 us -> 31.5 us
  waiting for transfers between devices: 40.2 us -> 46.2 us
  local copies, waits for them, and re-layouts: 6.17 us -> 2.07 us
  other arithmetic: 4.34 us -> 1.61 us
    unnamed x15 -> x11, local copies, waits for them, and re-layouts: 4.09 us -> 0.22 us
    all_to_all x2, waiting for transfers between devices: 12.1 us -> 15.8 us  [gather(): return lax.all_to_all(copies, axis, 0, 0).reshape(n * value.shape[0], 128)]
    ppermute x1 -> x2, starting transfers between devices: 5.51 us -> 2.43 us  [swap_both(): return lax.ppermute(value, ('yl', 'core'), [(i, 3 - i) for i in range(4)])]
    pallas_call x1, Pallas kernels: 6.36 us -> 3.65 us  [feature_rows(): pl.pallas_call(feature_kernel, grid=(atoms // block,), in_specs=[pl.Block...]
    pallas_call x1, Pallas kernels: 6.77 us -> 4.5 us  [class_sums(): pl.pallas_call(functools.partial(class_kernel, scale), grid=(waves // blo...]
    pallas_call x1, Pallas kernels: 7.89 us -> 5.73 us  [filter_rows(): pl.pallas_call(functools.partial(filter_kernel, scale), grid=(4,), in_spe...]
    ppermute x10 -> x9, starting transfers between devices: 8.7 us -> 10.8 us  [swap(): return lax.ppermute(value, axis, [(0, 1), (1, 0)])]
    ppermute x1 -> x2, waiting for transfers between devices: 0.53 us -> 2.35 us  [swap_both(): return lax.ppermute(value, ('yl', 'core'), [(i, 3 - i) for i in range(4)])]
  transfers between devices with their start and end apart: 15 -> 15, of which waited for: 6 -> 7; matrix products, arithmetic and copies ran while one was open for 5% -> 2% of each run, Pallas kernels for 20% -> 17%
where the time goes in v3:
time: 119 us; the launch traced here: 118 us
  waiting for transfers between devices  46.2 us (39%)
  starting transfers between devices  36 us (30%)
  Pallas kernels  31.5 us (26%)
  local copies, waits for them, and re-layouts  2.07 us (2%)
  other arithmetic  1.61 us (1%)
    all_to_all x2, waiting for transfers between devices, sum_scatter(): lax.all_to_all(value.reshape(n, value.shape[0] // n, 128), axis, 0, 0)  26.7 us
    all_to_all x2, waiting for transfers between devices, gather(): return lax.all_to_all(copies, axis, 0, 0).reshape(n * value.shape[0], 128)  15.8 us
    all_to_all x2, starting transfers between devices, sum_scatter(): lax.all_to_all(value.reshape(n, value.shape[0] // n, 128), axis, 0, 0)  15.8 us
    ppermute x9, starting transfers between devices, swap(): return lax.ppermute(value, axis, [(0, 1), (1, 0)])  10.8 us
    pallas_call x2, Pallas kernels, position_rows(): pl.pallas_call(position_kernel, grid=(1,), in_specs=[pl.BlockSpec(memory_...  7.82 us
    pallas_call x1, Pallas kernels, factors(): pl.pallas_call(factor_kernel, grid=(atoms // block,), in_specs=[pl.BlockS...  7.55 us
    all_to_all x2, starting transfers between devices, gather(): return lax.all_to_all(copies, axis, 0, 0).reshape(n * value.shape[0], 128)  6.95 us
    pallas_call x1, Pallas kernels, filter_rows(): pl.pallas_call(functools.partial(filter_kernel, scale), grid=(4,), in_spe...  5.73 us
  transfers between devices with their start and end apart: 15, of which 7 were waited for; matrix products, arithmetic and copies ran while one was open for 2% of the time, Pallas kernels for 17%

profile of v3, /device:TPU:1, one launch (start us, length us, event | category | flops | bytes accessed | tf_op | source)
XLA Modules:
  0.0 118.2 jit_solution(6724315624531056887)
XLA Ops:
  0.6 7.6 %factors.1 = f32[2560,128]{1,0:T(8,128)} custom-call(s32[1]{0:T(128)} %bitcast.pick_ref, f32[3,4096]{1,0:T(4,128)} %pos_ref.7, bf16[4096,128]{1,0:T(8,128)(2,1)} %feat_ref.5, bf16[4096,128]{1,0:T(8,128)(2,1)} %cot_ref.5), custom_call_target="tpu_custom_call" | custom-call | flops 2709520384 | bytes 2129920 | tf_op jit(solution)/shard_map/factors/pallas_call | solution.py:104
  8.2 7.6 %all-to-all-start = ((f32[8,320,128]{2,1,0:T(8,128)}), f32[8,320,128]{2,1,0:T(8,128)S(1)}, u32[]{:S(2)}, u32[]{:S(2)}) async-start(f32[8,320,128]{2,1,0:T(8,128)} %bitcast.9), calls=%async_computation | async-start | bytes 2621440 | tf_op jit(solution)/shard_map/all_to_all | solution.py:440
  16.6 18.4 %all-to-all-done = f32[8,320,128]{2,1,0:T(8,128)S(1)} async-done(((f32[8,320,128]{2,1,0:T(8,128)}), f32[8,320,128]{2,1,0:T(8,128)S(1)}, u32[]{:S(2)}, u32[]{:S(2)}) %all-to-all-start) | async-done | bytes 1310752 | tf_op jit(solution)/shard_map/all_to_all | solution.py:440
  35.1 0.7 reduce_sum.18
  35.8 8.2 %all-to-all-start.1 = ((f32[8,40,128]{2,1,0:T(8,128)}), f32[8,40,128]{2,1,0:T(8,128)S(1)}, u32[]{:S(2)}, u32[]{:S(2)}) async-start(f32[8,40,128]{2,1,0:T(8,128)} %bitcast.2), calls=%async_computation.1 | async-start | bytes 327680 | tf_op jit(solution)/shard_map/all_to_all | solution.py:440
  44.1 8.2 %all-to-all-done.1 = f32[8,40,128]{2,1,0:T(8,128)S(1)} async-done(((f32[8,40,128]{2,1,0:T(8,128)}), f32[8,40,128]{2,1,0:T(8,128)S(1)}, u32[]{:S(2)}, u32[]{:S(2)}) %all-to-all-start.1) | async-done | bytes 163872 | tf_op jit(solution)/shard_map/all_to_all | solution.py:440
  53.0 3.4 %all-to-all-start.2 = ((f32[8,40,128]{2,1,0:T(8,128)}), f32[8,40,128]{2,1,0:T(8,128)S(1)}, u32[]{:S(2)}, u32[]{:S(2)}) async-start(f32[8,40,128]{2,1,0:T(8,128)} %broadcast_in_dim.16), calls=%async_computation.2 | async-start | bytes 327680 | tf_op jit(solution)/shard_map/all_to_all | solution.py:447
  56.4 3.1 %collective-permute-start.1 = (f32[40,2048]{1,0:T(8,128)S(1)}, f32[40,2048]{1,0:T(8,128)S(1)}, u32[]{:S(2)}, u32[]{:S(2)}) collective-permute-start(f32[40,2048]{1,0:T(8,128)S(1)} %pad_maximum_fusion.1), channel_id=1, source_target_pairs={{0,1},{1,0},{2,3},{3,2},{4,5},{5,4},{6,7},{7,6},{8,9},{9,8},{10,11... | collective-permute-start | bytes 983048 | tf_op jit(solution)/shard_map/ppermute | solution.py:431
  59.5 5.0 %all-to-all-done.2 = f32[8,40,128]{2,1,0:T(8,128)S(1)} async-done(((f32[8,40,128]{2,1,0:T(8,128)}), f32[8,40,128]{2,1,0:T(8,128)S(1)}, u32[]{:S(2)}, u32[]{:S(2)}) %all-to-all-start.2) | async-done | bytes 163872 | tf_op jit(solution)/shard_map/all_to_all | solution.py:447
  64.6 1.1 broadcast_in_dim.18
  65.7 3.6 %all-to-all-start.3 = ((f32[8,320,128]{2,1,0:T(8,128)}), f32[8,320,128]{2,1,0:T(8,128)S(1)}, u32[]{:S(2)}, u32[]{:S(2)}) async-start(f32[8,320,128]{2,1,0:T(8,128)} %broadcast_in_dim.18), calls=%async_computation.3 | async-start | bytes 2621440 | tf_op jit(solution)/shard_map/all_to_all | solution.py:447
  69.4 4.5 %class_sums.1.class_ref = f32[4,896,128]{2,1,0:T(8,128)S(1)} custom-call(f32[8,4096]{1,0:T(8,128)S(1)} %pad_maximum_fusion.7.miller_ref, f32[32,4096]{1,0:T(8,128)S(1)} %pad_maximum_fusion.radial_ref), custom_call_target="tpu_custom_call" | custom-call | flops 1879048192 | bytes 655360 | tf_op jit(solution)/shard_map/class_sums/pallas_call | solution.py:169
  73.9 10.8 %all-to-all-done.3 = f32[8,320,128]{2,1,0:T(8,128)S(1)} async-done(((f32[8,320,128]{2,1,0:T(8,128)}), f32[8,320,128]{2,1,0:T(8,128)S(1)}, u32[]{:S(2)}, u32[]{:S(2)}) %all-to-all-start.3) | async-done | bytes 1310752 | tf_op jit(solution)/shard_map/all_to_all | solution.py:447
  84.7 3.6 %feature_rows.1 = (f32[32,4096]{1,0:T(8,128)S(1)}, bf16[608,1152]{1,0:T(8,128)(2,1)S(1)}) custom-call(f32[3,4096]{1,0:T(4,128)S(1)} %copy-done.2, f32[2560,128]{1,0:T(8,128)S(1)} %bitcast.6, f32[4,896,128]{2,1,0:T(8,128)S(1)} %class_sums.1.class_ref), custom_call_target="tpu_custom_call" | custom-call | flops 2709520384 | bytes 2867200 | tf_op jit(solution)/shard_map/feature_rows/pallas_call | solution.py:322
  88.8 5.7 %filter_rows.1 = (f32[32,1024]{1,0:T(8,128)S(1)}, f32[32,1024]{1,0:T(8,128)S(1)}, f32[32,1024]{1,0:T(8,128)S(1)}, f32[32,1024]{1,0:T(8,128)S(1)}) custom-call(f32[8,4096]{1,0:T(8,128)S(1)} %pad_maximum_fusion.7.miller_ref, f32[2560,128]{1,0:T(8,128)S(1)} %bitcast.7), custom_call_target="tpu_custom_call" | custom-call | flops 1879048192 | bytes 655360 | tf_op jit(solution)/shard_map/filter_rows/pallas_call | solution.py:293
  94.5 3.9 %position_rows.2.refs_0_ = f32[3,2048]{1,0:T(4,128)S(1)} custom-call(s32[1]{0:T(128)} %bitcast.pick_ref, f32[3,4096]{1,0:T(4,128)S(1)} %copy-done.2, bf16[4096,128]{1,0:T(8,128)(2,1)S(1)} %copy-done, bf16[4096,128]{1,0:T(8,128)(2,1)S(1)} %copy-done.1, bf16[608,1152]{1,0:T(8,128)(2,1)S(1)} %get-tuple-element.27.uv_ref), custom_call_target="tpu_custom_call" | custom-call | flops 1000000000 | bytes 1433600 | tf_op jit(solution)/shard_map/position_rows/pallas_call | solution.py:410
  98.5 5.2 %collective-permute-start.6 = (f32[32,4096]{1,0:T(8,128)S(1)}, f32[32,4096]{1,0:T(8,128)S(1)}, u32[]{:S(2)}, u32[]{:S(2)}) collective-permute-start(f32[32,4096]{1,0:T(8,128)S(1)} %collective-permute-done.3.refs_2_), channel_id=1, source_target_pairs={{0,1},{1,0},{2,3},{3,2},{4,5},{5,4},{6,7},{7,6},{8,9},{9,8},{10,11... | collective-permute-start | bytes 1572872 | tf_op jit(solution)/shard_map/ppermute | solution.py:431
  103.8 1.1 collective-permute-start.4
  104.8 1.0 collective-permute-start.5
  105.8 3.9 %position_rows.3 = f32[3,4096]{1,0:T(4,128)S(1)} custom-call(s32[1]{0:T(128)} %bitcast.pick_ref, f32[3,4096]{1,0:T(4,128)S(1)} %copy-done.2, bf16[4096,128]{1,0:T(8,128)(2,1)S(1)} %copy-done, bf16[4096,128]{1,0:T(8,128)(2,1)S(1)} %copy-done.1, bf16[608,1152]{1,0:T(8,128)(2,1)S(1)} %get-tuple-element.27.uv_ref, f32[3,2048]{1,0:T(4,128)S(1)} %position_rows.2.refs_0_), custom_call_target="tpu_custom_call" | custom-call | flops 1000000000 | bytes 1433600 | tf_op jit(solution)/shard_map/position_rows/pallas_call | solution.py:410
  109.7 2.1 %collective-permute-done.5.refs_7_ = f32[32,1024]{1,0:T(8,128)S(1)} collective-permute-done((f32[32,1024]{1,0:T(8,128)S(1)}, f32[32,1024]{1,0:T(8,128)S(1)}, u32[]{:S(2)}, u32[]{:S(2)}) %collective-permute-start.5) | collective-permute-done | bytes 131104 | tf_op jit(solution)/shard_map/ppermute | solution.py:435
  111.8 1.5 %collective-permute-start.8 = (f32[3,4096]{1,0:T(4,128)S(1)}, f32[3,4096]{1,0:T(4,128)S(1)}, u32[]{:S(2)}, u32[]{:S(2)}) collective-permute-start(f32[3,4096]{1,0:T(4,128)S(1)} %position_rows.3), channel_id=1, source_target_pairs={{0,3},{1,2},{2,1},{3,0},{4,7},{5,6},{6,5},{7,4},{8,11},{9,10},{10,... | collective-permute-start | bytes 147464 | tf_op jit(solution)/shard_map/ppermute | solution.py:435
  113.7 2.2 %place_rows.1 = (f32[4096,128]{1,0:T(8,128)}, f32[1024,128]{1,0:T(8,128)}) custom-call(s32[1]{0:T(128)} %bitcast.pick_ref, f32[32,4096]{1,0:T(8,128)S(1)} %get-tuple-element.23.refs_0_, f32[32,4096]{1,0:T(8,128)S(1)} %collective-permute-done.2.refs_1_, f32[32,4096]{1,0:T(8,128)S(1)} %collective-permute-done.3.refs_2_, ...), custom_call_target="tpu_custom_call" | custom-call | flops 6000000000 | bytes 4000000 | tf_op jit(solution)/shard_map/place_rows/pallas_call | solution.py:377
  116.2 1.3 %collective-permute-done.9 = f32[3,4096]{1,0:T(4,128)S(1)} collective-permute-done((f32[3,4096]{1,0:T(4,128)S(1)}, f32[3,4096]{1,0:T(4,128)S(1)}, u32[]{:S(2)}, u32[]{:S(2)}) %collective-permute-start.9) | collective-permute-done | bytes 49184 | tf_op jit(solution)/shard_map/ppermute | solution.py:431
  (40 shorter events, 3.5 us)
Async XLA Ops:
  8.2 7.6 %copy-start.3 = (f32[1024,128]{1,0:T(8,128)S(1)}, f32[1024,128]{1,0:T(8,128)}, u32[]{:S(2)}) copy-start(f32[1024,128]{1,0:T(8,128)} %param.9) | copy-start | bytes 1572868
  8.2 7.8 %copy-start.4 = (s32[3,1024]{1,0:T(4,128)S(1)}, s32[3,1024]{1,0:T(4,128)}, u32[]{:S(2)}) copy-start(s32[3,1024]{1,0:T(4,128)} %param.8) | copy-start | bytes 36868
  8.2 26.9 %all-to-all-start = ((f32[8,320,128]{2,1,0:T(8,128)}), f32[8,320,128]{2,1,0:T(8,128)S(1)}, u32[]{:S(2)}, u32[]{:S(2)}) async-start(f32[8,320,128]{2,1,0:T(8,128)} %bitcast.9), calls=%async_computation | async-start | bytes 2621440 | tf_op jit(solution)/shard_map/all_to_all | solution.py:440
  16.1 27.9 %collective-permute-start = (f32[72,1024]{1,0:T(8,128)S(1)}, f32[72,1024]{1,0:T(8,128)S(1)}, u32[]{:S(2)}, u32[]{:S(2)}) collective-permute-start(f32[72,1024]{1,0:T(8,128)S(1)} %pad_maximum_fusion.2), channel_id=1, source_target_pairs={{0,2},{2,0},{1,3},{3,1},{4,6},{6,4},{5,7},{7,5},{8,10},{10,8},{9,1... | collective-permute-start | bytes 884744 | tf_op jit(solution)/shard_map/ppermute | solution.py:431
  35.8 16.5 %all-to-all-start.1 = ((f32[8,40,128]{2,1,0:T(8,128)}), f32[8,40,128]{2,1,0:T(8,128)S(1)}, u32[]{:S(2)}, u32[]{:S(2)}) async-start(f32[8,40,128]{2,1,0:T(8,128)} %bitcast.2), calls=%async_computation.1 | async-start | bytes 327680 | tf_op jit(solution)/shard_map/all_to_all | solution.py:440
  53.0 11.6 %all-to-all-start.2 = ((f32[8,40,128]{2,1,0:T(8,128)}), f32[8,40,128]{2,1,0:T(8,128)S(1)}, u32[]{:S(2)}, u32[]{:S(2)}) async-start(f32[8,40,128]{2,1,0:T(8,128)} %broadcast_in_dim.16), calls=%async_computation.2 | async-start | bytes 327680 | tf_op jit(solution)/shard_map/all_to_all | solution.py:447
  56.4 12.9 %collective-permute-start.1 = (f32[40,2048]{1,0:T(8,128)S(1)}, f32[40,2048]{1,0:T(8,128)S(1)}, u32[]{:S(2)}, u32[]{:S(2)}) collective-permute-start(f32[40,2048]{1,0:T(8,128)S(1)} %pad_maximum_fusion.1), channel_id=1, source_target_pairs={{0,1},{1,0},{2,3},{3,2},{4,5},{5,4},{6,7},{7,6},{8,9},{9,8},{10,11... | collective-permute-start | bytes 983048 | tf_op jit(solution)/shard_map/ppermute | solution.py:431
  65.7 19.0 %all-to-all-start.3 = ((f32[8,320,128]{2,1,0:T(8,128)}), f32[8,320,128]{2,1,0:T(8,128)S(1)}, u32[]{:S(2)}, u32[]{:S(2)}) async-start(f32[8,320,128]{2,1,0:T(8,128)} %broadcast_in_dim.18), calls=%async_computation.3 | async-start | bytes 2621440 | tf_op jit(solution)/shard_map/all_to_all | solution.py:447
  69.4 15.3 %copy-start.2 = (f32[3,4096]{1,0:T(4,128)S(1)}, f32[3,4096]{1,0:T(4,128)}, u32[]{:S(2)}) copy-start(f32[3,4096]{1,0:T(4,128)} %pos_ref.7) | copy-start | bytes 147460
  88.3 6.2 %copy-start = (bf16[4096,128]{1,0:T(8,128)(2,1)S(1)}, bf16[4096,128]{1,0:T(8,128)(2,1)}, u32[]{:S(2)}) copy-start(bf16[4096,128]{1,0:T(8,128)(2,1)} %feat_ref.5) | copy-start | bytes 3145732
  88.4 6.2 %copy-start.1 = (bf16[4096,128]{1,0:T(8,128)(2,1)S(1)}, bf16[4096,128]{1,0:T(8,128)(2,1)}, u32[]{:S(2)}) copy-start(bf16[4096,128]{1,0:T(8,128)(2,1)} %cot_ref.5) | copy-start | bytes 3145732
  88.4 10.1 %collective-permute-start.3 = (f32[32,4096]{1,0:T(8,128)S(1)}, f32[32,4096]{1,0:T(8,128)S(1)}, u32[]{:S(2)}, u32[]{:S(2)}) collective-permute-start(f32[32,4096]{1,0:T(8,128)S(1)} %get-tuple-element.23.refs_0_), channel_id=1, source_target_pairs={{0,2},{2,0},{1,3},{3,1},{4,6},{6,4},{5,7},{7,5},{8,10},{10,8},{9,1... | collective-permute-start | bytes 1572872 | tf_op jit(solution)/shard_map/ppermute | solution.py:431
  98.5 13.3 %collective-permute-start.6 = (f32[32,4096]{1,0:T(8,128)S(1)}, f32[32,4096]{1,0:T(8,128)S(1)}, u32[]{:S(2)}, u32[]{:S(2)}) collective-permute-start(f32[32,4096]{1,0:T(8,128)S(1)} %collective-permute-done.3.refs_2_), channel_id=1, source_target_pairs={{0,1},{1,0},{2,3},{3,2},{4,5},{5,4},{6,7},{7,6},{8,9},{9,8},{10,11... | collective-permute-start | bytes 1572872 | tf_op jit(solution)/shard_map/ppermute | solution.py:431
  103.7 10.0 %collective-permute-start.2 = (f32[32,4096]{1,0:T(8,128)S(1)}, f32[32,4096]{1,0:T(8,128)S(1)}, u32[]{:S(2)}, u32[]{:S(2)}) collective-permute-start(f32[32,4096]{1,0:T(8,128)S(1)} %get-tuple-element.23.refs_0_), channel_id=1, source_target_pairs={{0,1},{1,0},{2,3},{3,2},{4,5},{5,4},{6,7},{7,6},{8,9},{9,8},{10,11... | collective-permute-start | bytes 1572872 | tf_op jit(solution)/shard_map/ppermute | solution.py:431
  103.8 6.0 %collective-permute-start.4 = (f32[32,1024]{1,0:T(8,128)S(1)}, f32[32,1024]{1,0:T(8,128)S(1)}, u32[]{:S(2)}, u32[]{:S(2)}) collective-permute-start(f32[32,1024]{1,0:T(8,128)S(1)} %get-tuple-element.29), channel_id=1, source_target_pairs={{0,2},{2,0},{1,3},{3,1},{4,6},{6,4},{5,7},{7,5},{8,10},{10,8},{9,1... | collective-permute-start | bytes 393224 | tf_op jit(solution)/shard_map/ppermute | solution.py:431
  104.8 7.0 %collective-permute-start.5 = (f32[32,1024]{1,0:T(8,128)S(1)}, f32[32,1024]{1,0:T(8,128)S(1)}, u32[]{:S(2)}, u32[]{:S(2)}) collective-permute-start(f32[32,1024]{1,0:T(8,128)S(1)} %get-tuple-element.30), channel_id=1, source_target_pairs={{0,3},{1,2},{2,1},{3,0},{4,7},{5,6},{6,5},{7,4},{8,11},{9,10},{10,... | collective-permute-start | bytes 393224 | tf_op jit(solution)/shard_map/ppermute | solution.py:435
  105.8 7.9 %collective-permute-start.7 = (f32[32,1024]{1,0:T(8,128)S(1)}, f32[32,1024]{1,0:T(8,128)S(1)}, u32[]{:S(2)}, u32[]{:S(2)}) collective-permute-start(f32[32,1024]{1,0:T(8,128)S(1)} %get-tuple-element.33), channel_id=1, source_target_pairs={{0,1},{1,0},{2,3},{3,2},{4,5},{5,4},{6,7},{7,6},{8,9},{9,8},{10,11... | collective-permute-start | bytes 393224 | tf_op jit(solution)/shard_map/ppermute | solution.py:431
  111.8 4.1 %collective-permute-start.10 = (f32[3,4096]{1,0:T(4,128)S(1)}, f32[3,4096]{1,0:T(4,128)S(1)}, u32[]{:S(2)}, u32[]{:S(2)}) collective-permute-start(f32[3,4096]{1,0:T(4,128)S(1)} %position_rows.3), channel_id=1, source_target_pairs={{0,1},{1,0},{2,3},{3,2},{4,5},{5,4},{6,7},{7,6},{8,9},{9,8},{10,11... | collective-permute-start | bytes 147464 | tf_op jit(solution)/shard_map/ppermute | solution.py:431
  111.8 4.4 %collective-permute-start.8 = (f32[3,4096]{1,0:T(4,128)S(1)}, f32[3,4096]{1,0:T(4,128)S(1)}, u32[]{:S(2)}, u32[]{:S(2)}) collective-permute-start(f32[3,4096]{1,0:T(4,128)S(1)} %position_rows.3), channel_id=1, source_target_pairs={{0,3},{1,2},{2,1},{3,0},{4,7},{5,6},{6,5},{7,4},{8,11},{9,10},{10,... | collective-permute-start | bytes 147464 | tf_op jit(solution)/shard_map/ppermute | solution.py:435
  113.3 4.3 %collective-permute-start.9 = (f32[3,4096]{1,0:T(4,128)S(1)}, f32[3,4096]{1,0:T(4,128)S(1)}, u32[]{:S(2)}, u32[]{:S(2)}) collective-permute-start(f32[3,4096]{1,0:T(4,128)S(1)} %position_rows.3), channel_id=1, source_target_pairs={{0,2},{2,0},{1,3},{3,1},{4,6},{6,4},{5,7},{7,5},{8,10},{10,8},{9,1... | collective-permute-start | bytes 147464 | tf_op jit(solution)/shard_map/ppermute | solution.py:431

commit v4 on v3

--- a/solution.py
+++ b/solution.py
@@ -86,15 +86,18 @@
     def _():
         total_ref[...] = product
 
-    @pl.when(step > 0)
+    final = pl.num_programs(0) - 1
+
+    @pl.when(jnp.logical_and(step > 0, step < final))
     def _():
         total_ref[...] += product
 
-    @pl.when(step == pl.num_programs(0) - 1)
+    @pl.when(step == final)
     def _():
         for t in range(8):
-            out_ref[PAIRS * t : PAIRS * (t + 1), :] = total_ref[0:PAIRS, 128 * t : 128 * t + 128]
-        last = total_ref[:, 1024:1088]
+            at = slice(128 * t, 128 * t + 128)
+            out_ref[PAIRS * t : PAIRS * (t + 1), :] = total_ref[0:PAIRS, at] + product[0:PAIRS, at]
+        last = total_ref[:, 1024:1088] + product[:, 1024:1088]
         out_ref[2368:2520, :] = jnp.concatenate([last[0:152], last[152:304]], 1)
         out_ref[2520:2560, :] = jnp.zeros((40, 128), f32)
 
@@ -267,14 +270,11 @@
     @pl.when(step == 0)
     def _():
         pair_products(total_ref, pair_ref)
-        hi, lo = split_hi_lo(pair_ref[...].T)
-        turned_ref[0:128, :] = hi
-        turned_ref[128:256, :] = lo
+        turned_ref[...] = pair_ref[...].T.astype(bf16)
 
     index, products = wave_class(miller_ref[0:3, :])
     hot = (lax.broadcasted_iota(jnp.int32, (CLASSES, index.shape[1]), 0) == index).astype(f32).astype(bf16)
     values = jnp.dot(turned_ref[...], hot, preferred_element_type=f32)
-    values = values[:128] + values[128:]
     rows = values[0:32]
     for q in range(3):
         rows = rows + products[q] * values[32 * (q + 1) : 32 * (q + 2)]
@@ -296,7 +296,7 @@
         in_specs=[pl.BlockSpec((8, block), lambda i: (0, i)), pl.BlockSpec((PACKED, 128), lambda i: (0, 0))],
         out_specs=(pl.BlockSpec((32, block), lambda i: (0, 0)),) * 4,
         out_shape=(one,) * 4,
-        scratch_shapes=[pltpu.VMEM((CLASSES, 128), f32), pltpu.VMEM((256, CLASSES), bf16)],
+        scratch_shapes=[pltpu.VMEM((CLASSES, 128), f32), pltpu.VMEM((128, CLASSES), bf16)],
         compiler_params=pltpu.CompilerParams(vmem_limit_bytes=18 * MIB),
         cost_estimate=pl.CostEstimate(flops=2 * CLASSES * 1024 * block, bytes_accessed=block * 640, transcendentals=0),
         name="filter_rows",
@@ -342,21 +342,12 @@
     )(positions, total, classes)
 
 
-def position_half(pick_ref, pos_ref, feat_ref, cot_ref, uv_ref, slots_ref):
+def position_kernel(pick_ref, pos_ref, feat_ref, cot_ref, uv_ref, posg_ref, slots_ref):
     trig = multiples(pos_ref[...])
     fill_slots(slots_ref, trig[0], row_tables(pick_ref, feat_ref[...], cot_ref[...]))
     both = jnp.dot(uv_ref[:, 0:1024], slots_ref[0:1024, :], preferred_element_type=f32)
     last = jnp.dot(uv_ref[0:PAIR_ROWS, 1024:SLOTS], slots_ref[1024:SLOTS, :], preferred_element_type=f32)
-    return position_sums(trig, both[0:PAIR_ROWS] + last, both[PAIR_ROWS:])
-
-
-def position_kernel(pick_ref, pos_ref, feat_ref, cot_ref, uv_ref, *refs):
-    *early_refs, posg_ref, slots_ref = refs
-    at = 0
-    for early_ref in early_refs:
-        at = early_ref.shape[1]
-        posg_ref[:, 0:at] = early_ref[...]
-    posg_ref[:, at : at + pos_ref.shape[1]] = position_half(pick_ref, pos_ref, feat_ref, cot_ref, uv_ref, slots_ref)
+    posg_ref[...] = position_sums(trig, both[0:PAIR_ROWS] + last, both[PAIR_ROWS:])
 
 
 def place_kernel(pick_ref, *refs):
@@ -404,27 +395,25 @@
     return phase_step * jnp.concatenate(rows, 0)
 
 
-def position_rows(pick, positions, features, cotangent, uv, half, early, flops):
-    block = positions.shape[1] // 2
-    width = block * (1 + len(early))
+def position_rows(pick, positions, features, cotangent, uv, block):
+    atoms = positions.shape[1]
     return pl.pallas_call(
         position_kernel,
-        grid=(1,),
+        grid=(atoms // block,),
         in_specs=[
             pl.BlockSpec(memory_space=pltpu.SMEM),
-            pl.BlockSpec((3, block), lambda i: (0, half)),
-            pl.BlockSpec((block, 128), lambda i: (half, 0)),
-            pl.BlockSpec((block, 128), lambda i: (half, 0)),
+            pl.BlockSpec((3, block), lambda i: (0, i)),
+            pl.BlockSpec((block, 128), lambda i: (i, 0)),
+            pl.BlockSpec((block, 128), lambda i: (i, 0)),
             pl.BlockSpec((2 * PAIR_ROWS, 128 * TILES), lambda i: (0, 0)),
-        ]
-        + [pl.BlockSpec((3, block), lambda i: (0, 0)) for _ in early],
-        out_specs=pl.BlockSpec((3, width), lambda i: (0, 0)),
-        out_shape=jax.ShapeDtypeStruct((3, width), f32),
+        ],
+        out_specs=pl.BlockSpec((3, block), lambda i: (0, i)),
+        out_shape=jax.ShapeDtypeStruct((3, atoms), f32),
         scratch_shapes=[pltpu.VMEM((SLOTS, block), bf16)],
         compiler_params=pltpu.CompilerParams(vmem_limit_bytes=24 * MIB),
-        cost_estimate=pl.CostEstimate(flops=flops, bytes_accessed=block * 700, transcendentals=0),
+        cost_estimate=pl.CostEstimate(flops=4 * PAIR_ROWS * SLOTS * atoms, bytes_accessed=atoms * 700, transcendentals=0),
         name="position_rows",
-    )(pick, positions, features, cotangent, uv, *early)
+    )(pick, positions, features, cotangent, uv)
 
 
 def swap(value, axis):
@@ -472,7 +461,7 @@
     miller_rows = jnp.concatenate([pair_indices, beside[32:]], 1)
     classes = class_sums(miller_rows, radial_rows, scale, min(1024, 4 * waves))
 
-    part = factors(pick, positions, features, cotangent, block, 1)
+    part = factors(pick, positions, features, cotangent, min(block, atoms // 2), 1)
     part = sum_scatter(part, ("x", "yh"))
     part = sum_scatter(part, "z")
     part = gather(part, "z")
@@ -483,11 +472,9 @@
     own, across, beside, far = filter_rows(miller_rows, total, scale)
     uv = lax.optimization_barrier((uv, own))[0]
     across, beside, far = swap(across, "yl"), swap(beside, "core"), swap_both(far)
-    early = position_rows(pick, positions, features, cotangent, uv, 0, [], 10**9)
-    grad_y, early = lax.optimization_barrier((grad_y, early))
+    posg = position_rows(pick, positions, features, cotangent, uv, min(block, atoms))
+    across, far, grad_y, posg = lax.optimization_barrier((across, far, grad_y, posg))
     grad_far = swap(grad_y, "core")
-    posg = position_rows(pick, positions, features, cotangent, uv, 1, [early], 10**9)
-    across, far, grad_far, posg = lax.optimization_barrier((across, far, grad_far, posg))
     posg_far, posg_y, posg_core = swap_both(posg), swap(posg, "yl"), swap(posg, "core")
     feature_grad, filter_grad = place_rows(pick, (grad, grad_core, grad_y, grad_far), (own, beside, across, far))
     posg_far, posg_y, posg_core, filter_grad = lax.optimization_barrier((posg_far, posg_y, posg_core, filter_grad))

time: 119 us -> 115 us (0.966)
  waiting for transfers between devices: 46.2 us -> 43.2 us
  Pallas kernels: 31.5 us -> 30.3 us
    ppermute x2, waiting for transfers between devices: 2.35 us -> 0.01 us  [swap_both(): return lax.ppermute(value, ('yl', 'core'), [(i, 3 - i) for i in range(4)])]
    ppermute x9, starting transfers between devices: 10.8 us -> 12 us  [swap(): return lax.ppermute(value, axis, [(0, 1), (1, 0)])]
    pallas_call x2 -> x1, Pallas kernels: 7.82 us -> 7.89 us  [position_rows(): pl.pallas_call(position_kernel, grid=(atoms // block,), in_specs=[pl.Bloc...]
  transfers between devices with their start and end apart: 15 -> 15, of which waited for: 7 -> 6; matrix products, arithmetic and copies ran while one was open for 2% -> 2% of each run, Pallas kernels for 17% -> 17%
where the time goes in v4:
time: 115 us
  waiting for transfers between devices  43.2 us (38%)
  starting transfers between devices  36.6 us (32%)
  Pallas kernels  30.3 us (26%)
  local copies, waits for them, and re-layouts  2.07 us (2%)
  other arithmetic  1.62 us (1%)
    all_to_all x2, waiting for transfers between devices, sum_scatter(): lax.all_to_all(value.reshape(n, value.shape[0] // n, 128), axis, 0, 0)  26.7 us
    all_to_all x2, waiting for transfers between devices, gather(): return lax.all_to_all(copies, axis, 0, 0).reshape(n * value.shape[0], 128)  15.8 us
    all_to_all x2, starting transfers between devices, sum_scatter(): lax.all_to_all(value.reshape(n, value.shape[0] // n, 128), axis, 0, 0)  15.8 us
    ppermute x9, starting transfers between devices, swap(): return lax.ppermute(value, axis, [(0, 1), (1, 0)])  12 us
    pallas_call x1, Pallas kernels, position_rows(): pl.pallas_call(position_kernel, grid=(atoms // block,), in_specs=[pl.Bloc...  7.89 us
    pallas_call x1, Pallas kernels, factors(): pl.pallas_call(factor_kernel, grid=(atoms // block,), in_specs=[pl.BlockS...  7.47 us
    all_to_all x2, starting transfers between devices, gather(): return lax.all_to_all(copies, axis, 0, 0).reshape(n * value.shape[0], 128)  6.95 us
    pallas_call x1, Pallas kernels, filter_rows(): pl.pallas_call(functools.partial(filter_kernel, scale), grid=(4,), in_spe...  4.54 us
  transfers between devices with their start and end apart: 15, of which 6 were waited for; matrix products, arithmetic and copies ran while one was open for 2% of the time, Pallas kernels for 17%

profile of v4, /device:TPU:1, one launch (start us, length us, event | category | flops | bytes accessed | tf_op | source)
XLA Modules:
  0.0 114.6 jit_solution(16847881962414580409)
XLA Ops:
  0.6 7.5 %factors.1 = f32[2560,128]{1,0:T(8,128)} custom-call(s32[1]{0:T(128)} %bitcast.pick_ref, f32[3,4096]{1,0:T(4,128)} %pos_ref.5, bf16[4096,128]{1,0:T(8,128)(2,1)} %feat_ref.3, bf16[4096,128]{1,0:T(8,128)(2,1)} %cot_ref.3), custom_call_target="tpu_custom_call" | custom-call | flops 2709520384 | bytes 2129920 | tf_op jit(solution)/shard_map/factors/pallas_call | solution.py:107
  8.1 7.6 %all-to-all-start = ((f32[8,320,128]{2,1,0:T(8,128)}), f32[8,320,128]{2,1,0:T(8,128)S(1)}, u32[]{:S(2)}, u32[]{:S(2)}) async-start(f32[8,320,128]{2,1,0:T(8,128)} %bitcast.9), calls=%async_computation | async-start | bytes 2621440 | tf_op jit(solution)/shard_map/all_to_all | solution.py:429
  16.5 18.4 %all-to-all-done = f32[8,320,128]{2,1,0:T(8,128)S(1)} async-done(((f32[8,320,128]{2,1,0:T(8,128)}), f32[8,320,128]{2,1,0:T(8,128)S(1)}, u32[]{:S(2)}, u32[]{:S(2)}) %all-to-all-start) | async-done | bytes 1310752 | tf_op jit(solution)/shard_map/all_to_all | solution.py:429
  35.0 0.7 reduce_sum.18
  35.7 8.2 %all-to-all-start.1 = ((f32[8,40,128]{2,1,0:T(8,128)}), f32[8,40,128]{2,1,0:T(8,128)S(1)}, u32[]{:S(2)}, u32[]{:S(2)}) async-start(f32[8,40,128]{2,1,0:T(8,128)} %bitcast.2), calls=%async_computation.1 | async-start | bytes 327680 | tf_op jit(solution)/shard_map/all_to_all | solution.py:429
  44.0 8.2 %all-to-all-done.1 = f32[8,40,128]{2,1,0:T(8,128)S(1)} async-done(((f32[8,40,128]{2,1,0:T(8,128)}), f32[8,40,128]{2,1,0:T(8,128)S(1)}, u32[]{:S(2)}, u32[]{:S(2)}) %all-to-all-start.1) | async-done | bytes 163872 | tf_op jit(solution)/shard_map/all_to_all | solution.py:429
  52.2 0.7 broadcast_in_dim.16
  52.9 3.4 %all-to-all-start.2 = ((f32[8,40,128]{2,1,0:T(8,128)}), f32[8,40,128]{2,1,0:T(8,128)S(1)}, u32[]{:S(2)}, u32[]{:S(2)}) async-start(f32[8,40,128]{2,1,0:T(8,128)} %broadcast_in_dim.16), calls=%async_computation.2 | async-start | bytes 327680 | tf_op jit(solution)/shard_map/all_to_all | solution.py:436
  56.3 3.1 %collective-permute-start.1 = (f32[40,2048]{1,0:T(8,128)S(1)}, f32[40,2048]{1,0:T(8,128)S(1)}, u32[]{:S(2)}, u32[]{:S(2)}) collective-permute-start(f32[40,2048]{1,0:T(8,128)S(1)} %pad_maximum_fusion.1), channel_id=1, source_target_pairs={{0,1},{1,0},{2,3},{3,2},{4,5},{5,4},{6,7},{7,6},{8,9},{9,8},{10,11... | collective-permute-start | bytes 983048 | tf_op jit(solution)/shard_map/ppermute | solution.py:420
  59.4 5.0 %all-to-all-done.2 = f32[8,40,128]{2,1,0:T(8,128)S(1)} async-done(((f32[8,40,128]{2,1,0:T(8,128)}), f32[8,40,128]{2,1,0:T(8,128)S(1)}, u32[]{:S(2)}, u32[]{:S(2)}) %all-to-all-start.2) | async-done | bytes 163872 | tf_op jit(solution)/shard_map/all_to_all | solution.py:436
  64.5 1.1 broadcast_in_dim.18
  65.6 3.6 %all-to-all-start.3 = ((f32[8,320,128]{2,1,0:T(8,128)}), f32[8,320,128]{2,1,0:T(8,128)S(1)}, u32[]{:S(2)}, u32[]{:S(2)}) async-start(f32[8,320,128]{2,1,0:T(8,128)} %broadcast_in_dim.18), calls=%async_computation.3 | async-start | bytes 2621440 | tf_op jit(solution)/shard_map/all_to_all | solution.py:436
  69.3 4.5 %class_sums.1.class_ref = f32[4,896,128]{2,1,0:T(8,128)S(1)} custom-call(f32[8,4096]{1,0:T(8,128)S(1)} %pad_maximum_fusion.7.miller_ref, f32[32,4096]{1,0:T(8,128)S(1)} %pad_maximum_fusion.radial_ref), custom_call_target="tpu_custom_call" | custom-call | flops 1879048192 | bytes 655360 | tf_op jit(solution)/shard_map/class_sums/pallas_call | solution.py:172
  73.8 10.8 %all-to-all-done.3 = f32[8,320,128]{2,1,0:T(8,128)S(1)} async-done(((f32[8,320,128]{2,1,0:T(8,128)}), f32[8,320,128]{2,1,0:T(8,128)S(1)}, u32[]{:S(2)}, u32[]{:S(2)}) %all-to-all-start.3) | async-done | bytes 1310752 | tf_op jit(solution)/shard_map/all_to_all | solution.py:436
  84.6 3.6 %feature_rows.1 = (f32[32,4096]{1,0:T(8,128)S(1)}, bf16[608,1152]{1,0:T(8,128)(2,1)S(1)}) custom-call(f32[3,4096]{1,0:T(4,128)S(1)} %copy-done.2, f32[2560,128]{1,0:T(8,128)S(1)} %bitcast.6, f32[4,896,128]{2,1,0:T(8,128)S(1)} %class_sums.1.class_ref), custom_call_target="tpu_custom_call" | custom-call | flops 2709520384 | bytes 2867200 | tf_op jit(solution)/shard_map/feature_rows/pallas_call | solution.py:322
  88.5 5.1 %collective-permute-start.2 = (f32[32,4096]{1,0:T(8,128)S(1)}, f32[32,4096]{1,0:T(8,128)S(1)}, u32[]{:S(2)}, u32[]{:S(2)}) collective-permute-start(f32[32,4096]{1,0:T(8,128)S(1)} %get-tuple-element.21.refs_0_), channel_id=1, source_target_pairs={{0,1},{1,0},{2,3},{3,2},{4,5},{5,4},{6,7},{7,6},{8,9},{9,8},{10,11... | collective-permute-start | bytes 1572872 | tf_op jit(solution)/shard_map/ppermute | solution.py:420
  93.6 4.5 %filter_rows.1 = (f32[32,1024]{1,0:T(8,128)S(1)}, f32[32,1024]{1,0:T(8,128)S(1)}, f32[32,1024]{1,0:T(8,128)S(1)}, f32[32,1024]{1,0:T(8,128)S(1)}) custom-call(f32[8,4096]{1,0:T(8,128)S(1)} %pad_maximum_fusion.7.miller_ref, f32[2560,128]{1,0:T(8,128)S(1)} %bitcast.7), custom_call_target="tpu_custom_call" | custom-call | flops 1879048192 | bytes 655360 | tf_op jit(solution)/shard_map/filter_rows/pallas_call | solution.py:293
  98.2 1.2 %collective-permute-start.3 = (f32[32,1024]{1,0:T(8,128)S(1)}, f32[32,1024]{1,0:T(8,128)S(1)}, u32[]{:S(2)}, u32[]{:S(2)}) collective-permute-start(f32[32,1024]{1,0:T(8,128)S(1)} %get-tuple-element.23), channel_id=1, source_target_pairs={{0,2},{2,0},{1,3},{3,1},{4,6},{6,4},{5,7},{7,5},{8,10},{10,8},{9,1... | collective-permute-start | bytes 393224 | tf_op jit(solution)/shard_map/ppermute | solution.py:420
  99.9 7.9 %position_rows.1 = f32[3,4096]{1,0:T(4,128)S(1)} custom-call(s32[1]{0:T(128)} %bitcast.pick_ref, f32[3,4096]{1,0:T(4,128)S(1)} %copy-done.2, bf16[4096,128]{1,0:T(8,128)(2,1)S(1)} %copy-done, bf16[4096,128]{1,0:T(8,128)(2,1)S(1)} %copy-done.1, bf16[608,1152]{1,0:T(8,128)(2,1)S(1)} %get-tuple-element.27.uv_ref), custom_call_target="tpu_custom_call" | custom-call | flops 5419040768 | bytes 2867200 | tf_op jit(solution)/shard_map/position_rows/pallas_call | solution.py:400
  108.7 1.2 %collective-permute-start.8 = (f32[3,4096]{1,0:T(4,128)S(1)}, f32[3,4096]{1,0:T(4,128)S(1)}, u32[]{:S(2)}, u32[]{:S(2)}) collective-permute-start(f32[3,4096]{1,0:T(4,128)S(1)} %position_rows.1), channel_id=1, source_target_pairs={{0,3},{1,2},{2,1},{3,0},{4,7},{5,6},{6,5},{7,4},{8,11},{9,10},{10,... | collective-permute-start | bytes 147464 | tf_op jit(solution)/shard_map/ppermute | solution.py:424
  110.0 1.1 collective-permute-start.9
  111.1 2.2 %place_rows.1 = (f32[4096,128]{1,0:T(8,128)}, f32[1024,128]{1,0:T(8,128)}) custom-call(s32[1]{0:T(128)} %bitcast.pick_ref, f32[32,4096]{1,0:T(8,128)S(1)} %get-tuple-element.21.refs_0_, f32[32,4096]{1,0:T(8,128)S(1)} %collective-permute-done.2.refs_1_, f32[32,4096]{1,0:T(8,128)S(1)} %collective-permute-done.5.refs_2_, ...), custom_call_target="tpu_custom_call" | custom-call | flops 6000000000 | bytes 4000000 | tf_op jit(solution)/shard_map/place_rows/pallas_call | solution.py:368
  113.3 0.6 collective-permute-done.9
  113.9 0.7 add_add_fusion
  (39 shorter events, 2.7 us)
Async XLA Ops:
  8.1 7.6 %copy-start.3 = (f32[1024,128]{1,0:T(8,128)S(1)}, f32[1024,128]{1,0:T(8,128)}, u32[]{:S(2)}) copy-start(f32[1024,128]{1,0:T(8,128)} %param.9) | copy-start | bytes 1572868
  8.1 7.8 %copy-start.4 = (s32[3,1024]{1,0:T(4,128)S(1)}, s32[3,1024]{1,0:T(4,128)}, u32[]{:S(2)}) copy-start(s32[3,1024]{1,0:T(4,128)} %param.8) | copy-start | bytes 36868
  8.1 26.9 %all-to-all-start = ((f32[8,320,128]{2,1,0:T(8,128)}), f32[8,320,128]{2,1,0:T(8,128)S(1)}, u32[]{:S(2)}, u32[]{:S(2)}) async-start(f32[8,320,128]{2,1,0:T(8,128)} %bitcast.9), calls=%async_computation | async-start | bytes 2621440 | tf_op jit(solution)/shard_map/all_to_all | solution.py:429
  16.1 27.9 %collective-permute-start = (f32[72,1024]{1,0:T(8,128)S(1)}, f32[72,1024]{1,0:T(8,128)S(1)}, u32[]{:S(2)}, u32[]{:S(2)}) collective-permute-start(f32[72,1024]{1,0:T(8,128)S(1)} %pad_maximum_fusion.2), channel_id=1, source_target_pairs={{0,2},{2,0},{1,3},{3,1},{4,6},{6,4},{5,7},{7,5},{8,10},{10,8},{9,1... | collective-permute-start | bytes 884744 | tf_op jit(solution)/shard_map/ppermute | solution.py:420
  35.7 16.5 %all-to-all-start.1 = ((f32[8,40,128]{2,1,0:T(8,128)}), f32[8,40,128]{2,1,0:T(8,128)S(1)}, u32[]{:S(2)}, u32[]{:S(2)}) async-start(f32[8,40,128]{2,1,0:T(8,128)} %bitcast.2), calls=%async_computation.1 | async-start | bytes 327680 | tf_op jit(solution)/shard_map/all_to_all | solution.py:429
  52.9 11.6 %all-to-all-start.2 = ((f32[8,40,128]{2,1,0:T(8,128)}), f32[8,40,128]{2,1,0:T(8,128)S(1)}, u32[]{:S(2)}, u32[]{:S(2)}) async-start(f32[8,40,128]{2,1,0:T(8,128)} %broadcast_in_dim.16), calls=%async_computation.2 | async-start | bytes 327680 | tf_op jit(solution)/shard_map/all_to_all | solution.py:436
  56.3 12.9 %collective-permute-start.1 = (f32[40,2048]{1,0:T(8,128)S(1)}, f32[40,2048]{1,0:T(8,128)S(1)}, u32[]{:S(2)}, u32[]{:S(2)}) collective-permute-start(f32[40,2048]{1,0:T(8,128)S(1)} %pad_maximum_fusion.1), channel_id=1, source_target_pairs={{0,1},{1,0},{2,3},{3,2},{4,5},{5,4},{6,7},{7,6},{8,9},{9,8},{10,11... | collective-permute-start | bytes 983048 | tf_op jit(solution)/shard_map/ppermute | solution.py:420
  65.6 19.0 %all-to-all-start.3 = ((f32[8,320,128]{2,1,0:T(8,128)}), f32[8,320,128]{2,1,0:T(8,128)S(1)}, u32[]{:S(2)}, u32[]{:S(2)}) async-start(f32[8,320,128]{2,1,0:T(8,128)} %broadcast_in_dim.18), calls=%async_computation.3 | async-start | bytes 2621440 | tf_op jit(solution)/shard_map/all_to_all | solution.py:436
  69.3 15.3 %copy-start.2 = (f32[3,4096]{1,0:T(4,128)S(1)}, f32[3,4096]{1,0:T(4,128)}, u32[]{:S(2)}) copy-start(f32[3,4096]{1,0:T(4,128)} %pos_ref.5) | copy-start | bytes 147460
  88.3 11.7 %copy-start = (bf16[4096,128]{1,0:T(8,128)(2,1)S(1)}, bf16[4096,128]{1,0:T(8,128)(2,1)}, u32[]{:S(2)}) copy-start(bf16[4096,128]{1,0:T(8,128)(2,1)} %feat_ref.3) | copy-start | bytes 3145732
  88.3 11.6 %copy-start.1 = (bf16[4096,128]{1,0:T(8,128)(2,1)S(1)}, bf16[4096,128]{1,0:T(8,128)(2,1)}, u32[]{:S(2)}) copy-start(bf16[4096,128]{1,0:T(8,128)(2,1)} %cot_ref.3) | copy-start | bytes 3145732
  88.3 19.6 %collective-permute-start.5 = (f32[32,4096]{1,0:T(8,128)S(1)}, f32[32,4096]{1,0:T(8,128)S(1)}, u32[]{:S(2)}, u32[]{:S(2)}) collective-permute-start(f32[32,4096]{1,0:T(8,128)S(1)} %get-tuple-element.21.refs_0_), channel_id=1, source_target_pairs={{0,2},{2,0},{1,3},{3,1},{4,6},{6,4},{5,7},{7,5},{8,10},{10,8},{9,1... | collective-permute-start | bytes 1572872 | tf_op jit(solution)/shard_map/ppermute | solution.py:420
  88.5 22.6 %collective-permute-start.2 = (f32[32,4096]{1,0:T(8,128)S(1)}, f32[32,4096]{1,0:T(8,128)S(1)}, u32[]{:S(2)}, u32[]{:S(2)}) collective-permute-start(f32[32,4096]{1,0:T(8,128)S(1)} %get-tuple-element.21.refs_0_), channel_id=1, source_target_pairs={{0,1},{1,0},{2,3},{3,2},{4,5},{5,4},{6,7},{7,6},{8,9},{9,8},{10,11... | collective-permute-start | bytes 1572872 | tf_op jit(solution)/shard_map/ppermute | solution.py:420
  98.2 9.6 %collective-permute-start.3 = (f32[32,1024]{1,0:T(8,128)S(1)}, f32[32,1024]{1,0:T(8,128)S(1)}, u32[]{:S(2)}, u32[]{:S(2)}) collective-permute-start(f32[32,1024]{1,0:T(8,128)S(1)} %get-tuple-element.23), channel_id=1, source_target_pairs={{0,2},{2,0},{1,3},{3,1},{4,6},{6,4},{5,7},{7,5},{8,10},{10,8},{9,1... | collective-permute-start | bytes 393224 | tf_op jit(solution)/shard_map/ppermute | solution.py:420
  99.3 8.5 %collective-permute-start.4 = (f32[32,1024]{1,0:T(8,128)S(1)}, f32[32,1024]{1,0:T(8,128)S(1)}, u32[]{:S(2)}, u32[]{:S(2)}) collective-permute-start(f32[32,1024]{1,0:T(8,128)S(1)} %get-tuple-element.24), channel_id=1, source_target_pairs={{0,3},{1,2},{2,1},{3,0},{4,7},{5,6},{6,5},{7,4},{8,11},{9,10},{10,... | collective-permute-start | bytes 393224 | tf_op jit(solution)/shard_map/ppermute | solution.py:424
  107.8 3.3 %collective-permute-start.6 = (f32[32,4096]{1,0:T(8,128)S(1)}, f32[32,4096]{1,0:T(8,128)S(1)}, u32[]{:S(2)}, u32[]{:S(2)}) collective-permute-start(f32[32,4096]{1,0:T(8,128)S(1)} %collective-permute-done.5.refs_2_), channel_id=1, source_target_pairs={{0,1},{1,0},{2,3},{3,2},{4,5},{5,4},{6,7},{7,6},{8,9},{9,8},{10,11... | collective-permute-start | bytes 1572872 | tf_op jit(solution)/shard_map/ppermute | solution.py:420
  108.2 1.9 %collective-permute-start.7 = (f32[32,1024]{1,0:T(8,128)S(1)}, f32[32,1024]{1,0:T(8,128)S(1)}, u32[]{:S(2)}, u32[]{:S(2)}) collective-permute-start(f32[32,1024]{1,0:T(8,128)S(1)} %get-tuple-element.29), channel_id=1, source_target_pairs={{0,1},{1,0},{2,3},{3,2},{4,5},{5,4},{6,7},{7,6},{8,9},{9,8},{10,11... | collective-permute-start | bytes 393224 | tf_op jit(solution)/shard_map/ppermute | solution.py:420
  108.4 4.9 %collective-permute-start.10 = (f32[3,4096]{1,0:T(4,128)S(1)}, f32[3,4096]{1,0:T(4,128)S(1)}, u32[]{:S(2)}, u32[]{:S(2)}) collective-permute-start(f32[3,4096]{1,0:T(4,128)S(1)} %position_rows.1), channel_id=1, source_target_pairs={{0,1},{1,0},{2,3},{3,2},{4,5},{5,4},{6,7},{7,6},{8,9},{9,8},{10,11... | collective-permute-start | bytes 147464 | tf_op jit(solution)/shard_map/ppermute | solution.py:420
  108.7 4.7 %collective-permute-start.8 = (f32[3,4096]{1,0:T(4,128)S(1)}, f32[3,4096]{1,0:T(4,128)S(1)}, u32[]{:S(2)}, u32[]{:S(2)}) collective-permute-start(f32[3,4096]{1,0:T(4,128)S(1)} %position_rows.1), channel_id=1, source_target_pairs={{0,3},{1,2},{2,1},{3,0},{4,7},{5,6},{6,5},{7,4},{8,11},{9,10},{10,... | collective-permute-start | bytes 147464 | tf_op jit(solution)/shard_map/ppermute | solution.py:424
  110.0 3.9 %collective-permute-start.9 = (f32[3,4096]{1,0:T(4,128)S(1)}, f32[3,4096]{1,0:T(4,128)S(1)}, u32[]{:S(2)}, u32[]{:S(2)}) collective-permute-start(f32[3,4096]{1,0:T(4,128)S(1)} %position_rows.1), channel_id=1, source_target_pairs={{0,2},{2,0},{1,3},{3,1},{4,6},{6,4},{5,7},{7,5},{8,10},{10,8},{9,1... | collective-permute-start | bytes 147464 | tf_op jit(solution)/shard_map/ppermute | solution.py:420

commit v5 on v4

--- a/solution.py
+++ b/solution.py
@@ -240,7 +240,7 @@
 
 def pair_products(total_ref, pair_ref):
     _, half = lane_signs()
-    pair_ref[...] = jnp.zeros((CLASSES, 128), f32)
+    pair_ref[:, 88 * TILES :, :] = jnp.zeros((4, CLASSES - 88 * TILES, 128), f32)
     for t in range(TILES):
         a = load_tile(total_ref, t)
         b = half * pltpu.roll(a, 64, 1)
@@ -256,11 +256,8 @@
             [sc * tcc + ss * tcs - cc * tsc - cs * tss, zero, e1s * te1c - e1c * te1s, zero],
             [cs * tcc + ss * tsc - cc * tcs - sc * tss, e2s * te2c - e2c * te2s, zero, zero],
         ]
-        parts = []
         for q in range(4):
-            z = jnp.concatenate(y[q], 0)
-            parts.append(z[:, 32:64] + z[:, 96:128])
-        pair_ref[88 * t : 88 * t + 88, :] = jnp.concatenate(parts, 1)
+            pair_ref[q, 88 * t : 88 * t + 88, :] = jnp.concatenate(y[q], 0)
 
 
 def filter_kernel(scale, miller_ref, total_ref, *refs):
@@ -270,7 +267,11 @@
     @pl.when(step == 0)
     def _():
         pair_products(total_ref, pair_ref)
-        turned_ref[...] = pair_ref[...].T.astype(bf16)
+        lane = lax.broadcasted_iota(jnp.int32, (32, 128), 1)
+        row = lax.broadcasted_iota(jnp.int32, (32, 128), 0)
+        pick = jnp.logical_or(lane == row + 32, lane == row + 96).astype(bf16)
+        for q in range(4):
+            turned_ref[32 * q : 32 * q + 32, :] = nt_dot(pick, pair_ref[q].astype(bf16)).astype(bf16)
 
     index, products = wave_class(miller_ref[0:3, :])
     hot = (lax.broadcasted_iota(jnp.int32, (CLASSES, index.shape[1]), 0) == index).astype(f32).astype(bf16)
@@ -296,7 +297,7 @@
         in_specs=[pl.BlockSpec((8, block), lambda i: (0, i)), pl.BlockSpec((PACKED, 128), lambda i: (0, 0))],
         out_specs=(pl.BlockSpec((32, block), lambda i: (0, 0)),) * 4,
         out_shape=(one,) * 4,
-        scratch_shapes=[pltpu.VMEM((CLASSES, 128), f32), pltpu.VMEM((128, CLASSES), bf16)],
+        scratch_shapes=[pltpu.VMEM((4, CLASSES, 128), f32), pltpu.VMEM((128, CLASSES), bf16)],
         compiler_params=pltpu.CompilerParams(vmem_limit_bytes=18 * MIB),
         cost_estimate=pl.CostEstimate(flops=2 * CLASSES * 1024 * block, bytes_accessed=block * 640, transcendentals=0),
         name="filter_rows",

time: 115 us -> 115 us (level)
  waiting for transfers between devices: 43.2 us -> 45.9 us
  starting transfers between devices: 36.6 us -> 34.8 us
  Pallas kernels: 30.3 us -> 29.1 us
    ppermute x9, waiting for transfers between devices: 0.72 us -> 2.09 us  [swap(): return lax.ppermute(value, axis, [(0, 1), (1, 0)])]
    ppermute x2, waiting for transfers between devices: 0.01 us -> 1.29 us  [swap_both(): return lax.ppermute(value, ('yl', 'core'), [(i, 3 - i) for i in range(4)])]
    pallas_call x1, Pallas kernels: 4.54 us -> 3.36 us  [filter_rows(): pl.pallas_call(functools.partial(filter_kernel, scale), grid=(4,), in_spe...]
  transfers between devices with their start and end apart: 15 -> 15, of which waited for: 6 -> 8; matrix products, arithmetic and copies ran while one was open for 2% -> 2% of each run, Pallas kernels for 17% -> 16%
where the time goes in v5:
time: 115 us; the launch traced here: 114 us
  waiting for transfers between devices  45.9 us (40%)
  starting transfers between devices  34.8 us (30%)
  Pallas kernels  29.1 us (25%)
  local copies, waits for them, and re-layouts  2.07 us (2%)
  other arithmetic  1.62 us (1%)
    all_to_all x2, waiting for transfers between devices, sum_scatter(): lax.all_to_all(value.reshape(n, value.shape[0] // n, 128), axis, 0, 0)  26.7 us
    all_to_all x2, waiting for transfers between devices, gather(): return lax.all_to_all(copies, axis, 0, 0).reshape(n * value.shape[0], 128)  15.8 us
    all_to_all x2, starting transfers between devices, sum_scatter(): lax.all_to_all(value.reshape(n, value.shape[0] // n, 128), axis, 0, 0)  15.8 us
    ppermute x9, starting transfers between devices, swap(): return lax.ppermute(value, axis, [(0, 1), (1, 0)])  10.9 us
    pallas_call x1, Pallas kernels, position_rows(): pl.pallas_call(position_kernel, grid=(atoms // block,), in_specs=[pl.Bloc...  7.89 us
    pallas_call x1, Pallas kernels, factors(): pl.pallas_call(factor_kernel, grid=(atoms // block,), in_specs=[pl.BlockS...  7.47 us
    all_to_all x2, starting transfers between devices, gather(): return lax.all_to_all(copies, axis, 0, 0).reshape(n * value.shape[0], 128)  6.95 us
    pallas_call x1, Pallas kernels, class_sums(): pl.pallas_call(functools.partial(class_kernel, scale), grid=(waves // blo...  4.51 us
  transfers between devices with their start and end apart: 15, of which 8 were waited for; matrix products, arithmetic and copies ran while one was open for 2% of the time, Pallas kernels for 16%

profile of v5, /device:TPU:1, one launch (start us, length us, event | category | flops | bytes accessed | tf_op | source)
XLA Modules:
  0.0 114.3 jit_solution(25410399172494506)
XLA Ops:
  0.6 7.5 %factors.1 = f32[2560,128]{1,0:T(8,128)} custom-call(s32[1]{0:T(128)} %bitcast.pick_ref, f32[3,4096]{1,0:T(4,128)} %pos_ref.5, bf16[4096,128]{1,0:T(8,128)(2,1)} %feat_ref.3, bf16[4096,128]{1,0:T(8,128)(2,1)} %cot_ref.3), custom_call_target="tpu_custom_call" | custom-call | flops 2709520384 | bytes 2129920 | tf_op jit(solution)/shard_map/factors/pallas_call | solution.py:107
  8.1 7.6 %all-to-all-start = ((f32[8,320,128]{2,1,0:T(8,128)}), f32[8,320,128]{2,1,0:T(8,128)S(1)}, u32[]{:S(2)}, u32[]{:S(2)}) async-start(f32[8,320,128]{2,1,0:T(8,128)} %bitcast.9), calls=%async_computation | async-start | bytes 2621440 | tf_op jit(solution)/shard_map/all_to_all | solution.py:430
  16.5 18.4 %all-to-all-done = f32[8,320,128]{2,1,0:T(8,128)S(1)} async-done(((f32[8,320,128]{2,1,0:T(8,128)}), f32[8,320,128]{2,1,0:T(8,128)S(1)}, u32[]{:S(2)}, u32[]{:S(2)}) %all-to-all-start) | async-done | bytes 1310752 | tf_op jit(solution)/shard_map/all_to_all | solution.py:430
  35.0 0.7 reduce_sum.18
  35.7 8.2 %all-to-all-start.1 = ((f32[8,40,128]{2,1,0:T(8,128)}), f32[8,40,128]{2,1,0:T(8,128)S(1)}, u32[]{:S(2)}, u32[]{:S(2)}) async-start(f32[8,40,128]{2,1,0:T(8,128)} %bitcast.2), calls=%async_computation.1 | async-start | bytes 327680 | tf_op jit(solution)/shard_map/all_to_all | solution.py:430
  44.0 8.2 %all-to-all-done.1 = f32[8,40,128]{2,1,0:T(8,128)S(1)} async-done(((f32[8,40,128]{2,1,0:T(8,128)}), f32[8,40,128]{2,1,0:T(8,128)S(1)}, u32[]{:S(2)}, u32[]{:S(2)}) %all-to-all-start.1) | async-done | bytes 163872 | tf_op jit(solution)/shard_map/all_to_all | solution.py:430
  52.2 0.7 broadcast_in_dim.16
  52.9 3.4 %all-to-all-start.2 = ((f32[8,40,128]{2,1,0:T(8,128)}), f32[8,40,128]{2,1,0:T(8,128)S(1)}, u32[]{:S(2)}, u32[]{:S(2)}) async-start(f32[8,40,128]{2,1,0:T(8,128)} %broadcast_in_dim.16), calls=%async_computation.2 | async-start | bytes 327680 | tf_op jit(solution)/shard_map/all_to_all | solution.py:437
  56.3 3.1 %collective-permute-start.1 = (f32[40,2048]{1,0:T(8,128)S(1)}, f32[40,2048]{1,0:T(8,128)S(1)}, u32[]{:S(2)}, u32[]{:S(2)}) collective-permute-start(f32[40,2048]{1,0:T(8,128)S(1)} %pad_maximum_fusion.1), channel_id=1, source_target_pairs={{0,1},{1,0},{2,3},{3,2},{4,5},{5,4},{6,7},{7,6},{8,9},{9,8},{10,11... | collective-permute-start | bytes 983048 | tf_op jit(solution)/shard_map/ppermute | solution.py:421
  59.4 5.0 %all-to-all-done.2 = f32[8,40,128]{2,1,0:T(8,128)S(1)} async-done(((f32[8,40,128]{2,1,0:T(8,128)}), f32[8,40,128]{2,1,0:T(8,128)S(1)}, u32[]{:S(2)}, u32[]{:S(2)}) %all-to-all-start.2) | async-done | bytes 163872 | tf_op jit(solution)/shard_map/all_to_all | solution.py:437
  64.5 1.1 broadcast_in_dim.18
  65.6 3.6 %all-to-all-start.3 = ((f32[8,320,128]{2,1,0:T(8,128)}), f32[8,320,128]{2,1,0:T(8,128)S(1)}, u32[]{:S(2)}, u32[]{:S(2)}) async-start(f32[8,320,128]{2,1,0:T(8,128)} %broadcast_in_dim.18), calls=%async_computation.3 | async-start | bytes 2621440 | tf_op jit(solution)/shard_map/all_to_all | solution.py:437
  69.3 4.5 %class_sums.1.class_ref = f32[4,896,128]{2,1,0:T(8,128)S(1)} custom-call(f32[8,4096]{1,0:T(8,128)S(1)} %pad_maximum_fusion.7.miller_ref, f32[32,4096]{1,0:T(8,128)S(1)} %pad_maximum_fusion.radial_ref), custom_call_target="tpu_custom_call" | custom-call | flops 1879048192 | bytes 655360 | tf_op jit(solution)/shard_map/class_sums/pallas_call | solution.py:172
  73.8 10.8 %all-to-all-done.3 = f32[8,320,128]{2,1,0:T(8,128)S(1)} async-done(((f32[8,320,128]{2,1,0:T(8,128)}), f32[8,320,128]{2,1,0:T(8,128)S(1)}, u32[]{:S(2)}, u32[]{:S(2)}) %all-to-all-start.3) | async-done | bytes 1310752 | tf_op jit(solution)/shard_map/all_to_all | solution.py:437
  84.6 3.6 %feature_rows.1 = (f32[32,4096]{1,0:T(8,128)S(1)}, bf16[608,1152]{1,0:T(8,128)(2,1)S(1)}) custom-call(f32[3,4096]{1,0:T(4,128)S(1)} %copy-done.2, f32[2560,128]{1,0:T(8,128)S(1)} %bitcast.6, f32[4,896,128]{2,1,0:T(8,128)S(1)} %class_sums.1.class_ref), custom_call_target="tpu_custom_call" | custom-call | flops 2709520384 | bytes 2867200 | tf_op jit(solution)/shard_map/feature_rows/pallas_call | solution.py:323
  88.5 5.1 %collective-permute-start.2 = (f32[32,4096]{1,0:T(8,128)S(1)}, f32[32,4096]{1,0:T(8,128)S(1)}, u32[]{:S(2)}, u32[]{:S(2)}) collective-permute-start(f32[32,4096]{1,0:T(8,128)S(1)} %get-tuple-element.21.refs_0_), channel_id=1, source_target_pairs={{0,1},{1,0},{2,3},{3,2},{4,5},{5,4},{6,7},{7,6},{8,9},{9,8},{10,11... | collective-permute-start | bytes 1572872 | tf_op jit(solution)/shard_map/ppermute | solution.py:421
  93.6 3.4 %filter_rows.1 = (f32[32,1024]{1,0:T(8,128)S(1)}, f32[32,1024]{1,0:T(8,128)S(1)}, f32[32,1024]{1,0:T(8,128)S(1)}, f32[32,1024]{1,0:T(8,128)S(1)}) custom-call(f32[8,4096]{1,0:T(8,128)S(1)} %pad_maximum_fusion.7.miller_ref, f32[2560,128]{1,0:T(8,128)S(1)} %bitcast.7), custom_call_target="tpu_custom_call" | custom-call | flops 1879048192 | bytes 655360 | tf_op jit(solution)/shard_map/filter_rows/pallas_call | solution.py:294
  97.0 1.2 %collective-permute-start.3 = (f32[32,1024]{1,0:T(8,128)S(1)}, f32[32,1024]{1,0:T(8,128)S(1)}, u32[]{:S(2)}, u32[]{:S(2)}) collective-permute-start(f32[32,1024]{1,0:T(8,128)S(1)} %get-tuple-element.23), channel_id=1, source_target_pairs={{0,2},{2,0},{1,3},{3,1},{4,6},{6,4},{5,7},{7,5},{8,10},{10,8},{9,1... | collective-permute-start | bytes 393224 | tf_op jit(solution)/shard_map/ppermute | solution.py:421
  98.7 7.9 %position_rows.1 = f32[3,4096]{1,0:T(4,128)S(1)} custom-call(s32[1]{0:T(128)} %bitcast.pick_ref, f32[3,4096]{1,0:T(4,128)S(1)} %copy-done.2, bf16[4096,128]{1,0:T(8,128)(2,1)S(1)} %copy-done, bf16[4096,128]{1,0:T(8,128)(2,1)S(1)} %copy-done.1, bf16[608,1152]{1,0:T(8,128)(2,1)S(1)} %get-tuple-element.27.uv_ref), custom_call_target="tpu_custom_call" | custom-call | flops 5419040768 | bytes 2867200 | tf_op jit(solution)/shard_map/position_rows/pallas_call | solution.py:401
  106.6 1.0 collective-permute-done.4.refs_7_
  108.7 1.0 collective-permute-done.7.refs_5_
  110.0 2.2 %place_rows.1 = (f32[4096,128]{1,0:T(8,128)}, f32[1024,128]{1,0:T(8,128)}) custom-call(s32[1]{0:T(128)} %bitcast.pick_ref, f32[32,4096]{1,0:T(8,128)S(1)} %get-tuple-element.21.refs_0_, f32[32,4096]{1,0:T(8,128)S(1)} %collective-permute-done.2.refs_1_, f32[32,4096]{1,0:T(8,128)S(1)} %collective-permute-done.5.refs_2_, ...), custom_call_target="tpu_custom_call" | custom-call | flops 6000000000 | bytes 4000000 | tf_op jit(solution)/shard_map/place_rows/pallas_call | solution.py:369
  112.6 1.1 collective-permute-done.9
  113.6 0.7 add_add_fusion
  (39 shorter events, 3.4 us)
Async XLA Ops:
  8.1 7.6 %copy-start.3 = (f32[1024,128]{1,0:T(8,128)S(1)}, f32[1024,128]{1,0:T(8,128)}, u32[]{:S(2)}) copy-start(f32[1024,128]{1,0:T(8,128)} %param.9) | copy-start | bytes 1572868
  8.1 7.8 %copy-start.4 = (s32[3,1024]{1,0:T(4,128)S(1)}, s32[3,1024]{1,0:T(4,128)}, u32[]{:S(2)}) copy-start(s32[3,1024]{1,0:T(4,128)} %param.8) | copy-start | bytes 36868
  8.1 26.9 %all-to-all-start = ((f32[8,320,128]{2,1,0:T(8,128)}), f32[8,320,128]{2,1,0:T(8,128)S(1)}, u32[]{:S(2)}, u32[]{:S(2)}) async-start(f32[8,320,128]{2,1,0:T(8,128)} %bitcast.9), calls=%async_computation | async-start | bytes 2621440 | tf_op jit(solution)/shard_map/all_to_all | solution.py:430
  16.1 27.9 %collective-permute-start = (f32[72,1024]{1,0:T(8,128)S(1)}, f32[72,1024]{1,0:T(8,128)S(1)}, u32[]{:S(2)}, u32[]{:S(2)}) collective-permute-start(f32[72,1024]{1,0:T(8,128)S(1)} %pad_maximum_fusion.2), channel_id=1, source_target_pairs={{0,2},{2,0},{1,3},{3,1},{4,6},{6,4},{5,7},{7,5},{8,10},{10,8},{9,1... | collective-permute-start | bytes 884744 | tf_op jit(solution)/shard_map/ppermute | solution.py:421
  35.7 16.5 %all-to-all-start.1 = ((f32[8,40,128]{2,1,0:T(8,128)}), f32[8,40,128]{2,1,0:T(8,128)S(1)}, u32[]{:S(2)}, u32[]{:S(2)}) async-start(f32[8,40,128]{2,1,0:T(8,128)} %bitcast.2), calls=%async_computation.1 | async-start | bytes 327680 | tf_op jit(solution)/shard_map/all_to_all | solution.py:430
  52.9 11.6 %all-to-all-start.2 = ((f32[8,40,128]{2,1,0:T(8,128)}), f32[8,40,128]{2,1,0:T(8,128)S(1)}, u32[]{:S(2)}, u32[]{:S(2)}) async-start(f32[8,40,128]{2,1,0:T(8,128)} %broadcast_in_dim.16), calls=%async_computation.2 | async-start | bytes 327680 | tf_op jit(solution)/shard_map/all_to_all | solution.py:437
  56.3 12.9 %collective-permute-start.1 = (f32[40,2048]{1,0:T(8,128)S(1)}, f32[40,2048]{1,0:T(8,128)S(1)}, u32[]{:S(2)}, u32[]{:S(2)}) collective-permute-start(f32[40,2048]{1,0:T(8,128)S(1)} %pad_maximum_fusion.1), channel_id=1, source_target_pairs={{0,1},{1,0},{2,3},{3,2},{4,5},{5,4},{6,7},{7,6},{8,9},{9,8},{10,11... | collective-permute-start | bytes 983048 | tf_op jit(solution)/shard_map/ppermute | solution.py:421
  65.6 19.0 %all-to-all-start.3 = ((f32[8,320,128]{2,1,0:T(8,128)}), f32[8,320,128]{2,1,0:T(8,128)S(1)}, u32[]{:S(2)}, u32[]{:S(2)}) async-start(f32[8,320,128]{2,1,0:T(8,128)} %broadcast_in_dim.18), calls=%async_computation.3 | async-start | bytes 2621440 | tf_op jit(solution)/shard_map/all_to_all | solution.py:437
  69.3 15.3 %copy-start.2 = (f32[3,4096]{1,0:T(4,128)S(1)}, f32[3,4096]{1,0:T(4,128)}, u32[]{:S(2)}) copy-start(f32[3,4096]{1,0:T(4,128)} %pos_ref.5) | copy-start | bytes 147460
  88.3 10.5 %copy-start = (bf16[4096,128]{1,0:T(8,128)(2,1)S(1)}, bf16[4096,128]{1,0:T(8,128)(2,1)}, u32[]{:S(2)}) copy-start(bf16[4096,128]{1,0:T(8,128)(2,1)} %feat_ref.3) | copy-start | bytes 3145732
  88.3 10.5 %copy-start.1 = (bf16[4096,128]{1,0:T(8,128)(2,1)S(1)}, bf16[4096,128]{1,0:T(8,128)(2,1)}, u32[]{:S(2)}) copy-start(bf16[4096,128]{1,0:T(8,128)(2,1)} %cot_ref.3) | copy-start | bytes 3145732
  88.3 19.4 %collective-permute-start.5 = (f32[32,4096]{1,0:T(8,128)S(1)}, f32[32,4096]{1,0:T(8,128)S(1)}, u32[]{:S(2)}, u32[]{:S(2)}) collective-permute-start(f32[32,4096]{1,0:T(8,128)S(1)} %get-tuple-element.21.refs_0_), channel_id=1, source_target_pairs={{0,2},{2,0},{1,3},{3,1},{4,6},{6,4},{5,7},{7,5},{8,10},{10,8},{9,1... | collective-permute-start | bytes 1572872 | tf_op jit(solution)/shard_map/ppermute | solution.py:421
  88.5 21.5 %collective-permute-start.2 = (f32[32,4096]{1,0:T(8,128)S(1)}, f32[32,4096]{1,0:T(8,128)S(1)}, u32[]{:S(2)}, u32[]{:S(2)}) collective-permute-start(f32[32,4096]{1,0:T(8,128)S(1)} %get-tuple-element.21.refs_0_), channel_id=1, source_target_pairs={{0,1},{1,0},{2,3},{3,2},{4,5},{5,4},{6,7},{7,6},{8,9},{9,8},{10,11... | collective-permute-start | bytes 1572872 | tf_op jit(solution)/shard_map/ppermute | solution.py:421
  97.0 9.6 %collective-permute-start.3 = (f32[32,1024]{1,0:T(8,128)S(1)}, f32[32,1024]{1,0:T(8,128)S(1)}, u32[]{:S(2)}, u32[]{:S(2)}) collective-permute-start(f32[32,1024]{1,0:T(8,128)S(1)} %get-tuple-element.23), channel_id=1, source_target_pairs={{0,2},{2,0},{1,3},{3,1},{4,6},{6,4},{5,7},{7,5},{8,10},{10,8},{9,1... | collective-permute-start | bytes 393224 | tf_op jit(solution)/shard_map/ppermute | solution.py:421
  98.2 9.5 %collective-permute-start.4 = (f32[32,1024]{1,0:T(8,128)S(1)}, f32[32,1024]{1,0:T(8,128)S(1)}, u32[]{:S(2)}, u32[]{:S(2)}) collective-permute-start(f32[32,1024]{1,0:T(8,128)S(1)} %get-tuple-element.24), channel_id=1, source_target_pairs={{0,3},{1,2},{2,1},{3,0},{4,7},{5,6},{6,5},{7,4},{8,11},{9,10},{10,... | collective-permute-start | bytes 393224 | tf_op jit(solution)/shard_map/ppermute | solution.py:425
  107.6 2.4 %collective-permute-start.6 = (f32[32,4096]{1,0:T(8,128)S(1)}, f32[32,4096]{1,0:T(8,128)S(1)}, u32[]{:S(2)}, u32[]{:S(2)}) collective-permute-start(f32[32,4096]{1,0:T(8,128)S(1)} %collective-permute-done.5.refs_2_), channel_id=1, source_target_pairs={{0,1},{1,0},{2,3},{3,2},{4,5},{5,4},{6,7},{7,6},{8,9},{9,8},{10,11... | collective-permute-start | bytes 1572872 | tf_op jit(solution)/shard_map/ppermute | solution.py:421
  107.6 2.1 %collective-permute-start.7 = (f32[32,1024]{1,0:T(8,128)S(1)}, f32[32,1024]{1,0:T(8,128)S(1)}, u32[]{:S(2)}, u32[]{:S(2)}) collective-permute-start(f32[32,1024]{1,0:T(8,128)S(1)} %get-tuple-element.29), channel_id=1, source_target_pairs={{0,1},{1,0},{2,3},{3,2},{4,5},{5,4},{6,7},{7,6},{8,9},{9,8},{10,11... | collective-permute-start | bytes 393224 | tf_op jit(solution)/shard_map/ppermute | solution.py:421
  108.2 4.1 %collective-permute-start.10 = (f32[3,4096]{1,0:T(4,128)S(1)}, f32[3,4096]{1,0:T(4,128)S(1)}, u32[]{:S(2)}, u32[]{:S(2)}) collective-permute-start(f32[3,4096]{1,0:T(4,128)S(1)} %position_rows.1), channel_id=1, source_target_pairs={{0,1},{1,0},{2,3},{3,2},{4,5},{5,4},{6,7},{7,6},{8,9},{9,8},{10,11... | collective-permute-start | bytes 147464 | tf_op jit(solution)/shard_map/ppermute | solution.py:421
  108.2 4.4 %collective-permute-start.8 = (f32[3,4096]{1,0:T(4,128)S(1)}, f32[3,4096]{1,0:T(4,128)S(1)}, u32[]{:S(2)}, u32[]{:S(2)}) collective-permute-start(f32[3,4096]{1,0:T(4,128)S(1)} %position_rows.1), channel_id=1, source_target_pairs={{0,3},{1,2},{2,1},{3,0},{4,7},{5,6},{6,5},{7,4},{8,11},{9,10},{10,... | collective-permute-start | bytes 147464 | tf_op jit(solution)/shard_map/ppermute | solution.py:425
  109.7 3.9 %collective-permute-start.9 = (f32[3,4096]{1,0:T(4,128)S(1)}, f32[3,4096]{1,0:T(4,128)S(1)}, u32[]{:S(2)}, u32[]{:S(2)}) collective-permute-start(f32[3,4096]{1,0:T(4,128)S(1)} %position_rows.1), channel_id=1, source_target_pairs={{0,2},{2,0},{1,3},{3,1},{4,6},{6,4},{5,7},{7,5},{8,10},{10,8},{9,1... | collective-permute-start | bytes 147464 | tf_op jit(solution)/shard_map/ppermute | solution.py:421

commit v6 on v5

--- a/solution.py
+++ b/solution.py
@@ -431,6 +431,24 @@
     return jnp.sum(parts, 0)
 
 
+def total_kernel(parts_ref, out_ref):
+    total = jnp.sum(parts_ref[...], 0)
+    for k in range(out_ref.shape[0]):
+        out_ref[k] = total
+
+
+def sum_everywhere(value, axis):
+    n = lax.axis_size(axis)
+    parts = lax.all_to_all(value.reshape(n, value.shape[0] // n, 128), axis, 0, 0)
+    copies = pl.pallas_call(
+        total_kernel,
+        out_shape=jax.ShapeDtypeStruct(parts.shape, f32),
+        compiler_params=pltpu.CompilerParams(vmem_limit_bytes=4 * MIB),
+        name="total_rows",
+    )(parts)
+    return lax.all_to_all(copies, axis, 0, 0).reshape(value.shape)
+
+
 def gather(value, axis):
     n = lax.axis_size(axis)
     copies = jnp.broadcast_to(value[None], (n,) + value.shape)
@@ -464,8 +482,7 @@
 
     part = factors(pick, positions, features, cotangent, min(block, atoms // 2), 1)
     part = sum_scatter(part, ("x", "yh"))
-    part = sum_scatter(part, "z")
-    part = gather(part, "z")
+    part = sum_everywhere(part, "z")
     total = gather(part, ("x", "yh"))
     grad, uv = feature_rows(positions, total, classes, atoms)
     grad_y, grad_core = swap(grad, "yl"), swap(grad, "core")

time: 115 us -> 115 us (level)
    all_to_all x0 -> x2, waiting for transfers between devices: none -> 13.3 us  [the longest x1 8.23 us: sum_everywhere(): lax.all_to_all(value.reshape(n, value.shape[0] // n, 128), axis, 0, 0)]
    all_to_all x0 -> x2, starting transfers between devices: none -> 11.6 us  [the longest x1 8.18 us: sum_everywhere(): lax.all_to_all(value.reshape(n, value.shape[0] // n, 128), axis, 0, 0)]
    all_to_all x2 -> x1, waiting for transfers between devices: 26.7 us -> 18.4 us  [sum_scatter(): lax.all_to_all(value.reshape(n, value.shape[0] // n, 128), axis, 0, 0)]
    all_to_all x2 -> x1, starting transfers between devices: 15.8 us -> 7.61 us  [sum_scatter(): lax.all_to_all(value.reshape(n, value.shape[0] // n, 128), axis, 0, 0)]
    all_to_all x2 -> x1, waiting for transfers between devices: 15.8 us -> 10.8 us  [gather(): return lax.all_to_all(copies, axis, 0, 0).reshape(n * value.shape[0], 128)]
    all_to_all x2 -> x1, starting transfers between devices: 6.95 us -> 3.57 us  [gather(): return lax.all_to_all(copies, axis, 0, 0).reshape(n * value.shape[0], 128)]
where the time goes in v6:
time: 115 us; the launch traced here: 114 us
  waiting for transfers between devices  45.9 us (40%)
  starting transfers between devices  34.8 us (30%)
  Pallas kernels  29.8 us (26%)
  other arithmetic  1.6 us (1%)
  local copies, waits for them, and re-layouts  1.39 us (1%)
    all_to_all x1, waiting for transfers between devices, sum_scatter(): lax.all_to_all(value.reshape(n, value.shape[0] // n, 128), axis, 0, 0)  18.4 us
    ppermute x9, starting transfers between devices, swap(): return lax.ppermute(value, axis, [(0, 1), (1, 0)])  10.9 us
    all_to_all x1, waiting for transfers between devices, gather(): return lax.all_to_all(copies, axis, 0, 0).reshape(n * value.shape[0], 128)  10.8 us
    all_to_all x1, waiting for transfers between devices, sum_everywhere(): lax.all_to_all(value.reshape(n, value.shape[0] // n, 128), axis, 0, 0)  8.23 us
    all_to_all x1, starting transfers between devices, sum_everywhere(): lax.all_to_all(value.reshape(n, value.shape[0] // n, 128), axis, 0, 0)  8.18 us
    pallas_call x1, Pallas kernels, position_rows(): pl.pallas_call(position_kernel, grid=(atoms // block,), in_specs=[pl.Bloc...  7.89 us
    all_to_all x1, starting transfers between devices, sum_scatter(): lax.all_to_all(value.reshape(n, value.shape[0] // n, 128), axis, 0, 0)  7.61 us
    pallas_call x1, Pallas kernels, factors(): pl.pallas_call(factor_kernel, grid=(atoms // block,), in_specs=[pl.BlockS...  7.47 us
  transfers between devices with their start and end apart: 15, of which 8 were waited for; matrix products, arithmetic and copies ran while one was open for 2% of the time, Pallas kernels for 16%

profile of v6, /device:TPU:1, one launch (start us, length us, event | category | flops | bytes accessed | tf_op | source)
XLA Modules:
  0.0 114.3 jit_solution(14730815327958316578)
XLA Ops:
  0.6 7.5 %factors.1 = f32[2560,128]{1,0:T(8,128)} custom-call(s32[1]{0:T(128)} %bitcast.pick_ref, f32[3,4096]{1,0:T(4,128)} %pos_ref.5, bf16[4096,128]{1,0:T(8,128)(2,1)} %feat_ref.3, bf16[4096,128]{1,0:T(8,128)(2,1)} %cot_ref.3), custom_call_target="tpu_custom_call" | custom-call | flops 2709520384 | bytes 2129920 | tf_op jit(solution)/shard_map/factors/pallas_call | solution.py:107
  8.1 7.6 %all-to-all-start = ((f32[8,320,128]{2,1,0:T(8,128)}), f32[8,320,128]{2,1,0:T(8,128)S(1)}, u32[]{:S(2)}, u32[]{:S(2)}) async-start(f32[8,320,128]{2,1,0:T(8,128)} %bitcast.9), calls=%async_computation | async-start | bytes 2621440 | tf_op jit(solution)/shard_map/all_to_all | solution.py:430
  16.5 18.4 %all-to-all-done = f32[8,320,128]{2,1,0:T(8,128)S(1)} async-done(((f32[8,320,128]{2,1,0:T(8,128)}), f32[8,320,128]{2,1,0:T(8,128)S(1)}, u32[]{:S(2)}, u32[]{:S(2)}) %all-to-all-start) | async-done | bytes 1310752 | tf_op jit(solution)/shard_map/all_to_all | solution.py:430
  35.0 0.7 reduce_sum.9
  35.7 8.2 %all-to-all-start.1 = ((f32[8,40,128]{2,1,0:T(8,128)}), f32[8,40,128]{2,1,0:T(8,128)S(1)}, u32[]{:S(2)}, u32[]{:S(2)}) async-start(f32[8,40,128]{2,1,0:T(8,128)} %bitcast.2), calls=%async_computation.1 | async-start | bytes 327680 | tf_op jit(solution)/shard_map/all_to_all | solution.py:442
  44.0 8.2 %all-to-all-done.1.parts_ref = f32[8,40,128]{2,1,0:T(8,128)S(1)} async-done(((f32[8,40,128]{2,1,0:T(8,128)}), f32[8,40,128]{2,1,0:T(8,128)S(1)}, u32[]{:S(2)}, u32[]{:S(2)}) %all-to-all-start.1) | async-done | bytes 163872 | tf_op jit(solution)/shard_map/all_to_all | solution.py:442
  52.2 0.7 total_rows.1
  52.9 3.4 %all-to-all-start.2 = ((f32[8,40,128]{2,1,0:T(8,128)}), f32[8,40,128]{2,1,0:T(8,128)S(1)}, u32[]{:S(2)}, u32[]{:S(2)}) async-start(f32[8,40,128]{2,1,0:T(8,128)} %total_rows.1), calls=%async_computation.2 | async-start | bytes 327680 | tf_op jit(solution)/shard_map/all_to_all | solution.py:449
  56.3 3.1 %collective-permute-start.1 = (f32[40,2048]{1,0:T(8,128)S(1)}, f32[40,2048]{1,0:T(8,128)S(1)}, u32[]{:S(2)}, u32[]{:S(2)}) collective-permute-start(f32[40,2048]{1,0:T(8,128)S(1)} %pad_maximum_fusion.1), channel_id=1, source_target_pairs={{0,1},{1,0},{2,3},{3,2},{4,5},{5,4},{6,7},{7,6},{8,9},{9,8},{10,11... | collective-permute-start | bytes 983048 | tf_op jit(solution)/shard_map/ppermute | solution.py:421
  59.4 5.0 %all-to-all-done.2 = f32[8,40,128]{2,1,0:T(8,128)S(1)} async-done(((f32[8,40,128]{2,1,0:T(8,128)}), f32[8,40,128]{2,1,0:T(8,128)S(1)}, u32[]{:S(2)}, u32[]{:S(2)}) %all-to-all-start.2) | async-done | bytes 163872 | tf_op jit(solution)/shard_map/all_to_all | solution.py:449
  64.5 1.1 broadcast_in_dim.11
  65.6 3.6 %all-to-all-start.3 = ((f32[8,320,128]{2,1,0:T(8,128)}), f32[8,320,128]{2,1,0:T(8,128)S(1)}, u32[]{:S(2)}, u32[]{:S(2)}) async-start(f32[8,320,128]{2,1,0:T(8,128)} %broadcast_in_dim.11), calls=%async_computation.3 | async-start | bytes 2621440 | tf_op jit(solution)/shard_map/all_to_all | solution.py:455
  69.3 4.5 %class_sums.1.class_ref = f32[4,896,128]{2,1,0:T(8,128)S(1)} custom-call(f32[8,4096]{1,0:T(8,128)S(1)} %pad_maximum_fusion.7.miller_ref, f32[32,4096]{1,0:T(8,128)S(1)} %pad_maximum_fusion.radial_ref), custom_call_target="tpu_custom_call" | custom-call | flops 1879048192 | bytes 655360 | tf_op jit(solution)/shard_map/class_sums/pallas_call | solution.py:172
  73.8 10.8 %all-to-all-done.3 = f32[8,320,128]{2,1,0:T(8,128)S(1)} async-done(((f32[8,320,128]{2,1,0:T(8,128)}), f32[8,320,128]{2,1,0:T(8,128)S(1)}, u32[]{:S(2)}, u32[]{:S(2)}) %all-to-all-start.3) | async-done | bytes 1310752 | tf_op jit(solution)/shard_map/all_to_all | solution.py:455
  84.6 3.7 %feature_rows.1 = (f32[32,4096]{1,0:T(8,128)S(1)}, bf16[608,1152]{1,0:T(8,128)(2,1)S(1)}) custom-call(f32[3,4096]{1,0:T(4,128)S(1)} %copy-done.2, f32[2560,128]{1,0:T(8,128)S(1)} %bitcast.6, f32[4,896,128]{2,1,0:T(8,128)S(1)} %class_sums.1.class_ref), custom_call_target="tpu_custom_call" | custom-call | flops 2709520384 | bytes 2867200 | tf_op jit(solution)/shard_map/feature_rows/pallas_call | solution.py:323
  88.5 5.1 %collective-permute-start.2 = (f32[32,4096]{1,0:T(8,128)S(1)}, f32[32,4096]{1,0:T(8,128)S(1)}, u32[]{:S(2)}, u32[]{:S(2)}) collective-permute-start(f32[32,4096]{1,0:T(8,128)S(1)} %get-tuple-element.21.refs_0_), channel_id=1, source_target_pairs={{0,1},{1,0},{2,3},{3,2},{4,5},{5,4},{6,7},{7,6},{8,9},{9,8},{10,11... | collective-permute-start | bytes 1572872 | tf_op jit(solution)/shard_map/ppermute | solution.py:421
  93.6 3.4 %filter_rows.1 = (f32[32,1024]{1,0:T(8,128)S(1)}, f32[32,1024]{1,0:T(8,128)S(1)}, f32[32,1024]{1,0:T(8,128)S(1)}, f32[32,1024]{1,0:T(8,128)S(1)}) custom-call(f32[8,4096]{1,0:T(8,128)S(1)} %pad_maximum_fusion.7.miller_ref, f32[2560,128]{1,0:T(8,128)S(1)} %bitcast.7), custom_call_target="tpu_custom_call" | custom-call | flops 1879048192 | bytes 655360 | tf_op jit(solution)/shard_map/filter_rows/pallas_call | solution.py:294
  97.0 1.1 %collective-permute-start.3 = (f32[32,1024]{1,0:T(8,128)S(1)}, f32[32,1024]{1,0:T(8,128)S(1)}, u32[]{:S(2)}, u32[]{:S(2)}) collective-permute-start(f32[32,1024]{1,0:T(8,128)S(1)} %get-tuple-element.23), channel_id=1, source_target_pairs={{0,2},{2,0},{1,3},{3,1},{4,6},{6,4},{5,7},{7,5},{8,10},{10,8},{9,1... | collective-permute-start | bytes 393224 | tf_op jit(solution)/shard_map/ppermute | solution.py:421
  98.7 7.9 %position_rows.1 = f32[3,4096]{1,0:T(4,128)S(1)} custom-call(s32[1]{0:T(128)} %bitcast.pick_ref, f32[3,4096]{1,0:T(4,128)S(1)} %copy-done.2, bf16[4096,128]{1,0:T(8,128)(2,1)S(1)} %copy-done, bf16[4096,128]{1,0:T(8,128)(2,1)S(1)} %copy-done.1, bf16[608,1152]{1,0:T(8,128)(2,1)S(1)} %get-tuple-element.27.uv_ref), custom_call_target="tpu_custom_call" | custom-call | flops 5419040768 | bytes 2867200 | tf_op jit(solution)/shard_map/position_rows/pallas_call | solution.py:401
  106.6 1.0 collective-permute-done.4.refs_7_
  108.7 1.0 collective-permute-done.7.refs_5_
  110.0 2.2 %place_rows.1 = (f32[4096,128]{1,0:T(8,128)}, f32[1024,128]{1,0:T(8,128)}) custom-call(s32[1]{0:T(128)} %bitcast.pick_ref, f32[32,4096]{1,0:T(8,128)S(1)} %get-tuple-element.21.refs_0_, f32[32,4096]{1,0:T(8,128)S(1)} %collective-permute-done.2.refs_1_, f32[32,4096]{1,0:T(8,128)S(1)} %collective-permute-done.5.refs_2_, ...), custom_call_target="tpu_custom_call" | custom-call | flops 6000000000 | bytes 4000000 | tf_op jit(solution)/shard_map/place_rows/pallas_call | solution.py:369
  112.5 1.1 collective-permute-done.9
  113.6 0.7 add_add_fusion
  (38 shorter events, 3.4 us)
Async XLA Ops:
  8.1 7.6 %copy-start.3 = (f32[1024,128]{1,0:T(8,128)S(1)}, f32[1024,128]{1,0:T(8,128)}, u32[]{:S(2)}) copy-start(f32[1024,128]{1,0:T(8,128)} %param.9) | copy-start | bytes 1572868
  8.1 7.8 %copy-start.4 = (s32[3,1024]{1,0:T(4,128)S(1)}, s32[3,1024]{1,0:T(4,128)}, u32[]{:S(2)}) copy-start(s32[3,1024]{1,0:T(4,128)} %param.8) | copy-start | bytes 36868
  8.1 26.9 %all-to-all-start = ((f32[8,320,128]{2,1,0:T(8,128)}), f32[8,320,128]{2,1,0:T(8,128)S(1)}, u32[]{:S(2)}, u32[]{:S(2)}) async-start(f32[8,320,128]{2,1,0:T(8,128)} %bitcast.9), calls=%async_computation | async-start | bytes 2621440 | tf_op jit(solution)/shard_map/all_to_all | solution.py:430
  16.1 27.9 %collective-permute-start = (f32[72,1024]{1,0:T(8,128)S(1)}, f32[72,1024]{1,0:T(8,128)S(1)}, u32[]{:S(2)}, u32[]{:S(2)}) collective-permute-start(f32[72,1024]{1,0:T(8,128)S(1)} %pad_maximum_fusion.2), channel_id=1, source_target_pairs={{0,2},{2,0},{1,3},{3,1},{4,6},{6,4},{5,7},{7,5},{8,10},{10,8},{9,1... | collective-permute-start | bytes 884744 | tf_op jit(solution)/shard_map/ppermute | solution.py:421
  35.7 16.5 %all-to-all-start.1 = ((f32[8,40,128]{2,1,0:T(8,128)}), f32[8,40,128]{2,1,0:T(8,128)S(1)}, u32[]{:S(2)}, u32[]{:S(2)}) async-start(f32[8,40,128]{2,1,0:T(8,128)} %bitcast.2), calls=%async_computation.1 | async-start | bytes 327680 | tf_op jit(solution)/shard_map/all_to_all | solution.py:442
  52.9 11.6 %all-to-all-start.2 = ((f32[8,40,128]{2,1,0:T(8,128)}), f32[8,40,128]{2,1,0:T(8,128)S(1)}, u32[]{:S(2)}, u32[]{:S(2)}) async-start(f32[8,40,128]{2,1,0:T(8,128)} %total_rows.1), calls=%async_computation.2 | async-start | bytes 327680 | tf_op jit(solution)/shard_map/all_to_all | solution.py:449
  56.3 12.9 %collective-permute-start.1 = (f32[40,2048]{1,0:T(8,128)S(1)}, f32[40,2048]{1,0:T(8,128)S(1)}, u32[]{:S(2)}, u32[]{:S(2)}) collective-permute-start(f32[40,2048]{1,0:T(8,128)S(1)} %pad_maximum_fusion.1), channel_id=1, source_target_pairs={{0,1},{1,0},{2,3},{3,2},{4,5},{5,4},{6,7},{7,6},{8,9},{9,8},{10,11... | collective-permute-start | bytes 983048 | tf_op jit(solution)/shard_map/ppermute | solution.py:421
  65.6 19.0 %all-to-all-start.3 = ((f32[8,320,128]{2,1,0:T(8,128)}), f32[8,320,128]{2,1,0:T(8,128)S(1)}, u32[]{:S(2)}, u32[]{:S(2)}) async-start(f32[8,320,128]{2,1,0:T(8,128)} %broadcast_in_dim.11), calls=%async_computation.3 | async-start | bytes 2621440 | tf_op jit(solution)/shard_map/all_to_all | solution.py:455
  69.3 15.3 %copy-start.2 = (f32[3,4096]{1,0:T(4,128)S(1)}, f32[3,4096]{1,0:T(4,128)}, u32[]{:S(2)}) copy-start(f32[3,4096]{1,0:T(4,128)} %pos_ref.5) | copy-start | bytes 147460
  88.3 10.5 %copy-start = (bf16[4096,128]{1,0:T(8,128)(2,1)S(1)}, bf16[4096,128]{1,0:T(8,128)(2,1)}, u32[]{:S(2)}) copy-start(bf16[4096,128]{1,0:T(8,128)(2,1)} %feat_ref.3) | copy-start | bytes 3145732
  88.3 10.5 %copy-start.1 = (bf16[4096,128]{1,0:T(8,128)(2,1)S(1)}, bf16[4096,128]{1,0:T(8,128)(2,1)}, u32[]{:S(2)}) copy-start(bf16[4096,128]{1,0:T(8,128)(2,1)} %cot_ref.3) | copy-start | bytes 3145732
  88.3 19.4 %collective-permute-start.5 = (f32[32,4096]{1,0:T(8,128)S(1)}, f32[32,4096]{1,0:T(8,128)S(1)}, u32[]{:S(2)}, u32[]{:S(2)}) collective-permute-start(f32[32,4096]{1,0:T(8,128)S(1)} %get-tuple-element.21.refs_0_), channel_id=1, source_target_pairs={{0,2},{2,0},{1,3},{3,1},{4,6},{6,4},{5,7},{7,5},{8,10},{10,8},{9,1... | collective-permute-start | bytes 1572872 | tf_op jit(solution)/shard_map/ppermute | solution.py:421
  88.5 21.5 %collective-permute-start.2 = (f32[32,4096]{1,0:T(8,128)S(1)}, f32[32,4096]{1,0:T(8,128)S(1)}, u32[]{:S(2)}, u32[]{:S(2)}) collective-permute-start(f32[32,4096]{1,0:T(8,128)S(1)} %get-tuple-element.21.refs_0_), channel_id=1, source_target_pairs={{0,1},{1,0},{2,3},{3,2},{4,5},{5,4},{6,7},{7,6},{8,9},{9,8},{10,11... | collective-permute-start | bytes 1572872 | tf_op jit(solution)/shard_map/ppermute | solution.py:421
  97.0 9.6 %collective-permute-start.3 = (f32[32,1024]{1,0:T(8,128)S(1)}, f32[32,1024]{1,0:T(8,128)S(1)}, u32[]{:S(2)}, u32[]{:S(2)}) collective-permute-start(f32[32,1024]{1,0:T(8,128)S(1)} %get-tuple-element.23), channel_id=1, source_target_pairs={{0,2},{2,0},{1,3},{3,1},{4,6},{6,4},{5,7},{7,5},{8,10},{10,8},{9,1... | collective-permute-start | bytes 393224 | tf_op jit(solution)/shard_map/ppermute | solution.py:421
  98.1 9.5 %collective-permute-start.4 = (f32[32,1024]{1,0:T(8,128)S(1)}, f32[32,1024]{1,0:T(8,128)S(1)}, u32[]{:S(2)}, u32[]{:S(2)}) collective-permute-start(f32[32,1024]{1,0:T(8,128)S(1)} %get-tuple-element.24), channel_id=1, source_target_pairs={{0,3},{1,2},{2,1},{3,0},{4,7},{5,6},{6,5},{7,4},{8,11},{9,10},{10,... | collective-permute-start | bytes 393224 | tf_op jit(solution)/shard_map/ppermute | solution.py:425
  107.6 2.4 %collective-permute-start.6 = (f32[32,4096]{1,0:T(8,128)S(1)}, f32[32,4096]{1,0:T(8,128)S(1)}, u32[]{:S(2)}, u32[]{:S(2)}) collective-permute-start(f32[32,4096]{1,0:T(8,128)S(1)} %collective-permute-done.5.refs_2_), channel_id=1, source_target_pairs={{0,1},{1,0},{2,3},{3,2},{4,5},{5,4},{6,7},{7,6},{8,9},{9,8},{10,11... | collective-permute-start | bytes 1572872 | tf_op jit(solution)/shard_map/ppermute | solution.py:421
  107.6 2.1 %collective-permute-start.7 = (f32[32,1024]{1,0:T(8,128)S(1)}, f32[32,1024]{1,0:T(8,128)S(1)}, u32[]{:S(2)}, u32[]{:S(2)}) collective-permute-start(f32[32,1024]{1,0:T(8,128)S(1)} %get-tuple-element.29), channel_id=1, source_target_pairs={{0,1},{1,0},{2,3},{3,2},{4,5},{5,4},{6,7},{7,6},{8,9},{9,8},{10,11... | collective-permute-start | bytes 393224 | tf_op jit(solution)/shard_map/ppermute | solution.py:421
  108.1 4.1 %collective-permute-start.10 = (f32[3,4096]{1,0:T(4,128)S(1)}, f32[3,4096]{1,0:T(4,128)S(1)}, u32[]{:S(2)}, u32[]{:S(2)}) collective-permute-start(f32[3,4096]{1,0:T(4,128)S(1)} %position_rows.1), channel_id=1, source_target_pairs={{0,1},{1,0},{2,3},{3,2},{4,5},{5,4},{6,7},{7,6},{8,9},{9,8},{10,11... | collective-permute-start | bytes 147464 | tf_op jit(solution)/shard_map/ppermute | solution.py:421
  108.2 4.4 %collective-permute-start.8 = (f32[3,4096]{1,0:T(4,128)S(1)}, f32[3,4096]{1,0:T(4,128)S(1)}, u32[]{:S(2)}, u32[]{:S(2)}) collective-permute-start(f32[3,4096]{1,0:T(4,128)S(1)} %position_rows.1), channel_id=1, source_target_pairs={{0,3},{1,2},{2,1},{3,0},{4,7},{5,6},{6,5},{7,4},{8,11},{9,10},{10,... | collective-permute-start | bytes 147464 | tf_op jit(solution)/shard_map/ppermute | solution.py:425
  109.7 3.9 %collective-permute-start.9 = (f32[3,4096]{1,0:T(4,128)S(1)}, f32[3,4096]{1,0:T(4,128)S(1)}, u32[]{:S(2)}, u32[]{:S(2)}) collective-permute-start(f32[3,4096]{1,0:T(4,128)S(1)} %position_rows.1), channel_id=1, source_target_pairs={{0,2},{2,0},{1,3},{3,1},{4,6},{6,4},{5,7},{7,5},{8,10},{10,8},{9,1... | collective-permute-start | bytes 147464 | tf_op jit(solution)/shard_map/ppermute | solution.py:421

commit v7 on v6

--- a/solution.py
+++ b/solution.py
@@ -484,7 +484,7 @@
     part = sum_scatter(part, ("x", "yh"))
     part = sum_everywhere(part, "z")
     total = gather(part, ("x", "yh"))
-    grad, uv = feature_rows(positions, total, classes, atoms)
+    grad, uv = feature_rows(positions, total, classes, atoms // 2)
     grad_y, grad_core = swap(grad, "yl"), swap(grad, "core")
     total = lax.optimization_barrier((total, grad))[0]
     own, across, beside, far = filter_rows(miller_rows, total, scale)

time: 115 us -> 117 us (1.017)
  Pallas kernels: 29.8 us -> 31.6 us
    pallas_call x1, Pallas kernels: 3.65 us -> 5.52 us  [feature_rows(): pl.pallas_call(feature_kernel, grid=(atoms // block,), in_specs=[pl.Block...]
  transfers between devices with their start and end apart: 15 -> 15, of which waited for: 8 -> 8; matrix products, arithmetic and copies ran while one was open for 2% -> 2% of each run, Pallas kernels for 16% -> 15%
where the time goes in v7:
time: 117 us; the launch traced here: 116 us
  waiting for transfers between devices  45.9 us (39%)
  starting transfers between devices  34.8 us (30%)
  Pallas kernels  31.6 us (27%)
  other arithmetic  1.6 us (1%)
  local copies, waits for them, and re-layouts  1.39 us (1%)
    all_to_all x1, waiting for transfers between devices, sum_scatter(): lax.all_to_all(value.reshape(n, value.shape[0] // n, 128), axis, 0, 0)  18.4 us
    ppermute x9, starting transfers between devices, swap(): return lax.ppermute(value, axis, [(0, 1), (1, 0)])  10.9 us
    all_to_all x1, waiting for transfers between devices, gather(): return lax.all_to_all(copies, axis, 0, 0).reshape(n * value.shape[0], 128)  10.8 us
    all_to_all x1, waiting for transfers between devices, sum_everywhere(): lax.all_to_all(value.reshape(n, value.shape[0] // n, 128), axis, 0, 0)  8.23 us
    all_to_all x1, starting transfers between devices, sum_everywhere(): lax.all_to_all(value.reshape(n, value.shape[0] // n, 128), axis, 0, 0)  8.18 us
    pallas_call x1, Pallas kernels, position_rows(): pl.pallas_call(position_kernel, grid=(atoms // block,), in_specs=[pl.Bloc...  7.89 us
    all_to_all x1, starting transfers between devices, sum_scatter(): lax.all_to_all(value.reshape(n, value.shape[0] // n, 128), axis, 0, 0)  7.61 us
    pallas_call x1, Pallas kernels, factors(): pl.pallas_call(factor_kernel, grid=(atoms // block,), in_specs=[pl.BlockS...  7.47 us
  transfers between devices with their start and end apart: 15, of which 8 were waited for; matrix products, arithmetic and copies ran while one was open for 2% of the time, Pallas kernels for 15%

profile of v7, /device:TPU:1, one launch (start us, length us, event | category | flops | bytes accessed | tf_op | source)
XLA Modules:
  0.0 116.1 jit_solution(14819876929158000466)
XLA Ops:
  0.6 7.5 %factors.1 = f32[2560,128]{1,0:T(8,128)} custom-call(s32[1]{0:T(128)} %bitcast.pick_ref, f32[3,4096]{1,0:T(4,128)} %pos_ref.5, bf16[4096,128]{1,0:T(8,128)(2,1)} %feat_ref.3, bf16[4096,128]{1,0:T(8,128)(2,1)} %cot_ref.3), custom_call_target="tpu_custom_call" | custom-call | flops 2709520384 | bytes 2129920 | tf_op jit(solution)/shard_map/factors/pallas_call | solution.py:107
  8.1 7.6 %all-to-all-start = ((f32[8,320,128]{2,1,0:T(8,128)}), f32[8,320,128]{2,1,0:T(8,128)S(1)}, u32[]{:S(2)}, u32[]{:S(2)}) async-start(f32[8,320,128]{2,1,0:T(8,128)} %bitcast.9), calls=%async_computation | async-start | bytes 2621440 | tf_op jit(solution)/shard_map/all_to_all | solution.py:430
  16.5 18.4 %all-to-all-done = f32[8,320,128]{2,1,0:T(8,128)S(1)} async-done(((f32[8,320,128]{2,1,0:T(8,128)}), f32[8,320,128]{2,1,0:T(8,128)S(1)}, u32[]{:S(2)}, u32[]{:S(2)}) %all-to-all-start) | async-done | bytes 1310752 | tf_op jit(solution)/shard_map/all_to_all | solution.py:430
  35.0 0.7 reduce_sum.9
  35.7 8.2 %all-to-all-start.1 = ((f32[8,40,128]{2,1,0:T(8,128)}), f32[8,40,128]{2,1,0:T(8,128)S(1)}, u32[]{:S(2)}, u32[]{:S(2)}) async-start(f32[8,40,128]{2,1,0:T(8,128)} %bitcast.2), calls=%async_computation.1 | async-start | bytes 327680 | tf_op jit(solution)/shard_map/all_to_all | solution.py:442
  44.0 8.2 %all-to-all-done.1.parts_ref = f32[8,40,128]{2,1,0:T(8,128)S(1)} async-done(((f32[8,40,128]{2,1,0:T(8,128)}), f32[8,40,128]{2,1,0:T(8,128)S(1)}, u32[]{:S(2)}, u32[]{:S(2)}) %all-to-all-start.1) | async-done | bytes 163872 | tf_op jit(solution)/shard_map/all_to_all | solution.py:442
  52.2 0.7 total_rows.1
  52.9 3.4 %all-to-all-start.2 = ((f32[8,40,128]{2,1,0:T(8,128)}), f32[8,40,128]{2,1,0:T(8,128)S(1)}, u32[]{:S(2)}, u32[]{:S(2)}) async-start(f32[8,40,128]{2,1,0:T(8,128)} %total_rows.1), calls=%async_computation.2 | async-start | bytes 327680 | tf_op jit(solution)/shard_map/all_to_all | solution.py:449
  56.3 3.1 %collective-permute-start.1 = (f32[40,2048]{1,0:T(8,128)S(1)}, f32[40,2048]{1,0:T(8,128)S(1)}, u32[]{:S(2)}, u32[]{:S(2)}) collective-permute-start(f32[40,2048]{1,0:T(8,128)S(1)} %pad_maximum_fusion.1), channel_id=1, source_target_pairs={{0,1},{1,0},{2,3},{3,2},{4,5},{5,4},{6,7},{7,6},{8,9},{9,8},{10,11... | collective-permute-start | bytes 983048 | tf_op jit(solution)/shard_map/ppermute | solution.py:421
  59.4 5.0 %all-to-all-done.2 = f32[8,40,128]{2,1,0:T(8,128)S(1)} async-done(((f32[8,40,128]{2,1,0:T(8,128)}), f32[8,40,128]{2,1,0:T(8,128)S(1)}, u32[]{:S(2)}, u32[]{:S(2)}) %all-to-all-start.2) | async-done | bytes 163872 | tf_op jit(solution)/shard_map/all_to_all | solution.py:449
  64.5 1.1 broadcast_in_dim.11
  65.6 3.6 %all-to-all-start.3 = ((f32[8,320,128]{2,1,0:T(8,128)}), f32[8,320,128]{2,1,0:T(8,128)S(1)}, u32[]{:S(2)}, u32[]{:S(2)}) async-start(f32[8,320,128]{2,1,0:T(8,128)} %broadcast_in_dim.11), calls=%async_computation.3 | async-start | bytes 2621440 | tf_op jit(solution)/shard_map/all_to_all | solution.py:455
  69.3 4.5 %class_sums.1.class_ref = f32[4,896,128]{2,1,0:T(8,128)S(1)} custom-call(f32[8,4096]{1,0:T(8,128)S(1)} %pad_maximum_fusion.7.miller_ref, f32[32,4096]{1,0:T(8,128)S(1)} %pad_maximum_fusion.radial_ref), custom_call_target="tpu_custom_call" | custom-call | flops 1879048192 | bytes 655360 | tf_op jit(solution)/shard_map/class_sums/pallas_call | solution.py:172
  73.8 10.8 %all-to-all-done.3 = f32[8,320,128]{2,1,0:T(8,128)S(1)} async-done(((f32[8,320,128]{2,1,0:T(8,128)}), f32[8,320,128]{2,1,0:T(8,128)S(1)}, u32[]{:S(2)}, u32[]{:S(2)}) %all-to-all-start.3) | async-done | bytes 1310752 | tf_op jit(solution)/shard_map/all_to_all | solution.py:455
  84.6 5.5 %feature_rows.1 = (f32[32,4096]{1,0:T(8,128)S(1)}, bf16[608,1152]{1,0:T(8,128)(2,1)S(1)}) custom-call(f32[3,4096]{1,0:T(4,128)S(1)} %copy-done.2, f32[2560,128]{1,0:T(8,128)S(1)} %bitcast.6, f32[4,896,128]{2,1,0:T(8,128)S(1)} %class_sums.1.class_ref), custom_call_target="tpu_custom_call" | custom-call | flops 2709520384 | bytes 2867200 | tf_op jit(solution)/shard_map/feature_rows/pallas_call | solution.py:323
  90.4 5.1 %collective-permute-start.2 = (f32[32,4096]{1,0:T(8,128)S(1)}, f32[32,4096]{1,0:T(8,128)S(1)}, u32[]{:S(2)}, u32[]{:S(2)}) collective-permute-start(f32[32,4096]{1,0:T(8,128)S(1)} %get-tuple-element.21.refs_0_), channel_id=1, source_target_pairs={{0,1},{1,0},{2,3},{3,2},{4,5},{5,4},{6,7},{7,6},{8,9},{9,8},{10,11... | collective-permute-start | bytes 1572872 | tf_op jit(solution)/shard_map/ppermute | solution.py:421
  95.5 3.4 %filter_rows.1 = (f32[32,1024]{1,0:T(8,128)S(1)}, f32[32,1024]{1,0:T(8,128)S(1)}, f32[32,1024]{1,0:T(8,128)S(1)}, f32[32,1024]{1,0:T(8,128)S(1)}) custom-call(f32[8,4096]{1,0:T(8,128)S(1)} %pad_maximum_fusion.7.miller_ref, f32[2560,128]{1,0:T(8,128)S(1)} %bitcast.7), custom_call_target="tpu_custom_call" | custom-call | flops 1879048192 | bytes 655360 | tf_op jit(solution)/shard_map/filter_rows/pallas_call | solution.py:294
  98.9 1.2 collective-permute-start.3
  100.6 7.9 %position_rows.1 = f32[3,4096]{1,0:T(4,128)S(1)} custom-call(s32[1]{0:T(128)} %bitcast.pick_ref, f32[3,4096]{1,0:T(4,128)S(1)} %copy-done.2, bf16[4096,128]{1,0:T(8,128)(2,1)S(1)} %copy-done, bf16[4096,128]{1,0:T(8,128)(2,1)S(1)} %copy-done.1, bf16[608,1152]{1,0:T(8,128)(2,1)S(1)} %get-tuple-element.27.uv_ref), custom_call_target="tpu_custom_call" | custom-call | flops 5419040768 | bytes 2867200 | tf_op jit(solution)/shard_map/position_rows/pallas_call | solution.py:401
  108.5 1.0 collective-permute-done.4.refs_7_
  110.6 1.0 collective-permute-done.7.refs_5_
  111.9 2.2 %place_rows.1 = (f32[4096,128]{1,0:T(8,128)}, f32[1024,128]{1,0:T(8,128)}) custom-call(s32[1]{0:T(128)} %bitcast.pick_ref, f32[32,4096]{1,0:T(8,128)S(1)} %get-tuple-element.21.refs_0_, f32[32,4096]{1,0:T(8,128)S(1)} %collective-permute-done.2.refs_1_, f32[32,4096]{1,0:T(8,128)S(1)} %collective-permute-done.5.refs_2_, ...), custom_call_target="tpu_custom_call" | custom-call | flops 6000000000 | bytes 4000000 | tf_op jit(solution)/shard_map/place_rows/pallas_call | solution.py:369
  114.4 1.1 collective-permute-done.9
  115.5 0.7 add_add_fusion
  (38 shorter events, 3.4 us)
Async XLA Ops:
  8.1 7.6 %copy-start.3 = (f32[1024,128]{1,0:T(8,128)S(1)}, f32[1024,128]{1,0:T(8,128)}, u32[]{:S(2)}) copy-start(f32[1024,128]{1,0:T(8,128)} %param.9) | copy-start | bytes 1572868
  8.1 7.8 %copy-start.4 = (s32[3,1024]{1,0:T(4,128)S(1)}, s32[3,1024]{1,0:T(4,128)}, u32[]{:S(2)}) copy-start(s32[3,1024]{1,0:T(4,128)} %param.8) | copy-start | bytes 36868
  8.1 26.9 %all-to-all-start = ((f32[8,320,128]{2,1,0:T(8,128)}), f32[8,320,128]{2,1,0:T(8,128)S(1)}, u32[]{:S(2)}, u32[]{:S(2)}) async-start(f32[8,320,128]{2,1,0:T(8,128)} %bitcast.9), calls=%async_computation | async-start | bytes 2621440 | tf_op jit(solution)/shard_map/all_to_all | solution.py:430
  16.1 27.9 %collective-permute-start = (f32[72,1024]{1,0:T(8,128)S(1)}, f32[72,1024]{1,0:T(8,128)S(1)}, u32[]{:S(2)}, u32[]{:S(2)}) collective-permute-start(f32[72,1024]{1,0:T(8,128)S(1)} %pad_maximum_fusion.2), channel_id=1, source_target_pairs={{0,2},{2,0},{1,3},{3,1},{4,6},{6,4},{5,7},{7,5},{8,10},{10,8},{9,1... | collective-permute-start | bytes 884744 | tf_op jit(solution)/shard_map/ppermute | solution.py:421
  35.7 16.5 %all-to-all-start.1 = ((f32[8,40,128]{2,1,0:T(8,128)}), f32[8,40,128]{2,1,0:T(8,128)S(1)}, u32[]{:S(2)}, u32[]{:S(2)}) async-start(f32[8,40,128]{2,1,0:T(8,128)} %bitcast.2), calls=%async_computation.1 | async-start | bytes 327680 | tf_op jit(solution)/shard_map/all_to_all | solution.py:442
  52.9 11.6 %all-to-all-start.2 = ((f32[8,40,128]{2,1,0:T(8,128)}), f32[8,40,128]{2,1,0:T(8,128)S(1)}, u32[]{:S(2)}, u32[]{:S(2)}) async-start(f32[8,40,128]{2,1,0:T(8,128)} %total_rows.1), calls=%async_computation.2 | async-start | bytes 327680 | tf_op jit(solution)/shard_map/all_to_all | solution.py:449
  56.3 12.9 %collective-permute-start.1 = (f32[40,2048]{1,0:T(8,128)S(1)}, f32[40,2048]{1,0:T(8,128)S(1)}, u32[]{:S(2)}, u32[]{:S(2)}) collective-permute-start(f32[40,2048]{1,0:T(8,128)S(1)} %pad_maximum_fusion.1), channel_id=1, source_target_pairs={{0,1},{1,0},{2,3},{3,2},{4,5},{5,4},{6,7},{7,6},{8,9},{9,8},{10,11... | collective-permute-start | bytes 983048 | tf_op jit(solution)/shard_map/ppermute | solution.py:421
  65.6 19.0 %all-to-all-start.3 = ((f32[8,320,128]{2,1,0:T(8,128)}), f32[8,320,128]{2,1,0:T(8,128)S(1)}, u32[]{:S(2)}, u32[]{:S(2)}) async-start(f32[8,320,128]{2,1,0:T(8,128)} %broadcast_in_dim.11), calls=%async_computation.3 | async-start | bytes 2621440 | tf_op jit(solution)/shard_map/all_to_all | solution.py:455
  69.3 15.3 %copy-start.2 = (f32[3,4096]{1,0:T(4,128)S(1)}, f32[3,4096]{1,0:T(4,128)}, u32[]{:S(2)}) copy-start(f32[3,4096]{1,0:T(4,128)} %pos_ref.5) | copy-start | bytes 147460
  90.1 10.5 %copy-start = (bf16[4096,128]{1,0:T(8,128)(2,1)S(1)}, bf16[4096,128]{1,0:T(8,128)(2,1)}, u32[]{:S(2)}) copy-start(bf16[4096,128]{1,0:T(8,128)(2,1)} %feat_ref.3) | copy-start | bytes 3145732
  90.1 10.5 %copy-start.1 = (bf16[4096,128]{1,0:T(8,128)(2,1)S(1)}, bf16[4096,128]{1,0:T(8,128)(2,1)}, u32[]{:S(2)}) copy-start(bf16[4096,128]{1,0:T(8,128)(2,1)} %cot_ref.3) | copy-start | bytes 3145732
  90.2 19.4 %collective-permute-start.5 = (f32[32,4096]{1,0:T(8,128)S(1)}, f32[32,4096]{1,0:T(8,128)S(1)}, u32[]{:S(2)}, u32[]{:S(2)}) collective-permute-start(f32[32,4096]{1,0:T(8,128)S(1)} %get-tuple-element.21.refs_0_), channel_id=1, source_target_pairs={{0,2},{2,0},{1,3},{3,1},{4,6},{6,4},{5,7},{7,5},{8,10},{10,8},{9,1... | collective-permute-start | bytes 1572872 | tf_op jit(solution)/shard_map/ppermute | solution.py:421
  90.4 21.5 %collective-permute-start.2 = (f32[32,4096]{1,0:T(8,128)S(1)}, f32[32,4096]{1,0:T(8,128)S(1)}, u32[]{:S(2)}, u32[]{:S(2)}) collective-permute-start(f32[32,4096]{1,0:T(8,128)S(1)} %get-tuple-element.21.refs_0_), channel_id=1, source_target_pairs={{0,1},{1,0},{2,3},{3,2},{4,5},{5,4},{6,7},{7,6},{8,9},{9,8},{10,11... | collective-permute-start | bytes 1572872 | tf_op jit(solution)/shard_map/ppermute | solution.py:421
  98.9 9.6 %collective-permute-start.3 = (f32[32,1024]{1,0:T(8,128)S(1)}, f32[32,1024]{1,0:T(8,128)S(1)}, u32[]{:S(2)}, u32[]{:S(2)}) collective-permute-start(f32[32,1024]{1,0:T(8,128)S(1)} %get-tuple-element.23), channel_id=1, source_target_pairs={{0,2},{2,0},{1,3},{3,1},{4,6},{6,4},{5,7},{7,5},{8,10},{10,8},{9,1... | collective-permute-start | bytes 393224 | tf_op jit(solution)/shard_map/ppermute | solution.py:421
  100.0 9.5 %collective-permute-start.4 = (f32[32,1024]{1,0:T(8,128)S(1)}, f32[32,1024]{1,0:T(8,128)S(1)}, u32[]{:S(2)}, u32[]{:S(2)}) collective-permute-start(f32[32,1024]{1,0:T(8,128)S(1)} %get-tuple-element.24), channel_id=1, source_target_pairs={{0,3},{1,2},{2,1},{3,0},{4,7},{5,6},{6,5},{7,4},{8,11},{9,10},{10,... | collective-permute-start | bytes 393224 | tf_op jit(solution)/shard_map/ppermute | solution.py:425
  109.5 2.4 %collective-permute-start.6 = (f32[32,4096]{1,0:T(8,128)S(1)}, f32[32,4096]{1,0:T(8,128)S(1)}, u32[]{:S(2)}, u32[]{:S(2)}) collective-permute-start(f32[32,4096]{1,0:T(8,128)S(1)} %collective-permute-done.5.refs_2_), channel_id=1, source_target_pairs={{0,1},{1,0},{2,3},{3,2},{4,5},{5,4},{6,7},{7,6},{8,9},{9,8},{10,11... | collective-permute-start | bytes 1572872 | tf_op jit(solution)/shard_map/ppermute | solution.py:421
  109.5 2.1 %collective-permute-start.7 = (f32[32,1024]{1,0:T(8,128)S(1)}, f32[32,1024]{1,0:T(8,128)S(1)}, u32[]{:S(2)}, u32[]{:S(2)}) collective-permute-start(f32[32,1024]{1,0:T(8,128)S(1)} %get-tuple-element.29), channel_id=1, source_target_pairs={{0,1},{1,0},{2,3},{3,2},{4,5},{5,4},{6,7},{7,6},{8,9},{9,8},{10,11... | collective-permute-start | bytes 393224 | tf_op jit(solution)/shard_map/ppermute | solution.py:421
  110.0 4.1 %collective-permute-start.10 = (f32[3,4096]{1,0:T(4,128)S(1)}, f32[3,4096]{1,0:T(4,128)S(1)}, u32[]{:S(2)}, u32[]{:S(2)}) collective-permute-start(f32[3,4096]{1,0:T(4,128)S(1)} %position_rows.1), channel_id=1, source_target_pairs={{0,1},{1,0},{2,3},{3,2},{4,5},{5,4},{6,7},{7,6},{8,9},{9,8},{10,11... | collective-permute-start | bytes 147464 | tf_op jit(solution)/shard_map/ppermute | solution.py:421
  110.0 4.4 %collective-permute-start.8 = (f32[3,4096]{1,0:T(4,128)S(1)}, f32[3,4096]{1,0:T(4,128)S(1)}, u32[]{:S(2)}, u32[]{:S(2)}) collective-permute-start(f32[3,4096]{1,0:T(4,128)S(1)} %position_rows.1), channel_id=1, source_target_pairs={{0,3},{1,2},{2,1},{3,0},{4,7},{5,6},{6,5},{7,4},{8,11},{9,10},{10,... | collective-permute-start | bytes 147464 | tf_op jit(solution)/shard_map/ppermute | solution.py:425
  111.6 3.9 %collective-permute-start.9 = (f32[3,4096]{1,0:T(4,128)S(1)}, f32[3,4096]{1,0:T(4,128)S(1)}, u32[]{:S(2)}, u32[]{:S(2)}) collective-permute-start(f32[3,4096]{1,0:T(4,128)S(1)} %position_rows.1), channel_id=1, source_target_pairs={{0,2},{2,0},{1,3},{3,1},{4,6},{6,4},{5,7},{7,5},{8,10},{10,8},{9,1... | collective-permute-start | bytes 147464 | tf_op jit(solution)/shard_map/ppermute | solution.py:421
